TPU v7x, 32 devices: a whole 2x2x4 slice. The times are simulated.
32 devices in a mesh: tile: 2 (over x), beam: 16 (over z, y, core).
Axes of the slice: x: 2, y: 2, z: 4, core: 2. Of those that a mesh axis runs over, the one named last changes fastest.
Arguments:
- echoes: bfloat16 [2, 2048, 8192], P(None, 'tile', 'beam'), may hold values from -160 to 160
- steer: bfloat16 [2, 2048, 2048], P(None, None, 'tile'), may hold values from -0.09375 to 0.09375
- code: bfloat16 [2, 8], replicated, may hold values from -1 to 1
- beam_order: int32 [2048], replicated, may hold values from 0 to 2047, each once
- dwell: int32 [2048], replicated, may hold values from 64 to 256, as said below
- code_len: int32 [2048], replicated, may hold values from 1 to 8, as said below
Outputs:
- spectrum: float32 [2048, 2, 32, 256], P(('tile', 'beam'))
Inputs may be any that keep to these rules, and one draw needn't show every extreme that they name: dwell[b] counts the leading pulses that beam b keeps; some beam keeps all 256. `code_len`: some beam uses all 8 taps.
All inputs are finite; a program needn't handle non-finite values.
Results may differ from a plain program's by a relative error of at most 0.015.
Values may be sent and summed in bfloat16 or wider, within the bound.
No kernel may reach another device: no remote copies, remote signals or barrier semaphores. Data moves between devices by JAX's collectives and lax.ppermute only.
A program may use at most 64 MiB of HBM per device.

v0:
```python
import math

import jax
import jax.numpy as jnp
from jax import lax
from jax.sharding import PartitionSpec as P

G = 32


def complex_block(weight_re, weight_im):
    upper = jnp.concatenate([weight_re, -weight_im], axis=1)
    lower = jnp.concatenate([weight_im, weight_re], axis=1)
    return jnp.stack([upper, lower], axis=1).reshape(2 * weight_re.shape[0], 2 * weight_re.shape[1])


def phase_table(rows, cols, period):
    row_index = jnp.arange(rows, dtype=jnp.int32)
    col_index = jnp.arange(cols, dtype=jnp.int32)
    phase = row_index[:, None] * col_index[None, :] % period
    angle = phase.astype(jnp.float32) * (2.0 * math.pi / period)
    return (jnp.cos(angle), -jnp.sin(angle))


def compress(values, code, lens, limits, first_pulse):
    gates = values.shape[3]
    taps = code.shape[1]
    padded = jnp.pad(values, ((0, 0), (0, 0), (0, 0), (0, taps)))
    code_re = code[0].astype(jnp.float32)
    code_im = code[1].astype(jnp.float32)
    out_re = jnp.zeros((values.shape[0], values.shape[2], gates), jnp.float32)
    out_im = jnp.zeros((values.shape[0], values.shape[2], gates), jnp.float32)
    for tap in range(taps):
        live = (tap < lens).astype(jnp.float32)[:, None, None]
        shift_re = padded[:, 0, :, tap : tap + gates]
        shift_im = padded[:, 1, :, tap : tap + gates]
        out_re = out_re + live * (code_re[tap] * shift_re + code_im[tap] * shift_im)
        out_im = out_im + live * (code_re[tap] * shift_im - code_im[tap] * shift_re)
    pulse_index = first_pulse + jnp.arange(values.shape[2], dtype=jnp.int32)
    keep = (pulse_index[None, :] < limits[:, None]).astype(jnp.float32)[:, None, :, None]
    return (jnp.stack([out_re, out_im], axis=1) * keep).astype(jnp.bfloat16)


def highest(form, left, right):
    return jnp.einsum(form, left, right, precision=lax.Precision.HIGHEST)


def on_device(echoes, steer, code, beam_order, dwell, code_len):
    tiles = lax.axis_size("tile")
    owners = lax.axis_size("beam")
    chans = echoes.shape[1]
    columns = echoes.shape[2]
    beam_total = steer.shape[1]
    pulses_dev = columns // G
    pulses_all = pulses_dev * owners
    tile_beams = beam_total // tiles
    values = echoes.astype(jnp.float32)
    local_power = jnp.sum(values * values, axis=(0, 2))
    power = lax.psum(local_power, "beam") / (pulses_all * G)
    gain = lax.rsqrt(power + 1e-05)
    ordered = jnp.take(steer, beam_order, axis=1)
    weights = (ordered.astype(jnp.float32) * gain).astype(jnp.bfloat16)
    stacked = complex_block(weights[0], weights[1])
    flat = echoes.reshape(2 * chans, columns)
    summed = lax.psum_scatter(
        jnp.dot(stacked, flat, preferred_element_type=jnp.float32)
        .reshape(tile_beams * lax.axis_size("tile"), 2, columns)
        .astype(jnp.bfloat16),
        "tile",
        scatter_dimension=0,
        tiled=True,
    )
    rounded = lax.optimization_barrier(summed)
    beams = rounded.astype(jnp.float32).reshape(tile_beams, 2, pulses_dev, G)
    first_slot = lax.axis_index("tile") * tile_beams
    slot_ids = lax.dynamic_slice_in_dim(beam_order, first_slot, tile_beams, 0)
    lens = jnp.take(code_len, slot_ids)
    limits = jnp.take(dwell, slot_ids)
    compressed = compress(beams, code, lens, limits, lax.axis_index("beam") * pulses_dev)
    scale = 1.0 / math.sqrt(pulses_all)
    table_re, table_im = phase_table(pulses_all, pulses_all, pulses_all)
    wide = lax.all_to_all(compressed, "beam", split_axis=0, concat_axis=2, tiled=True).astype(
        jnp.float32
    )
    first = highest("bcpg,pk->bcgk", wide, table_re)
    second = highest("bcpg,pk->bcgk", wide, table_im)
    joined = jnp.stack([first[:, 0] - second[:, 1], first[:, 1] + second[:, 0]], axis=1)
    return joined * scale


def solution(mesh):
    placed = (P(None, "tile", "beam"), P(None, None, "tile"), P(), P(), P(), P())
    return jax.shard_map(
        on_device,
        mesh=mesh,
        in_specs=placed,
        out_specs=P(("tile", "beam"), None, None, None),
        check_vma=False,
    )
```

profile of v0, /device:TPU:9, one launch (start us, length us, event | category | flops | bytes accessed | tf_op | source)
XLA Modules:
  0.0 344.7 jit_solution(8987734472389934649)
XLA Ops:
  6.5 0.0 copy-start
  6.5 0.0 reduce-scatter.2.cloned.1.call-start
  6.5 0.7 fusion.24
  7.3 0.7 compare_and_fusion
  8.0 2.1 multiply_reduce_fusion
  10.0 22.3 %psum.7 = f32[1024]{0:T(1024)S(1)} all-reduce(f32[1024]{0:T(1024)S(1)} %multiply_reduce_fusion), channel_id=1, replica_groups=mesh['tile'=2,'beam'=16] {'beam'}, use_global_device_ids=true, to_apply=%region_1.3 | all-reduce | flops 1024 | bytes 8192 | tf_op jit(solution)/shard_map/psum | solution.py:59
  32.4 54.6 %gather_fusion = bf16[2048,2,1024]{2,0,1:T(8,128)(2,1)} fusion(bf16[2,2048,1024]{2,1,0:T(8,128)(2,1)} %param.9, s32[2048]{0:T(1024)S(1)} %fusion.24), kind=kCustom, calls=%fused_computation.2 | custom fusion | bytes 16785408 | tf_op jit(solution)/shard_map/jit(_take)/gather | solution.py:61
  87.0 5.4 %fusion.4 = bf16[2,2048,1024]{2,1,0:T(8,128)(2,1)S(1)} fusion(f32[1024]{0:T(1024)S(1)} %add_rsqrt_fusion, bf16[2048,2,1024]{2,0,1:T(8,128)(2,1)} %gather_fusion, pred[2048]{0:T(1024)(128)(4,1)S(1)} %compare_and_fusion), kind=kLoop, calls=%fused_computation.8 | loop fusion | flops 16777216 | bytes 16783360 | tf_op jit(solution)/shard_map/convert_element_type | solution.py:62
  92.4 0.3 fusion.35
  92.7 0.9 slice_bitcast_fusion
  93.6 0.0 copy-start.3
  93.6 4.0 %maximum_bitcast_fusion = (bf16[2048,1,2048]{2,0,1:T(8,128)(2,1)S(1)}, bf16[2048,1,2048]{2,0,1:T(8,128)(2,1)}) fusion(bf16[2048,1024]{1,0:T(8,128)(2,1)S(1)} %fusion.35, bf16[2048,1024]{1,0:T(8,128)(2,1)S(1)} %get-tuple-element.11, bf16[2048,1024]{1,0:T(8,128)(2,1)S(1)} %get-tuple-element.10), kind=kLoop, calls=%fused_computation.9 | loop fusion | flops 33554432 | bytes 29360128 | tf_op jit(solution)/shard_map/stack | solution.py:14
  97.6 0.0 copy-done.3
  97.6 12.6 %fusion.6 = bf16[2048,2,512]{2,0,1:T(8,128)(2,1)} fusion(bf16[2048,512,1]{1,0,2:T(8,128)(2,1)S(1)} %bitcast.53, bf16[2048,1,2048]{2,0,1:T(8,128)(2,1)} %get-tuple-element.13, bf16[2048,1,2048]{2,0,1:T(8,128)(2,1)S(1)} %get-tuple-element.12), kind=kOutput, calls=%fused_computation.31 | convolution fusion | flops 8600420352 | bytes 23068672 | tf_op jit(solution)/shard_map/dot_general | solution.py:66
  110.2 0.0 copy-start.4
  110.2 0.0 reduce-scatter.2.cloned.1.call-update
  110.2 0.7 copy-done.4
  110.9 0.0 copy-done
  110.9 0.0 copy-start.1
  110.9 6.2 %gather_fusion.2 = s32[1024]{0:T(1024)S(1)} fusion(s32[2048]{0:T(1024)S(1)} %copy-done, s32[1024]{0:T(1024)S(1)} %fusion.25), kind=kCustom, calls=%fused_computation.1.clone | custom fusion | bytes 12288 | tf_op jit(solution)/shard_map/jit(_take)/gather | solution.py:78
  117.1 0.0 copy-done.1
  117.1 0.0 copy-start.5
  117.1 6.2 %gather_fusion.1 = s32[1024]{0:T(1024)S(1)} fusion(s32[2048]{0:T(1024)S(1)} %copy-done.1, s32[1024]{0:T(1024)S(1)} %fusion.25), kind=kCustom, calls=%fused_computation.clone | custom fusion | bytes 12288 | tf_op jit(solution)/shard_map/jit(_take)/gather | solution.py:77
  123.3 0.0 copy-done.5
  123.3 0.7 fusion.36
  124.0 0.1 compare_convert_fusion
  124.1 48.9 %reduce-scatter.2.cloned.1.call-done = bf16[1024,2,512]{2,0,1:T(8,128)(2,1)} async-done(((bf16[2048,2,512]{2,0,1:T(8,128)(2,1)}), bf16[1024,2,512]{2,0,1:T(8,128)(2,1)}) %reduce-scatter.2.cloned.1.call-update) | async-done | bytes 2097168 | tf_op jit(solution)/shard_map/reduce_scatter | solution.py:65
  173.0 4.1 %copy.12 = f32[1024,2,512]{0,2,1:T(8,128)} copy(bf16[1024,2,512]{2,0,1:T(8,128)(2,1)} %reduce-scatter.2.cloned.1.call-done) | data formatting | bytes 6291456 | tf_op jit(solution)/shard_map/reshape | solution.py:74
  177.1 0.0 copy-start.2
  177.1 26.3 %multiply_add_fusion = f32[1024,1,16,32]{0,3,2,1:T(8,128)S(1)} fusion(f32[1024,2,16,32]{0,3,2,1:T(8,128)} %bitcast.49, f32[]{:T(128)} %bitcast.23, f32[]{:T(128)} %bitcast.22, f32[1024]{0:T(1024)S(1)} %get-tuple-element.20, f32[]{:T(128)} %bitcast.21, f32[]{:T(128)} %bitcast.20, f32[1024]{0:T(1024)S(1)} %get-tuple-element.19, f32[]{:T(128)} %bitcast.19, ...), kind=kLoop, calls=%fused_computation.34 | loop fusion | flops 20447232 | bytes 10526720 | tf_op jit(solution)/shard_map/add | solution.py:38
  203.4 0.0 copy-done.2
  203.4 14.5 %multiply_add_fusion.1 = f32[1024,1,16,32]{0,3,2,1:T(8,128)S(1)} fusion(f32[1024,2,16,32]{0,3,2,1:T(8,128)S(1)} %bitcast.50, f32[]{:T(128)} %bitcast.23, f32[]{:T(128)} %bitcast.22, f32[1024]{0:T(1024)S(1)} %get-tuple-element.20, f32[]{:T(128)} %bitcast.21, f32[]{:T(128)} %bitcast.20, f32[1024]{0:T(1024)S(1)} %get-tuple-element.19, f32[]{:T(128)} %bitcast.19, ...), kind=kLoop, calls=%fused_computation.35 | loop fusion | flops 20447232 | bytes 10518592 | tf_op jit(solution)/shard_map/add | solution.py:37
  217.9 0.6 fusion.5
  218.6 12.1 %copy.13 = bf16[1024,2,16,32]{3,2,1,0:T(8,128)(2,1)} copy(bf16[1024,2,16,32]{0,3,2,1:T(8,128)(2,1)S(1)} %fusion.5) | data formatting | bytes 4194304 | tf_op jit(solution)/shard_map/convert_element_type | solution.py:41
  230.7 13.4 %reshape.136 = bf16[16,2,32768]{2,1,0:T(2,128)(2,1)S(1)} reshape(bf16[1024,2,16,32]{3,2,1,0:T(8,128)(2,1)} %copy.13) | data formatting | bytes 4194304
  244.1 54.1 %all_to_all.18 = bf16[16,2,32768]{2,1,0:T(2,128)(2,1)} all-to-all(bf16[16,2,32768]{2,1,0:T(2,128)(2,1)S(1)} %reshape.136), channel_id=1, replica_groups=mesh['tile'=2,'beam'=16] {'beam'}, dimensions={0} | all-to-all | bytes 4194304 | tf_op jit(solution)/shard_map/all_to_all | solution.py:82
  298.2 12.9 %reshape.137 = bf16[1024,2,16,32]{3,2,1,0:T(8,128)(2,1)} reshape(bf16[16,2,32768]{2,1,0:T(2,128)(2,1)} %all_to_all.18) | data formatting | bytes 4194304
  311.1 10.2 %copy.14 = bf16[16,64,2,16,32]{1,4,3,0,2:T(8,128)(2,1)} copy(bf16[16,64,2,16,32]{4,3,2,1,0:T(8,128)(2,1)} %bitcast.51) | data formatting | bytes 4194304 | tf_op jit(solution)/shard_map/all_to_all | solution.py:82
  321.3 7.0 %copy.15 = bf16[64,2,256,32]{2,3,1,0:T(8,128)(2,1)S(1)} copy(bf16[64,2,256,32]{0,3,2,1:T(8,128)(2,1)} %bitcast.52) | data formatting | bytes 4194304 | tf_op jit(solution)/shard_map/all_to_all | solution.py:82
  328.3 2.8 fusion.12
  331.1 2.8 fusion.14
  333.9 1.4 slice_subtract_fusion
  335.3 2.6 maximum_multiply_fusion.1
  (6 shorter events, 0.0 us)
Async XLA Ops:
  6.5 104.4 %copy-start = (s32[2048]{0:T(1024)S(1)}, s32[2048]{0:T(1024)}, u32[]{:S(2)}) copy-start(s32[2048]{0:T(1024)} %param.12) | copy-start | bytes 24580
  6.5 166.4 %reduce-scatter.2.cloned.1.call-start = ((), (), s32[]{:S(2)}) async-start(), calls=%async_computation.2 | async-start | bytes 6291456 | tf_op jit(solution)/shard_map/reduce_scatter | solution.py:65
  93.6 4.0 %copy-start.3 = (bf16[2,1024,512]{2,1,0:T(8,128)(2,1)S(1)}, bf16[2,1024,512]{2,1,0:T(8,128)(2,1)}, u32[]{:S(2)}) copy-start(bf16[2,1024,512]{2,1,0:T(8,128)(2,1)} %param.8) | copy-start | bytes 6291460
  110.2 0.7 copy-start.4
  110.9 6.2 %copy-start.1 = (s32[2048]{0:T(1024)S(1)}, s32[2048]{0:T(1024)}, u32[]{:S(2)}) copy-start(s32[2048]{0:T(1024)} %param.13) | copy-start | bytes 24580
  117.1 6.2 %copy-start.5 = (bf16[2,8]{1,0:T(2,128)(2,1)S(1)}, bf16[2,8]{1,0:T(2,128)(2,1)}, u32[]{:S(2)}) copy-start(bf16[2,8]{1,0:T(2,128)(2,1)} %param.10) | copy-start | bytes 100
  177.1 26.3 %copy-start.2 = (f32[1024,2,512]{0,2,1:T(8,128)S(1)}, f32[1024,2,512]{0,2,1:T(8,128)}, u32[]{:S(2)}) copy-start(f32[1024,2,512]{0,2,1:T(8,128)} %copy.12) | copy-start | bytes 12582916
Sparse Core Ops, SparseCore 0:
  110.3 62.5 reduce-scatter.1
where the time goes:
time: 348 us; the launch traced here: 345 us
  local copies, waits for them, and re-layouts  129 us (37%)
  blocking collectives  76.5 us (22%)
  other arithmetic  58.6 us (17%)
  waiting for transfers between devices  48.9 us (14%)
  matrix products  18.2 us (5%)
  between operations  13.6 us (4%)
    gather x1, local copies, waits for them, and re-layouts, on_device(): ordered = jnp.take(steer, beam_order, axis=1)  54.6 us
    all_to_all x1, blocking collectives, on_device(): lax.all_to_all(compressed, 'beam', split_axis=0, concat_axis=2, tiled=True)  54.1 us
    reduce_scatter x1, waiting for transfers between devices, on_device(): lax.psum_scatter(jnp.dot(stacked, flat, preferred_element_type=jnp.float3...  48.9 us
    unnamed x14, local copies, waits for them, and re-layouts  27 us
    add x1, other arithmetic, compress(): out_im = out_im + live * (code_re[tap] * shift_im - code_im[tap] * shift_re)  26.3 us
    psum x1, blocking collectives, on_device(): power = lax.psum(local_power, 'beam') / (pulses_all * G)  22.3 us
    all_to_all x2, local copies, waits for them, and re-layouts, on_device(): lax.all_to_all(compressed, 'beam', split_axis=0, concat_axis=2, tiled=True)  17.2 us
    add x1, other arithmetic, compress(): out_re = out_re + live * (code_re[tap] * shift_re + code_im[tap] * shift_im)  14.5 us
  transfers between devices with their start and end apart: 1, of which 1 were waited for; matrix products, arithmetic and copies ran while one was open for 4% of the time, Pallas kernels for 0%

commit v1 on v0

v1 whole, which is shorter than its diff:
```python
import functools
import math

import jax
import jax.numpy as jnp
import numpy as np
from jax import lax
from jax.experimental import pallas as pl
from jax.experimental.pallas import tpu as pltpu
from jax.sharding import PartitionSpec as P

G = 32
EPS = 1e-05
SPLIT = (8, 8, 16)
NT = (((1,), (1,)), ((), ()))
TN = (((0,), (0,)), ((), ()))
VMEM = pl.BlockSpec(memory_space=pltpu.VMEM)
LIMIT = 40 * 1024 * 1024


def params():
    return pltpu.CompilerParams(vmem_limit_bytes=LIMIT)


def block_of(size, most):
    return max(n for n in range(1, min(size, most) + 1) if size % n == 0)


def chunks_of(gates):
    sizes = SPLIT if sum(SPLIT) == gates else (gates,)
    found, end = [], gates
    for size in sizes:
        found.append((end - size, size))
        end -= size
    return found


def prep_kernel(gates, echoes_ref, turned_ref, power_ref, order_ref):
    columns = order_ref.shape[0]
    pulses = columns // gates

    @pl.when(pl.program_id(0) == 0)
    def _():
        row = lax.broadcasted_iota(jnp.int32, (columns, columns), 0)
        col = lax.broadcasted_iota(jnp.int32, (columns, columns), 1)
        source = (row % pulses) * gates + row // pulses
        order_ref[...] = jnp.where(source == col, 1.0, 0.0).astype(jnp.bfloat16)

    power = None
    for part in range(2):
        turned = lax.dot_general(order_ref[...], echoes_ref[part], NT, preferred_element_type=jnp.float32)
        turned_ref[part] = turned.astype(jnp.bfloat16)
        term = jnp.sum(turned * turned, axis=0, keepdims=True)
        power = term if power is None else power + term
    power_ref[...] = power


def prep(echoes, gates):
    _, chans, columns = echoes.shape
    width = block_of(chans, 256)
    return pl.pallas_call(
        functools.partial(prep_kernel, gates),
        grid=(chans // width,),
        in_specs=[pl.BlockSpec((2, width, columns), lambda i: (0, i, 0))],
        out_specs=[
            pl.BlockSpec((2, columns, width), lambda i: (0, 0, i)),
            pl.BlockSpec((1, width), lambda i: (0, i)),
        ],
        out_shape=[
            jax.ShapeDtypeStruct((2, columns, chans), jnp.bfloat16),
            jax.ShapeDtypeStruct((1, chans), jnp.float32),
        ],
        scratch_shapes=[pltpu.VMEM((columns, columns), jnp.bfloat16)],
        compiler_params=params(),
        name="prep",
    )(echoes)


def beam_kernel(first, rows, samples, b_steps, turned_ref, power_ref, order_ref, steer_ref, *rest):
    out_refs, (scaled_ref, beams_ref) = rest[:-2], rest[-2:]
    step = pl.program_id(0)
    chans = power_ref.shape[1]
    wide = steer_ref.shape[1]

    @pl.when(step == 0)
    def _():
        gain = lax.rsqrt(power_ref[...] / samples + EPS)
        real = turned_ref[0, first : first + rows].astype(jnp.float32) * gain
        imag = turned_ref[1, first : first + rows].astype(jnp.float32) * gain
        scaled_ref[:rows, :chans] = real.astype(jnp.bfloat16)
        scaled_ref[:rows, chans:] = (-imag).astype(jnp.bfloat16)
        scaled_ref[rows:, :chans] = imag.astype(jnp.bfloat16)
        scaled_ref[rows:, chans:] = real.astype(jnp.bfloat16)

    @pl.when(step < b_steps)
    def _():
        total = lax.dot_general(scaled_ref[:, :chans], steer_ref[0], NT, preferred_element_type=jnp.float32)
        total += lax.dot_general(scaled_ref[:, chans:], steer_ref[1], NT, preferred_element_type=jnp.float32)
        beams_ref[:, pl.ds(pl.multiple_of(step * wide, wide), wide)] = total.astype(jnp.bfloat16)

    @pl.when(step >= b_steps)
    def _():
        beam_total, slots = beams_ref.shape[1], order_ref.shape[1]
        row = lax.broadcasted_iota(jnp.int32, (beam_total, slots), 0)
        pick = jnp.where(row == order_ref[...], 1.0, 0.0).astype(jnp.bfloat16)
        picked = jnp.dot(beams_ref[...], pick, preferred_element_type=jnp.float32).astype(jnp.bfloat16)
        per = (pl.num_programs(0) - b_steps) // len(out_refs)
        for index, out_ref in enumerate(out_refs):

            @pl.when((step - b_steps) // per == index)
            def _(out_ref=out_ref):
                out_ref[...] = picked


def form_beams(turned, power, order, steer, first, rows, samples, tiles):
    _, columns, chans = turned.shape
    beam_total = steer.shape[1]
    tile_beams = beam_total // tiles
    wide = block_of(beam_total, 512)
    slots = block_of(tile_beams, 512)
    b_steps, per = beam_total // wide, tile_beams // slots
    steps = b_steps + per * tiles

    def out_map(index):
        return lambda i: (0, jnp.clip(i - b_steps - index * per, 0, per - 1))

    return pl.pallas_call(
        functools.partial(beam_kernel, first, rows, samples, b_steps),
        grid=(steps,),
        in_specs=[
            pl.BlockSpec((2, columns, chans), lambda i: (0, 0, 0)),
            pl.BlockSpec((1, chans), lambda i: (0, 0)),
            pl.BlockSpec((1, slots), lambda i: (0, jnp.maximum(i - b_steps, 0))),
            pl.BlockSpec((2, wide, chans), lambda i: (0, jnp.minimum(i, b_steps - 1), 0)),
        ],
        out_specs=[pl.BlockSpec((2 * rows, slots), out_map(index)) for index in range(tiles)],
        out_shape=[jax.ShapeDtypeStruct((2 * rows, tile_beams), jnp.bfloat16)] * tiles,
        scratch_shapes=[
            pltpu.VMEM((2 * rows, 2 * chans), jnp.bfloat16),
            pltpu.VMEM((2 * rows, beam_total), jnp.bfloat16),
        ],
        compiler_params=params(),
        cost_estimate=pl.CostEstimate(
            flops=4 * rows * beam_total * (2 * chans + beam_total),
            bytes_accessed=steer.size * 2 + turned.size * 2 + 4 * rows * beam_total,
            transcendentals=0,
        ),
        name="beams",
    )(turned, power, order, steer)


def compress_kernel(pulses, taps, parts_in, halo, keep_ahead, own, code_ref, at_ref, lens_ref, limits_ref, *rest):
    part_refs, rest = rest[:parts_in], rest[parts_in:]
    if halo:
        ahead_ref, rest = rest[0], rest[1:]
    out_ref, rest = rest[0], rest[1:]
    if keep_ahead:
        beams_ref, rest = rest[0], rest[1:]
    (wide_ref,) = rest
    rows = part_refs[0].shape[0] // 2
    edge = (taps - 1) * pulses
    lanes = part_refs[0].shape[1]
    for part in range(2):
        total = part_refs[0][part * rows : (part + 1) * rows].astype(jnp.float32)
        for ref in part_refs[1:]:
            total += ref[part * rows : (part + 1) * rows].astype(jnp.float32)
        rounded = total.astype(jnp.bfloat16)
        if keep_ahead:
            beams_ref[part] = rounded[:edge]
        wide_ref[part, :rows] = rounded.astype(jnp.float32)
        if halo:
            wide_ref[part, rows:] = ahead_ref[part].astype(jnp.float32)
        else:
            wide_ref[part, rows:] = jnp.zeros((edge, lanes), jnp.float32)
    lens, limits = lens_ref[...], limits_ref[...]
    pulse = at_ref[0] + lax.broadcasted_iota(jnp.int32, (pulses, lanes), 0)
    keep = pulse < limits
    factors = [
        (jnp.where(tap < lens, code_ref[0, tap], 0.0), jnp.where(tap < lens, code_ref[1, tap], 0.0))
        for tap in range(taps)
    ]
    for gate in range(rows // pulses):
        real = imag = None
        for tap, (code_re, code_im) in enumerate(factors):
            start = (gate + tap) * pulses
            shift_re = wide_ref[0, start : start + pulses]
            shift_im = wide_ref[1, start : start + pulses]
            term_re = code_re * shift_re + code_im * shift_im
            term_im = code_re * shift_im - code_im * shift_re
            real = term_re if real is None else real + term_re
            imag = term_im if imag is None else imag + term_im
        real = jnp.where(keep, real, 0.0)
        imag = jnp.where(keep, imag, 0.0)
        for owner in range(lanes // own):
            block = jnp.concatenate(
                [real[:, owner * own : (owner + 1) * own], imag[:, owner * own : (owner + 1) * own]], axis=1
            )
            out_ref[owner, gate * pulses : (gate + 1) * pulses] = block.astype(jnp.bfloat16)


def compress(parts, ahead, code, at, lens, limits, pulses, owners, keep_ahead):
    taps = code.shape[1]
    rows, tile_beams = parts[0].shape[0] // 2, parts[0].shape[1]
    own = tile_beams // owners
    lanes = block_of(tile_beams, 256)
    edge = (taps - 1) * pulses
    flat = pl.BlockSpec((2 * rows, lanes), lambda i: (0, i))
    line = pl.BlockSpec((1, lanes), lambda i: (0, i))
    edges = pl.BlockSpec((2, edge, lanes), lambda i: (0, 0, i))
    scalars = pl.BlockSpec(memory_space=pltpu.SMEM)
    out_specs = [pl.BlockSpec((lanes // own, rows, 2 * own), lambda i: (i, 0, 0))]
    out_shape = [jax.ShapeDtypeStruct((owners, rows, 2 * own), jnp.bfloat16)]
    if keep_ahead:
        out_specs.append(edges)
        out_shape.append(jax.ShapeDtypeStruct((2, edge, tile_beams), jnp.bfloat16))
    halo = [] if ahead is None else [ahead]
    done = pl.pallas_call(
        functools.partial(compress_kernel, pulses, taps, len(parts), len(halo), keep_ahead, own),
        grid=(tile_beams // lanes,),
        in_specs=[scalars, scalars, line, line] + [flat] * len(parts) + [edges] * len(halo),
        out_specs=out_specs,
        out_shape=out_shape,
        scratch_shapes=[pltpu.VMEM((2, rows + edge, lanes), jnp.float32)],
        compiler_params=params(),
        cost_estimate=pl.CostEstimate(
            flops=rows * tile_beams * 8 * taps, bytes_accessed=rows * tile_beams * 12, transcendentals=0
        ),
        name="compress",
    )(code, at, lens, limits, *parts, *halo)
    return done if keep_ahead else (done[0], None)


def doppler_kernel(pulses, got_ref, table_ref, *rest):
    out_ref, lines_ref = rest[-2:]
    owners, rows, lanes = got_ref.shape
    own, bins = lanes // 2, table_ref.shape[1] // 2
    gates = rows // pulses
    for gate in range(gates):
        values = got_ref[:, gate * pulses : (gate + 1) * pulses].reshape(owners * pulses, lanes)
        both = lax.dot_general(values, table_ref[...], TN, preferred_element_type=jnp.float32)
        real = both[:own, :bins] - both[own:, bins:]
        imag = both[own:, :bins] + both[:own, bins:]
        for part, values in enumerate((real, imag)):
            for at in range(lines_ref.shape[0]):
                lines_ref[at, pl.ds(part * gates + gate, own, stride=2 * gates), :] = values[:, at * 128 : (at + 1) * 128]
    for at in range(lines_ref.shape[0]):
        out_ref[:, :, :, at * 128 : (at + 1) * 128] = lines_ref[at].reshape(own, 2, gates, 128)


def doppler(got, table, out, first, pulses):
    owners, rows, lanes = got.shape
    own, bins, gates = lanes // 2, table.shape[1] // 2, rows // pulses
    return pl.pallas_call(
        functools.partial(doppler_kernel, pulses),
        grid=(1,),
        in_specs=[
            pl.BlockSpec(got.shape, lambda i: (0, 0, 0)),
            pl.BlockSpec(table.shape, lambda i: (0, 0)),
        ]
        + ([] if out is None else [pl.BlockSpec(memory_space=pl.ANY)]),
        out_specs=pl.BlockSpec((own, 2, gates, bins), lambda i: (0, 0, first // gates, 0)),
        out_shape=jax.ShapeDtypeStruct((own, 2, G, bins), jnp.float32),
        scratch_shapes=[pltpu.VMEM((bins // 128, own * 2 * gates, 128), jnp.float32)],
        input_output_aliases={} if out is None else {2: 0},
        compiler_params=params(),
        cost_estimate=pl.CostEstimate(
            flops=rows * lanes * owners * bins * 4, bytes_accessed=got.size * 2 + own * 8 * gates * bins, transcendentals=0
        ),
        name="doppler",
    )(got, table, *([] if out is None else [out]))


def phase_table(total):
    angle = np.outer(np.arange(total), np.arange(total)) % total * (2.0 * math.pi / total)
    return np.concatenate([np.cos(angle), -np.sin(angle)], axis=1) / math.sqrt(total)


def sum_over(values, axis):
    size = lax.axis_size(axis)
    if size & (size - 1):
        return lax.psum(values, axis)
    step = 1
    while step < size:
        values = values + lax.ppermute(values, axis, [(i, i ^ step) for i in range(size)])
        step *= 2
    return values


def on_device(echoes, steer, code, beam_order, dwell, code_len):
    tiles, owners = lax.axis_size("tile"), lax.axis_size("beam")
    columns = echoes.shape[2]
    beam_total = steer.shape[1]
    pulses = columns // G
    total = pulses * owners
    tile_beams = beam_total // tiles
    own = tile_beams // owners

    turned, local = prep(echoes, G)
    power = sum_over(local, "beam")

    mine = lax.axis_index("tile")
    order = jnp.roll(beam_order, -mine * tile_beams)
    here = order[:tile_beams]
    match = jnp.arange(beam_total, dtype=jnp.int32)[:, None] == here[None, :]
    both = jnp.sum(jnp.where(match, (dwell * 16 + code_len)[:, None], 0), axis=0)
    lens, limits = (both % 16)[None, :], (both // 16)[None, :]
    at = (lax.axis_index("beam") * pulses)[None]
    taps = code.astype(jnp.float32)
    table = jnp.asarray(phase_table(total).astype(jnp.bfloat16))

    out = ahead = None
    chunks = chunks_of(G)
    for number, (gate, gates) in enumerate(chunks):
        with jax.named_scope("beams"):
            parts = form_beams(
                turned, power, order[None, :], steer, gate * pulses, gates * pulses, total * G, tiles
            )
        with jax.named_scope("tile_sum"):
            parts = [parts[0]] + [
                lax.ppermute(part, "tile", [(i, (i + away) % tiles) for i in range(tiles)])
                for away, part in enumerate(parts[1:], 1)
            ]
        with jax.named_scope("compress"):
            ready, ahead = compress(
                parts, ahead, taps, at, lens, limits, pulses, owners, number < len(chunks) - 1
            )
        with jax.named_scope("to_owners"):
            got = lax.all_to_all(ready, "beam", split_axis=0, concat_axis=0)
        with jax.named_scope("doppler"):
            out = doppler(got, table, out, gate, pulses)
    return out


def solution(mesh):
    placed = (P(None, "tile", "beam"), P(None, None, "tile"), P(), P(), P(), P())
    return jax.shard_map(
        on_device,
        mesh=mesh,
        in_specs=placed,
        out_specs=P(("tile", "beam"), None, None, None),
        check_vma=False,
    )
```

time: 348 us -> 140 us (0.40)
  local copies, waits for them, and re-layouts: 129 us -> 12.5 us
  blocking collectives: 76.5 us -> 0 us
  other arithmetic: 58.6 us -> 2.56 us
  Pallas kernels: 0 us -> 46 us
  starting transfers between devices: 0.01 us -> 31.5 us
  matrix products: 18.2 us -> 0 us
  between operations: 13.6 us -> 0.15 us
    gather x3 -> x0, local copies, waits for them, and re-layouts: 66.9 us -> none  [the longest x1 54.6 us: on_device(): ordered = jnp.take(steer, beam_order, axis=1)]
    all_to_all x1 -> x0, blocking collectives: 54.1 us -> none  [on_device(): lax.all_to_all(compressed, 'beam', split_axis=0, concat_axis=2, tiled=True)]
    reduce_scatter x1 -> x0, waiting for transfers between devices: 48.9 us -> none  [on_device(): lax.psum_scatter(jnp.dot(stacked, flat, preferred_element_type=jnp.float3...]
    pallas_call x0 -> x10, Pallas kernels: none -> 46 us  [the longest x3 26.6 us: form_beams(): pl.pallas_call(functools.partial(beam_kernel, first, rows, samples, b_ste...]
    add x3 -> x5, other arithmetic: 40.8 us -> 0.74 us  [the longest x1 0.72 us: on_device(): dwell * 16 + code_len]
    ppermute x0 -> x7, waiting for transfers between devices: none -> 24.8 us  [the longest x3 20.7 us: on_device(): lax.ppermute(part, 'tile', [(i, (i + away) % tiles) for i in range(tiles)])]
    all_to_all x0 -> x3, starting transfers between devices: none -> 24.4 us  [on_device(): got = lax.all_to_all(ready, 'beam', split_axis=0, concat_axis=0)]
    psum x1 -> x0, blocking collectives: 22.3 us -> none  [on_device(): power = lax.psum(local_power, 'beam') / (pulses_all * G)]
  transfers between devices with their start and end apart: 1 -> 10, of which waited for: 1 -> 7; matrix products, arithmetic and copies ran while one was open for 4% -> 2% of each run, Pallas kernels for 0% -> 22%
where the time goes in v1:
time: 140 us; the launch traced here: 139 us
  waiting for transfers between devices  46.1 us (33%)
  Pallas kernels  46 us (33%)
  starting transfers between devices  31.5 us (22%)
  local copies, waits for them, and re-layouts  12.5 us (9%)
  other arithmetic  2.56 us (2%)
    pallas_call x3, Pallas kernels, form_beams(): pl.pallas_call(functools.partial(beam_kernel, first, rows, samples, b_ste...  26.6 us
    all_to_all x3, starting transfers between devices, on_device(): got = lax.all_to_all(ready, 'beam', split_axis=0, concat_axis=0)  24.4 us
    all_to_all x3, waiting for transfers between devices, on_device(): got = lax.all_to_all(ready, 'beam', split_axis=0, concat_axis=0)  21.3 us
    ppermute x3, waiting for transfers between devices, on_device(): lax.ppermute(part, 'tile', [(i, (i + away) % tiles) for i in range(tiles)])  20.7 us
    unnamed x22, local copies, waits for them, and re-layouts  12.5 us
    pallas_call x3, Pallas kernels, compress(): pl.pallas_call(functools.partial(compress_kernel, pulses, taps, len(parts...  9.94 us
    pallas_call x3, Pallas kernels, doppler(): pl.pallas_call(functools.partial(doppler_kernel, pulses), grid=(1,), in_s...  7.01 us
    ppermute x4, starting transfers between devices, sum_over(): lax.ppermute(values, axis, [(i, i ^ step) for i in range(size)])  4.29 us
  transfers between devices with their start and end apart: 10, of which 7 were waited for; matrix products, arithmetic and copies ran while one was open for 2% of the time, Pallas kernels for 22%

profile of v1, /device:TPU:9, one launch (start us, length us, event | category | flops | bytes accessed | tf_op | source)
XLA Modules:
  0.0 138.9 jit_solution(13405781089227851835)
XLA Ops:
  0.0 0.0 copy-start.1
  0.0 1.6 %copy-done.1 = bf16[2,1024,512]{2,1,0:T(8,128)(2,1)S(1)} copy-done((bf16[2,1024,512]{2,1,0:T(8,128)(2,1)S(1)}, bf16[2,1024,512]{2,1,0:T(8,128)(2,1)}, u32[]{:S(2)}) %copy-start.1) | copy-done | bytes 2097176
  1.6 2.5 %prep.1 = (bf16[2,512,1024]{2,1,0:T(8,128)(2,1)S(1)}, f32[1,1024]{1,0:T(1,128)S(1)}) custom-call(bf16[2,1024,512]{2,1,0:T(8,128)(2,1)S(1)} %copy-done.1), custom_call_target="tpu_custom_call" | custom-call | tf_op jit(solution)/shard_map/prep/pallas_call | solution.py:61
  4.1 0.0 copy-start.8
  4.1 0.0 copy-start.10
  4.1 0.7 collective-permute-start
  4.8 0.8 collective-permute-done
  5.7 1.2 collective-permute-start.1
  6.9 1.2 collective-permute-done.1
  8.1 0.0 collective-permute-start.2
  8.1 0.7 multiply_add_fusion
  8.9 1.7 %collective-permute-done.2 = f32[1,1024]{1,0:T(1,128)S(1)} collective-permute-done((f32[1,1024]{1,0:T(1,128)S(1)}, f32[1,1024]{1,0:T(1,128)S(1)}, u32[]{:S(2)}, u32[]{:S(2)}) %collective-permute-start.2) | collective-permute-done | bytes 4128 | tf_op jit(solution)/shard_map/ppermute | solution.py:284
  10.6 2.3 %collective-permute-start.3 = (f32[1,1024]{1,0:T(1,128)S(1)}, f32[1,1024]{1,0:T(1,128)S(1)}, u32[]{:S(2)}, u32[]{:S(2)}) collective-permute-start(f32[1,1024]{1,0:T(1,128)S(1)} %add.52), channel_id=1, source_target_pairs={{0,8},{1,9},{2,10},{3,11},{4,12},{5,13},{6,14},{7,15},{8,0},{9,1},... | collective-permute-start | bytes 12296 | tf_op jit(solution)/shard_map/ppermute | solution.py:284
  12.9 0.7 fusion
  13.6 0.3 collective-permute-done.3
  14.0 0.0 copy-start.5
  14.0 3.4 %copy-done.5 = bf16[2,2048,1024]{2,1,0:T(8,128)(2,1)S(1)} copy-done((bf16[2,2048,1024]{2,1,0:T(8,128)(2,1)S(1)}, bf16[2,2048,1024]{2,1,0:T(8,128)(2,1)}, u32[]{:S(2)}) %copy-start.5) | copy-done | bytes 8388632
  17.3 7.1 %beams.5 = (bf16[256,1024]{1,0:T(8,128)(2,1)S(1)}, bf16[256,1024]{1,0:T(8,128)(2,1)S(1)}) custom-call(bf16[2,512,1024]{2,1,0:T(8,128)(2,1)S(1)} %get-tuple-element.17.turned_ref, f32[1,1024]{1,0:T(1,128)S(1)} %add.53.power_ref, s32[1,2048]{1,0:T(1,128)S(1)} %bitcast.3, bf16[2,2048,1024]{2,1,0:T(8,128)(2,1)S(1)} %copy-done.5), custom_call_target="tpu_custom_call" | custom-call | flops 4294967296 | bytes 11534336 | tf_op jit(solution)/shard_map/beams/beams/pallas_call | solution.py:127
  24.5 0.0 copy-done.8
  24.5 1.3 collective-permute-start.6
  25.7 1.1 select_reduce_fusion
  26.8 0.0 copy-done.10
  26.9 7.2 %collective-permute-done.6.rest_1_ = bf16[256,1024]{1,0:T(8,128)(2,1)S(1)} collective-permute-done((bf16[256,1024]{1,0:T(8,128)(2,1)S(1)}, bf16[256,1024]{1,0:T(8,128)(2,1)S(1)}, u32[]{:S(2)}, u32[]{:S(2)}) %collective-permute-start.6) | collective-permute-done | bytes 524320 | tf_op jit(solution)/shard_map/tile_sum/ppermute | solution.py:320
  34.1 3.0 %compress.3 = (bf16[16,128,128]{2,1,0:T(8,128)(2,1)}, bf16[2,112,1024]{2,1,0:T(8,128)(2,1)S(1)}) custom-call(f32[2,8]{1,0:T(2,128)S(1)} %convert_element_type.3.code_ref, s32[1]{0:T(128)} %bitcast.at_ref, s32[1,1024]{1,0:T(1,128)S(1)} %and_select_fusion.1.lens_ref, s32[1,1024]{1,0:T(1,128)S(1)} %get-tuple-element.29.limits_ref, ...), custom_call_target="tpu_custom_call" | custom-call | flops 8388608 | bytes 1572864 | tf_op jit(solution)/shard_map/compress/compress/pallas_call | solution.py:217
  37.1 10.7 %all-to-all-start.2 = ((bf16[16,128,128]{2,1,0:T(8,128)(2,1)}), bf16[16,128,128]{2,1,0:T(8,128)(2,1)S(1)}, u32[]{:S(2)}, u32[]{:S(2)}) async-start(bf16[16,128,128]{2,1,0:T(8,128)(2,1)} %get-tuple-element.28), calls=%async_computation.2 | async-start | bytes 1048576 | tf_op jit(solution)/shard_map/to_owners/all_to_all | solution.py:328
  47.8 0.0 copy-start.6
  47.8 3.4 %copy-done.6 = bf16[2,2048,1024]{2,1,0:T(8,128)(2,1)S(1)} copy-done((bf16[2,2048,1024]{2,1,0:T(8,128)(2,1)S(1)}, bf16[2,2048,1024]{2,1,0:T(8,128)(2,1)}, u32[]{:S(2)}) %copy-start.6) | copy-done | bytes 8388632
  51.2 0.0 copy-start.9
  51.2 1.6 %copy-done.9 = bf16[2,512,1024]{2,1,0:T(8,128)(2,1)S(1)} copy-done((bf16[2,512,1024]{2,1,0:T(8,128)(2,1)S(1)}, bf16[2,512,1024]{2,1,0:T(8,128)(2,1)}, u32[]{:S(2)}) %copy-start.9) | copy-done | bytes 2097176
  52.8 0.0 copy-start.7
  52.8 7.1 %beams.4 = (bf16[256,1024]{1,0:T(8,128)(2,1)S(1)}, bf16[256,1024]{1,0:T(8,128)(2,1)S(1)}) custom-call(bf16[2,512,1024]{2,1,0:T(8,128)(2,1)S(1)} %copy-done.9, f32[1,1024]{1,0:T(1,128)S(1)} %add.53.power_ref, s32[1,2048]{1,0:T(1,128)S(1)} %bitcast.4, bf16[2,2048,1024]{2,1,0:T(8,128)(2,1)S(1)} %copy-done.6), custom_call_target="tpu_custom_call" | custom-call | flops 4294967296 | bytes 11534336 | tf_op jit(solution)/shard_map/beams/beams/pallas_call | solution.py:127
  59.9 1.3 collective-permute-start.5
  61.2 0.0 copy-done.7
  61.2 12.4 %beams.3 = (bf16[512,1024]{1,0:T(8,128)(2,1)S(1)}, bf16[512,1024]{1,0:T(8,128)(2,1)}) custom-call(bf16[2,512,1024]{2,1,0:T(8,128)(2,1)S(1)} %copy-done.9, f32[1,1024]{1,0:T(1,128)S(1)} %add.53.power_ref, s32[1,2048]{1,0:T(1,128)S(1)} %bitcast.5, bf16[2,2048,1024]{2,1,0:T(8,128)(2,1)S(1)} %copy-done.7), custom_call_target="tpu_custom_call" | custom-call | flops 8589934592 | bytes 12582912 | tf_op jit(solution)/shard_map/beams/beams/pallas_call | solution.py:127
  73.6 0.0 copy-start
  73.6 0.2 collective-permute-start.4
  73.8 0.0 collective-permute-done.5.rest_1_
  73.8 2.4 %compress.4 = (bf16[16,128,128]{2,1,0:T(8,128)(2,1)S(1)}, bf16[2,112,1024]{2,1,0:T(8,128)(2,1)S(1)}) custom-call(f32[2,8]{1,0:T(2,128)S(1)} %convert_element_type.3.code_ref, s32[1]{0:T(128)} %bitcast.at_ref, s32[1,1024]{1,0:T(1,128)S(1)} %and_select_fusion.1.lens_ref, s32[1,1024]{1,0:T(1,128)S(1)} %get-tuple-element.29.limits_ref, ...), custom_call_target="tpu_custom_call" | custom-call | flops 8388608 | bytes 1572864 | tf_op jit(solution)/shard_map/compress/compress/pallas_call | solution.py:217
  76.3 0.0 copy-start.2
  76.3 0.8 copy-done.2
  77.1 0.0 copy-start.3
  77.1 0.8 copy-done.3
  77.8 0.0 all-to-all-done.2.got_ref
  77.8 6.6 %all-to-all-start.1 = ((bf16[16,128,128]{2,1,0:T(8,128)(2,1)}), bf16[16,128,128]{2,1,0:T(8,128)(2,1)S(1)}, u32[]{:S(2)}, u32[]{:S(2)}) async-start(bf16[16,128,128]{2,1,0:T(8,128)(2,1)} %copy-done.2), calls=%async_computation.1 | async-start | bytes 1048576 | tf_op jit(solution)/shard_map/to_owners/all_to_all | solution.py:328
  84.4 13.4 %collective-permute-done.4.rest_1_ = bf16[512,1024]{1,0:T(8,128)(2,1)S(1)} collective-permute-done((bf16[512,1024]{1,0:T(8,128)(2,1)}, bf16[512,1024]{1,0:T(8,128)(2,1)S(1)}, u32[]{:S(2)}, u32[]{:S(2)}) %collective-permute-start.4) | collective-permute-done | bytes 1048608 | tf_op jit(solution)/shard_map/tile_sum/ppermute | solution.py:320
  97.9 0.0 copy-start.4
  97.9 1.0 copy-done.4
  98.9 4.5 %compress.5 = bf16[16,256,128]{2,1,0:T(8,128)(2,1)} custom-call(f32[2,8]{1,0:T(2,128)S(1)} %convert_element_type.3.code_ref, s32[1]{0:T(128)} %bitcast.at_ref, s32[1,1024]{1,0:T(1,128)S(1)} %and_select_fusion.1.lens_ref, s32[1,1024]{1,0:T(1,128)S(1)} %get-tuple-element.29.limits_ref, bf16[512,1024]{1,0:T(8,128)(2,1)S(1)} %get-tuple-element.19.rest_0_, ...), custom_call_target="tpu_custom_call" | custom-call | flops 16777216 | bytes 3145728 | tf_op jit(solution)/shard_map/compress/compress/pallas_call | solution.py:217
  103.4 0.0 all-to-all-done.1.got_ref
  103.4 7.2 %all-to-all-start = ((bf16[16,256,128]{2,1,0:T(8,128)(2,1)}), bf16[16,256,128]{2,1,0:T(8,128)(2,1)S(1)}, u32[]{:S(2)}, u32[]{:S(2)}) async-start(bf16[16,256,128]{2,1,0:T(8,128)(2,1)} %compress.5), calls=%async_computation | async-start | bytes 2097152 | tf_op jit(solution)/shard_map/to_owners/all_to_all | solution.py:328
  110.6 0.0 copy-done
  110.6 1.8 %doppler.3.rest_0_ = f32[64,2,32,256]{3,2,1,0:T(8,128)} custom-call(bf16[16,128,128]{2,1,0:T(8,128)(2,1)S(1)} %all-to-all-done.2.got_ref, bf16[256,512]{1,0:T(8,128)(2,1)S(1)} %copy-done), custom_call_target="tpu_custom_call" | custom-call | flops 268435456 | bytes 1572864 | tf_op jit(solution)/shard_map/doppler/doppler/pallas_call | solution.py:253
  112.3 1.8 %doppler.4.rest_0_ = f32[64,2,32,256]{3,2,1,0:T(8,128)} custom-call(bf16[16,128,128]{2,1,0:T(8,128)(2,1)S(1)} %all-to-all-done.1.got_ref, bf16[256,512]{1,0:T(8,128)(2,1)S(1)} %copy-done, f32[64,2,32,256]{3,2,1,0:T(8,128)} %doppler.3.rest_0_), custom_call_target="tpu_custom_call", output_to_operand_aliasing={{}: (2, {})} | custom-call | flops 268435456 | bytes 1572864 | tf_op jit(solution)/shard_map/doppler/doppler/pallas_call | solution.py:253
  114.1 21.3 %all-to-all-done.got_ref = bf16[16,256,128]{2,1,0:T(8,128)(2,1)S(1)} async-done(((bf16[16,256,128]{2,1,0:T(8,128)(2,1)}), bf16[16,256,128]{2,1,0:T(8,128)(2,1)S(1)}, u32[]{:S(2)}, u32[]{:S(2)}) %all-to-all-start) | async-done | bytes 1048608 | tf_op jit(solution)/shard_map/to_owners/all_to_all | solution.py:328
  135.4 3.5 %doppler.5 = f32[64,2,32,256]{3,2,1,0:T(8,128)} custom-call(bf16[16,256,128]{2,1,0:T(8,128)(2,1)S(1)} %all-to-all-done.got_ref, bf16[256,512]{1,0:T(8,128)(2,1)S(1)} %copy-done, f32[64,2,32,256]{3,2,1,0:T(8,128)} %doppler.4.rest_0_), custom_call_target="tpu_custom_call", output_to_operand_aliasing={{}: (2, {})} | custom-call | flops 536870912 | bytes 3145728 | tf_op jit(solution)/shard_map/doppler/doppler/pallas_call | solution.py:253
  (8 shorter events, 0.1 us)
Async XLA Ops:
  0.0 1.6 %copy-start.1 = (bf16[2,1024,512]{2,1,0:T(8,128)(2,1)S(1)}, bf16[2,1024,512]{2,1,0:T(8,128)(2,1)}, u32[]{:S(2)}) copy-start(bf16[2,1024,512]{2,1,0:T(8,128)(2,1)} %echoes_ref.1) | copy-start | bytes 6291460
  4.1 20.4 %copy-start.8 = (bf16[2,512,1024]{2,1,0:T(8,128)(2,1)}, bf16[2,512,1024]{2,1,0:T(8,128)(2,1)S(1)}, u32[]{:S(2)}) copy-start(bf16[2,512,1024]{2,1,0:T(8,128)(2,1)S(1)} %get-tuple-element.17.turned_ref) | copy-start | bytes 6291460
  4.1 22.7 %copy-start.10 = (bf16[2,8]{1,0:T(2,128)(2,1)S(1)}, bf16[2,8]{1,0:T(2,128)(2,1)}, u32[]{:S(2)}) copy-start(bf16[2,8]{1,0:T(2,128)(2,1)} %param.9) | copy-start | bytes 100
  4.1 1.6 %collective-permute-start = (f32[1,1024]{1,0:T(1,128)S(1)}, f32[1,1024]{1,0:T(1,128)S(1)}, u32[]{:S(2)}, u32[]{:S(2)}) collective-permute-start(f32[1,1024]{1,0:T(1,128)S(1)} %get-tuple-element.18), channel_id=1, source_target_pairs={{0,1},{1,0},{2,3},{3,2},{4,5},{5,4},{6,7},{7,6},{8,9},{9,8},{10,11... | collective-permute-start | bytes 12296 | tf_op jit(solution)/shard_map/ppermute | solution.py:284
  5.7 2.5 %collective-permute-start.1 = (f32[1,1024]{1,0:T(1,128)S(1)}, f32[1,1024]{1,0:T(1,128)S(1)}, u32[]{:S(2)}, u32[]{:S(2)}) collective-permute-start(f32[1,1024]{1,0:T(1,128)S(1)} %add.50), channel_id=1, source_target_pairs={{0,2},{1,3},{2,0},{3,1},{4,6},{5,7},{6,4},{7,5},{8,10},{9,11},{10,... | collective-permute-start | bytes 12296 | tf_op jit(solution)/shard_map/ppermute | solution.py:284
  8.1 2.5 %collective-permute-start.2 = (f32[1,1024]{1,0:T(1,128)S(1)}, f32[1,1024]{1,0:T(1,128)S(1)}, u32[]{:S(2)}, u32[]{:S(2)}) collective-permute-start(f32[1,1024]{1,0:T(1,128)S(1)} %add.51), channel_id=1, source_target_pairs={{0,4},{1,5},{2,6},{3,7},{4,0},{5,1},{6,2},{7,3},{8,12},{9,13},{10,... | collective-permute-start | bytes 12296 | tf_op jit(solution)/shard_map/ppermute | solution.py:284
  10.6 3.4 %collective-permute-start.3 = (f32[1,1024]{1,0:T(1,128)S(1)}, f32[1,1024]{1,0:T(1,128)S(1)}, u32[]{:S(2)}, u32[]{:S(2)}) collective-permute-start(f32[1,1024]{1,0:T(1,128)S(1)} %add.52), channel_id=1, source_target_pairs={{0,8},{1,9},{2,10},{3,11},{4,12},{5,13},{6,14},{7,15},{8,0},{9,1},... | collective-permute-start | bytes 12296 | tf_op jit(solution)/shard_map/ppermute | solution.py:284
  14.0 3.4 %copy-start.5 = (bf16[2,2048,1024]{2,1,0:T(8,128)(2,1)S(1)}, bf16[2,2048,1024]{2,1,0:T(8,128)(2,1)}, u32[]{:S(2)}) copy-start(bf16[2,2048,1024]{2,1,0:T(8,128)(2,1)} %steer_ref.5) | copy-start | bytes 25165828
  24.5 9.7 %collective-permute-start.6 = (bf16[256,1024]{1,0:T(8,128)(2,1)S(1)}, bf16[256,1024]{1,0:T(8,128)(2,1)S(1)}, u32[]{:S(2)}, u32[]{:S(2)}) collective-permute-start(bf16[256,1024]{1,0:T(8,128)(2,1)S(1)} %get-tuple-element.24), channel_id=1, source_target_pairs={{0,16},{16,0},{1,17},{17,1},{2,18},{18,2},{3,19},{19,3},{4,20},{20... | collective-permute-start | bytes 1572872 | tf_op jit(solution)/shard_map/tile_sum/ppermute | solution.py:320
  37.1 40.7 %all-to-all-start.2 = ((bf16[16,128,128]{2,1,0:T(8,128)(2,1)}), bf16[16,128,128]{2,1,0:T(8,128)(2,1)S(1)}, u32[]{:S(2)}, u32[]{:S(2)}) async-start(bf16[16,128,128]{2,1,0:T(8,128)(2,1)} %get-tuple-element.28), calls=%async_computation.2 | async-start | bytes 1048576 | tf_op jit(solution)/shard_map/to_owners/all_to_all | solution.py:328
  47.8 3.4 %copy-start.6 = (bf16[2,2048,1024]{2,1,0:T(8,128)(2,1)S(1)}, bf16[2,2048,1024]{2,1,0:T(8,128)(2,1)}, u32[]{:S(2)}) copy-start(bf16[2,2048,1024]{2,1,0:T(8,128)(2,1)} %steer_ref.5) | copy-start | bytes 25165828
  51.2 1.6 %copy-start.9 = (bf16[2,512,1024]{2,1,0:T(8,128)(2,1)S(1)}, bf16[2,512,1024]{2,1,0:T(8,128)(2,1)}, u32[]{:S(2)}) copy-start(bf16[2,512,1024]{2,1,0:T(8,128)(2,1)} %copy-done.8) | copy-start | bytes 6291460
  52.8 8.4 %copy-start.7 = (bf16[2,2048,1024]{2,1,0:T(8,128)(2,1)S(1)}, bf16[2,2048,1024]{2,1,0:T(8,128)(2,1)}, u32[]{:S(2)}) copy-start(bf16[2,2048,1024]{2,1,0:T(8,128)(2,1)} %steer_ref.5) | copy-start | bytes 25165828
  59.9 14.0 %collective-permute-start.5 = (bf16[256,1024]{1,0:T(8,128)(2,1)S(1)}, bf16[256,1024]{1,0:T(8,128)(2,1)S(1)}, u32[]{:S(2)}, u32[]{:S(2)}) collective-permute-start(bf16[256,1024]{1,0:T(8,128)(2,1)S(1)} %get-tuple-element.22), channel_id=1, source_target_pairs={{0,16},{16,0},{1,17},{17,1},{2,18},{18,2},{3,19},{19,3},{4,20},{20... | collective-permute-start | bytes 1572872 | tf_op jit(solution)/shard_map/tile_sum/ppermute | solution.py:320
  73.6 37.0 %copy-start = (bf16[256,512]{1,0:T(8,128)(2,1)S(1)}, bf16[256,512]{1,0:T(8,128)(2,1)}, u32[]{:S(2)}) copy-start(bf16[256,512]{1,0:T(8,128)(2,1)} %constant.64.clone.table_ref) | copy-start | bytes 786436
  73.6 24.3 %collective-permute-start.4 = (bf16[512,1024]{1,0:T(8,128)(2,1)}, bf16[512,1024]{1,0:T(8,128)(2,1)S(1)}, u32[]{:S(2)}, u32[]{:S(2)}) collective-permute-start(bf16[512,1024]{1,0:T(8,128)(2,1)} %get-tuple-element.20), channel_id=1, source_target_pairs={{0,16},{16,0},{1,17},{17,1},{2,18},{18,2},{3,19},{19,3},{4,20},{20... | collective-permute-start | bytes 3145736 | tf_op jit(solution)/shard_map/tile_sum/ppermute | solution.py:320
  76.3 0.8 copy-start.2
  77.1 0.8 copy-start.3
  77.8 25.6 %all-to-all-start.1 = ((bf16[16,128,128]{2,1,0:T(8,128)(2,1)}), bf16[16,128,128]{2,1,0:T(8,128)(2,1)S(1)}, u32[]{:S(2)}, u32[]{:S(2)}) async-start(bf16[16,128,128]{2,1,0:T(8,128)(2,1)} %copy-done.2), calls=%async_computation.1 | async-start | bytes 1048576 | tf_op jit(solution)/shard_map/to_owners/all_to_all | solution.py:328
  97.9 1.0 copy-start.4
  103.4 32.0 %all-to-all-start = ((bf16[16,256,128]{2,1,0:T(8,128)(2,1)}), bf16[16,256,128]{2,1,0:T(8,128)(2,1)S(1)}, u32[]{:S(2)}, u32[]{:S(2)}) async-start(bf16[16,256,128]{2,1,0:T(8,128)(2,1)} %compress.5), calls=%async_computation | async-start | bytes 2097152 | tf_op jit(solution)/shard_map/to_owners/all_to_all | solution.py:328

commit v2 on v1

v2 whole, which is shorter than its diff:
```python
import functools
import math

import jax
import jax.numpy as jnp
import numpy as np
from jax import lax
from jax.experimental import pallas as pl
from jax.experimental.pallas import tpu as pltpu
from jax.sharding import PartitionSpec as P

G = 32
EPS = 1e-05
CHUNK = 8
TOGETHER = (2, 2)
NT = (((1,), (1,)), ((), ()))
TN = (((0,), (0,)), ((), ()))
MIB = 1024 * 1024


def params(mib):
    return pltpu.CompilerParams(vmem_limit_bytes=mib * MIB)


def block_of(size, most):
    return max(n for n in range(1, min(size, most) + 1) if size % n == 0)


def groups_of(gates):
    if CHUNK * sum(TOGETHER) != gates:
        return [[(0, gates)]]
    found, end = [], gates
    for count in TOGETHER:
        found.append([(end - CHUNK * (i + 1), CHUNK) for i in range(count)])
        end -= CHUNK * count
    return found


def in_hbm(*values):
    return [pltpu.with_memory_space_constraint(x, pltpu.HBM) for x in values]


def beam_kernel(samples, gates, gate, count, echoes_hbm, power_ref, order_ref, steer_hbm, *rest):
    out_refs = rest[:-7]
    echoes_ref, steer_ref, scaled_ref, row_ref, picked_ref, echoes_sem, steer_sem = rest[-7:]
    _, chans, columns = echoes_ref.shape
    beam_total, wide = steer_ref.shape[1], row_ref.shape[0]
    pulses = columns // gates
    rows = count * pulses

    def echoes_copy(part):
        return pltpu.make_async_copy(echoes_hbm.at[part], echoes_ref.at[part], echoes_sem.at[part])

    def steer_copy(part, step):
        at = pl.ds(step * wide, wide)
        return pltpu.make_async_copy(
            steer_hbm.at[part, at], steer_ref.at[part, at], steer_sem.at[part, step]
        )

    def begin(step):
        for part in range(2):
            steer_copy(part, step).start()

    steps = beam_total // wide
    for part in range(2):
        echoes_copy(part).start()
    begin(0)
    row = lax.broadcasted_iota(jnp.int32, (rows, columns), 0)
    col = lax.broadcasted_iota(jnp.int32, (rows, columns), 1)
    source = (row % pulses) * gates + row // pulses + gate
    moved = jnp.where(source == col, 1.0, 0.0).astype(jnp.bfloat16)
    row_ref[...] = lax.broadcasted_iota(jnp.int32, row_ref.shape, 0)
    gain = lax.rsqrt(power_ref[...] / samples + EPS)
    for part in range(2):
        echoes_copy(part).wait()
        if part == 0 and steps > 1:
            begin(1)
        turned = lax.dot_general(moved, echoes_ref[part], NT, preferred_element_type=jnp.float32) * gain
        if part == 0:
            scaled_ref[:rows, :chans] = turned.astype(jnp.bfloat16)
            scaled_ref[rows:, chans:] = turned.astype(jnp.bfloat16)
        else:
            scaled_ref[:rows, chans:] = (-turned).astype(jnp.bfloat16)
            scaled_ref[rows:, :chans] = turned.astype(jnp.bfloat16)

    slots = row_ref.shape[1]
    for step in range(steps):
        at = slice(step * wide, (step + 1) * wide)
        for part in range(2):
            steer_copy(part, step).wait()
        if step + 2 < steps:
            begin(step + 2)
        beams = lax.dot_general(scaled_ref[:, :chans], steer_ref[0, at], NT, preferred_element_type=jnp.float32)
        beams += lax.dot_general(scaled_ref[:, chans:], steer_ref[1, at], NT, preferred_element_type=jnp.float32)
        beams = beams.astype(jnp.bfloat16)
        for start in range(0, beam_total, slots):
            wanted = order_ref[:, start : start + slots] - step * wide
            pick = jnp.where(row_ref[...] == wanted, 1.0, 0.0).astype(jnp.bfloat16)
            picked = jnp.dot(beams, pick, preferred_element_type=jnp.float32)
            if step > 0:
                picked += picked_ref[:, start : start + slots]
            picked_ref[:, start : start + slots] = picked

    for index, out_ref in enumerate(out_refs):
        slots = out_ref.shape[1]
        out_ref[...] = picked_ref[:, index * slots : (index + 1) * slots].astype(jnp.bfloat16)


def form_beams(echoes, power, order, steer, gates, gate, count, samples, tiles):
    _, chans, columns = echoes.shape
    beam_total = steer.shape[1]
    tile_beams = beam_total // tiles
    rows = columns // gates * count
    wide = block_of(beam_total, 512)
    echoes, steer = in_hbm(echoes, steer)
    whole = pl.BlockSpec(memory_space=pltpu.VMEM)
    apart = pl.BlockSpec(memory_space=pl.ANY)
    return pl.pallas_call(
        functools.partial(beam_kernel, samples, gates, gate, count),
        in_specs=[apart, whole, whole, apart],
        out_specs=[whole] * tiles,
        out_shape=[pltpu.HBM((2 * rows, tile_beams), jnp.bfloat16)] * tiles,
        scratch_shapes=[
            pltpu.VMEM(echoes.shape, jnp.bfloat16),
            pltpu.VMEM(steer.shape, jnp.bfloat16),
            pltpu.VMEM((2 * rows, 2 * chans), jnp.bfloat16),
            pltpu.VMEM((wide, block_of(beam_total, 512)), jnp.int32),
            pltpu.VMEM((2 * rows, beam_total), jnp.float32),
            pltpu.SemaphoreType.DMA((2,)),
            pltpu.SemaphoreType.DMA((2, beam_total // wide)),
        ],
        compiler_params=params(40),
        cost_estimate=pl.CostEstimate(
            flops=4 * rows * beam_total * (2 * chans + beam_total),
            bytes_accessed=steer.size * 2 + 4 * rows * beam_total,
            transcendentals=0,
        ),
        name="beams",
    )(echoes, power, order, steer)


def compress_kernel(pulses, taps, parts_in, halo, shared, keep_ahead, own, code_ref, at_ref, lens_ref, limits_ref, *rest):
    part_refs, rest = rest[:parts_in], rest[parts_in:]
    if halo:
        ahead_ref, rest = rest[0], rest[1:]
    out_ref, rest = rest[shared], rest[shared + 1 :]
    if keep_ahead:
        beams_ref, rest = rest[0], rest[1:]
    (wide_ref,) = rest
    rows = part_refs[0].shape[0] // 2
    edge = (taps - 1) * pulses
    lanes = part_refs[0].shape[1]
    for part in range(2):
        total = part_refs[0][part * rows : (part + 1) * rows].astype(jnp.float32)
        for ref in part_refs[1:]:
            total += ref[part * rows : (part + 1) * rows].astype(jnp.float32)
        rounded = total.astype(jnp.bfloat16)
        if keep_ahead:
            beams_ref[part] = rounded[:edge]
        wide_ref[part, :rows] = rounded.astype(jnp.float32)
        if halo:
            wide_ref[part, rows:] = ahead_ref[part].astype(jnp.float32)
        else:
            wide_ref[part, rows:] = jnp.zeros((edge, lanes), jnp.float32)
    lens, limits = lens_ref[...], limits_ref[...]
    pulse = at_ref[0] + lax.broadcasted_iota(jnp.int32, (pulses, lanes), 0)
    keep = pulse < limits
    factors = [
        (jnp.where(tap < lens, code_ref[0, tap], 0.0), jnp.where(tap < lens, code_ref[1, tap], 0.0))
        for tap in range(taps)
    ]
    for gate in range(rows // pulses):
        real = imag = None
        for tap, (code_re, code_im) in enumerate(factors):
            start = (gate + tap) * pulses
            shift_re = wide_ref[0, start : start + pulses]
            shift_im = wide_ref[1, start : start + pulses]
            term_re = code_re * shift_re + code_im * shift_im
            term_im = code_re * shift_im - code_im * shift_re
            real = term_re if real is None else real + term_re
            imag = term_im if imag is None else imag + term_im
        real = jnp.where(keep, real, 0.0)
        imag = jnp.where(keep, imag, 0.0)
        for owner in range(lanes // own):
            block = jnp.concatenate(
                [real[:, owner * own : (owner + 1) * own], imag[:, owner * own : (owner + 1) * own]], axis=1
            )
            out_ref[owner, gate * pulses : (gate + 1) * pulses] = block.astype(jnp.bfloat16)


def compress(parts, ahead, code, at, lens, limits, pulses, owners, keep_ahead, ready, place, places):
    taps = code.shape[1]
    rows, tile_beams = parts[0].shape[0] // 2, parts[0].shape[1]
    own = tile_beams // owners
    lanes = block_of(tile_beams, 256)
    edge = (taps - 1) * pulses
    flat = pl.BlockSpec((2 * rows, lanes), lambda i: (0, i))
    line = pl.BlockSpec((1, lanes), lambda i: (0, i))
    edges = pl.BlockSpec((2, edge, lanes), lambda i: (0, 0, i))
    scalars = pl.BlockSpec(memory_space=pltpu.SMEM)
    out_specs = [pl.BlockSpec((lanes // own, rows, 2 * own), lambda i: (i, place, 0))]
    out_shape = [pltpu.HBM((owners, places * rows, 2 * own), jnp.bfloat16)]
    if keep_ahead:
        out_specs.append(edges)
        out_shape.append(pltpu.HBM((2, edge, tile_beams), jnp.bfloat16))
    halo = [] if ahead is None else [ahead]
    shared = [] if ready is None else [ready]
    done = pl.pallas_call(
        functools.partial(compress_kernel, pulses, taps, len(parts), len(halo), len(shared), keep_ahead, own),
        grid=(tile_beams // lanes,),
        in_specs=[scalars, scalars, line, line] + [flat] * len(parts)
        + [edges] * len(halo)
        + [pl.BlockSpec(memory_space=pl.ANY)] * len(shared),
        out_specs=out_specs,
        out_shape=out_shape,
        scratch_shapes=[pltpu.VMEM((2, rows + edge, lanes), jnp.float32)],
        input_output_aliases={4 + len(parts) + len(halo): 0} if shared else {},
        compiler_params=params(16),
        cost_estimate=pl.CostEstimate(
            flops=rows * tile_beams * 8 * taps, bytes_accessed=rows * tile_beams * 12, transcendentals=0
        ),
        name="compress",
    )(code, at, lens, limits, *parts, *halo, *shared)
    return done if keep_ahead else (done[0], None)


def doppler_kernel(pulses, got_ref, table_ref, *rest):
    out_ref, lines_ref = rest[-2:]
    owners, rows, lanes = got_ref.shape
    own, bins = lanes // 2, table_ref.shape[1] // 2
    gates = rows // pulses
    for gate in range(gates):
        values = got_ref[:, gate * pulses : (gate + 1) * pulses].reshape(owners * pulses, lanes)
        both = lax.dot_general(values, table_ref[...], TN, preferred_element_type=jnp.float32)
        real = both[:own, :bins] - both[own:, bins:]
        imag = both[own:, :bins] + both[:own, bins:]
        for part, values in enumerate((real, imag)):
            for at in range(lines_ref.shape[0]):
                lines_ref[at, pl.ds(part * gates + gate, own, stride=2 * gates), :] = values[:, at * 128 : (at + 1) * 128]
    for at in range(lines_ref.shape[0]):
        out_ref[:, :, :, at * 128 : (at + 1) * 128] = lines_ref[at].reshape(own, 2, gates, 128)


def doppler(got, table, out, first, pulses):
    owners, rows, lanes = got.shape
    own, bins, gates = lanes // 2, table.shape[1] // 2, rows // pulses
    return pl.pallas_call(
        functools.partial(doppler_kernel, pulses),
        grid=(1,),
        in_specs=[
            pl.BlockSpec(got.shape, lambda i: (0, 0, 0)),
            pl.BlockSpec(table.shape, lambda i: (0, 0)),
        ]
        + ([] if out is None else [pl.BlockSpec(memory_space=pl.ANY)]),
        out_specs=pl.BlockSpec((own, 2, gates, bins), lambda i: (0, 0, first // gates, 0)),
        out_shape=jax.ShapeDtypeStruct((own, 2, G, bins), jnp.float32),
        scratch_shapes=[pltpu.VMEM((bins // 128, own * 2 * gates, 128), jnp.float32)],
        input_output_aliases={} if out is None else {2: 0},
        compiler_params=params(24),
        cost_estimate=pl.CostEstimate(
            flops=rows * lanes * owners * bins * 4, bytes_accessed=got.size * 2 + own * 8 * gates * bins, transcendentals=0
        ),
        name="doppler",
    )(got, table, *([] if out is None else [out]))


def phase_table(total):
    angle = np.outer(np.arange(total), np.arange(total)) % total * (2.0 * math.pi / total)
    return np.concatenate([np.cos(angle), -np.sin(angle)], axis=1) / math.sqrt(total)


def sum_over(values, axis):
    size = lax.axis_size(axis)
    if size & (size - 1):
        return lax.psum(values, axis)
    step = 1
    while step < size:
        steps = [step * i for i in (1, 2, 3) if step * i < size] if step * 2 < size else [step]
        values = values + sum(
            lax.ppermute(values, axis, [(i, i ^ away) for i in range(size)]) for away in steps
        )
        step *= len(steps) + 1
    return values


def order_of(groups):
    count = sum(len(group) for group in groups)
    if count == 1:
        return [("beams", 0), ("compress", 0), ("send", 0), ("doppler", 0)]
    return [
        ("beams", 0),
        ("beams<beams", 0),
        ("beams", 1),
        ("beams<compress", (1, 0)),
        ("compress", 0),
        ("compress<beams", 0),
        ("beams", 2),
        ("beams<compress", (2, 1)),
        ("compress", 1),
        ("compress<beams", 1),
        ("send", 0),
        ("beams", 3),
        ("beams<compress", (3, 2)),
        ("compress", 2),
        ("compress", 3),
        ("send", 1),
        ("doppler", 0),
        ("doppler", 1),
    ]


def on_device(echoes, steer, code, beam_order, dwell, code_len):
    tiles, owners = lax.axis_size("tile"), lax.axis_size("beam")
    columns = echoes.shape[2]
    beam_total = steer.shape[1]
    pulses = columns // G
    total = pulses * owners
    tile_beams = beam_total // tiles
    own = tile_beams // owners

    values = echoes.astype(jnp.float32)
    power = sum_over(jnp.sum(values * values, axis=(0, 2))[None, :], "beam")

    mine = lax.axis_index("tile")
    order = jnp.roll(beam_order, -mine * tile_beams)
    here = order[:tile_beams]
    match = jnp.arange(beam_total, dtype=jnp.int32)[:, None] == here[None, :]
    both = jnp.sum(jnp.where(match, (dwell * 16 + code_len)[:, None], 0), axis=0)
    lens, limits = (both % 16)[None, :], (both // 16)[None, :]
    at = (lax.axis_index("beam") * pulses)[None]
    taps = code.astype(jnp.float32)
    table = jnp.asarray(phase_table(total).astype(jnp.bfloat16))

    groups = groups_of(G)
    chunks = [chunk for group in groups for chunk in group]
    owner_of = [index for index, group in enumerate(groups) for _ in group]
    firsts = [owner_of.index(index) for index in range(len(groups))]
    own_parts, others, ready, ahead, got, out = {}, {}, {}, {}, {}, None
    for kind, number in order_of(groups):
        if kind == "beams":
            gate, gates = chunks[number]
            with jax.named_scope("beams"):
                parts = form_beams(
                    echoes, power, order[None, :], steer, G, gate, gates, total * G, tiles
                )
            own_parts[number] = parts[0]
            with jax.named_scope("tile_sum"):
                others[number] = [
                    lax.ppermute(part, "tile", [(i, (i + away) % tiles) for i in range(tiles)])
                    for away, part in enumerate(parts[1:], 1)
                ]
        elif kind == "compress":
            index = owner_of[number]
            place = number - firsts[index]
            with jax.named_scope("compress"):
                ready[index], ahead[number] = compress(
                    [own_parts[number]] + others[number],
                    ahead.get(number - 1), taps, at, lens, limits, pulses, owners, number < len(chunks) - 1,
                    ready.get(index), len(groups[index]) - 1 - place, len(groups[index]),
                )
        elif kind == "send":
            with jax.named_scope("to_owners"):
                got[number] = lax.all_to_all(ready[number], "beam", split_axis=0, concat_axis=0)
        elif kind == "doppler":
            with jax.named_scope("doppler"):
                out = doppler(got[number], table, out, groups[number][-1][0], pulses)
        elif kind == "beams<beams":
            power, own_parts[number] = lax.optimization_barrier((power, own_parts[number]))
        elif kind == "beams<compress":
            own_parts[number[1]], own_parts[number[0]] = lax.optimization_barrier(
                (own_parts[number[1]], own_parts[number[0]])
            )
        elif kind == "arrived<beams":
            power, others[number][0] = lax.optimization_barrier((power, others[number][0]))
        elif kind == "arrived<doppler":
            table, others[number][0] = lax.optimization_barrier((table, others[number][0]))
        elif kind == "compress<beams":
            index = owner_of[number]
            power, ready[index] = lax.optimization_barrier((power, ready[index]))
        elif kind == "compress<doppler":
            table, ahead[number] = lax.optimization_barrier((table, ahead[number]))
        elif kind == "doppler<compress":
            ahead[number], out = lax.optimization_barrier((ahead[number], out))
        elif kind == "last<doppler":
            out, ready[number] = lax.optimization_barrier((out, ready[number]))
    return out


def solution(mesh):
    placed = (P(None, "tile", "beam"), P(None, None, "tile"), P(), P(), P(), P())
    return jax.shard_map(
        on_device,
        mesh=mesh,
        in_specs=placed,
        out_specs=P(("tile", "beam"), None, None, None),
        check_vma=False,
    )
```

time: 140 us -> 124 us (0.89)
  waiting for transfers between devices: 46.1 us -> 34.7 us
  local copies, waits for them, and re-layouts: 12.5 us -> 2.09 us
  Pallas kernels: 46 us -> 55.1 us
  starting transfers between devices: 31.5 us -> 26 us
  other arithmetic: 2.56 us -> 5.28 us
    unnamed x22 -> x18, local copies, waits for them, and re-layouts: 12.5 us -> 2.09 us
    all_to_all x3 -> x2, starting transfers between devices: 24.4 us -> 16.3 us  [on_device(): lax.all_to_all(ready[number], 'beam', split_axis=0, concat_axis=0)]
    ppermute x3 -> x4, waiting for transfers between devices: 20.7 us -> 12.6 us  [on_device(): lax.ppermute(part, 'tile', [(i, (i + away) % tiles) for i in range(tiles)])]
    pallas_call x4, Pallas kernels: 29.1 us -> 34.9 us  [form_beams(): pl.pallas_call(functools.partial(beam_kernel, samples, gates, gate, count...]
    ppermute x4 -> x6, waiting for transfers between devices: 4.11 us -> 0.67 us  [sum_over(): lax.ppermute(values, axis, [(i, i ^ away) for i in range(size)])]
    pallas_call x3 -> x4, Pallas kernels: 9.94 us -> 13.2 us  [compress(): pl.pallas_call(functools.partial(compress_kernel, pulses, taps, len(parts...]
    reduce_sum x0 -> x1, other arithmetic: none -> 2.07 us  [on_device(): power = sum_over(jnp.sum(values * values, axis=(0, 2))[None, :], 'beam')]
    ppermute x4 -> x6, starting transfers between devices: 4.29 us -> 5.9 us  [sum_over(): lax.ppermute(values, axis, [(i, i ^ away) for i in range(size)])]
  transfers between devices with their start and end apart: 10 -> 12, of which waited for: 7 -> 7; matrix products, arithmetic and copies ran while one was open for 2% -> 3% of each run, Pallas kernels for 22% -> 32%
where the time goes in v2:
time: 124 us; the launch traced here: 123 us
  Pallas kernels  55.1 us (44%)
  waiting for transfers between devices  34.7 us (28%)
  starting transfers between devices  26 us (21%)
  other arithmetic  5.28 us (4%)
  local copies, waits for them, and re-layouts  2.09 us (2%)
    pallas_call x4, Pallas kernels, form_beams(): pl.pallas_call(functools.partial(beam_kernel, samples, gates, gate, count...  34.9 us
    all_to_all x2, waiting for transfers between devices, on_device(): lax.all_to_all(ready[number], 'beam', split_axis=0, concat_axis=0)  21.3 us
    all_to_all x2, starting transfers between devices, on_device(): lax.all_to_all(ready[number], 'beam', split_axis=0, concat_axis=0)  16.3 us
    pallas_call x4, Pallas kernels, compress(): pl.pallas_call(functools.partial(compress_kernel, pulses, taps, len(parts...  13.2 us
    ppermute x4, waiting for transfers between devices, on_device(): lax.ppermute(part, 'tile', [(i, (i + away) % tiles) for i in range(tiles)])  12.6 us
    pallas_call x2, Pallas kernels, doppler(): pl.pallas_call(functools.partial(doppler_kernel, pulses), grid=(1,), in_s...  7.01 us
    ppermute x6, starting transfers between devices, sum_over(): lax.ppermute(values, axis, [(i, i ^ away) for i in range(size)])  5.9 us
    ppermute x4, starting transfers between devices, on_device(): lax.ppermute(part, 'tile', [(i, (i + away) % tiles) for i in range(tiles)])  3.89 us
  transfers between devices with their start and end apart: 12, of which 7 were waited for; matrix products, arithmetic and copies ran while one was open for 3% of the time, Pallas kernels for 32%

profile of v2, /device:TPU:9, one launch (start us, length us, event | category | flops | bytes accessed | tf_op | source)
XLA Modules:
  0.0 123.3 jit_solution(18099454140309323736)
XLA Ops:
  0.0 2.1 %multiply_reduce_fusion = f32[1024]{0:T(1024)S(1)} fusion(bf16[2,1024,512]{2,1,0:T(8,128)(2,1)} %echoes_hbm.7), kind=kLoop, calls=%fused_computation.2 | loop fusion | flops 3144704 | bytes 2101248 | tf_op jit(solution)/shard_map/reduce_sum | solution.py:322
  2.1 1.9 %collective-permute-start.2 = (f32[1,1024]{1,0:T(1,128)S(1)}, f32[1,1024]{1,0:T(1,128)S(1)}, u32[]{:S(2)}, u32[]{:S(2)}) collective-permute-start(f32[1,1024]{1,0:T(1,128)S(1)} %bitcast.8), channel_id=1, source_target_pairs={{0,3},{1,2},{2,1},{3,0},{4,7},{5,6},{6,5},{7,4},{8,11},{9,10},{10,... | collective-permute-start | bytes 12296 | tf_op jit(solution)/shard_map/ppermute | solution.py:280
  3.9 0.2 collective-permute-start.1
  4.2 0.2 collective-permute-start
  4.4 0.7 fusion
  5.1 0.7 multiply_add_fusion
  5.8 1.1 select_reduce_fusion
  6.9 0.0 collective-permute-done.2
  6.9 0.0 collective-permute-done.1
  6.9 0.0 collective-permute-done
  7.0 1.4 %collective-permute-start.5 = (f32[1,1024]{1,0:T(1,128)S(1)}, f32[1,1024]{1,0:T(1,128)S(1)}, u32[]{:S(2)}, u32[]{:S(2)}) collective-permute-start(f32[1,1024]{1,0:T(1,128)S(1)} %add_add_fusion.1), channel_id=1, source_target_pairs={{0,12},{1,13},{2,14},{3,15},{4,8},{5,9},{6,10},{7,11},{8,4},{9,5},... | collective-permute-start | bytes 12296 | tf_op jit(solution)/shard_map/ppermute | solution.py:280
  8.3 1.1 collective-permute-start.4
  9.4 1.1 collective-permute-start.3
  10.6 0.7 convert_element_type.6.code_ref
  11.2 0.0 collective-permute-done.5
  11.2 0.5 collective-permute-done.4
  11.7 0.2 collective-permute-done.3
  11.9 8.7 %beams.4 = (bf16[256,1024]{1,0:T(8,128)(2,1)}, bf16[256,1024]{1,0:T(8,128)(2,1)}) custom-call(bf16[2,1024,512]{2,1,0:T(8,128)(2,1)} %echoes_hbm.7, f32[1,1024]{1,0:T(1,128)S(1)} %add_add_fusion.power_ref, s32[1,2048]{1,0:T(1,128)S(1)} %bitcast.4, bf16[2,2048,1024]{2,1,0:T(8,128)(2,1)} %steer_hbm.7), custom_call_target="tpu_custom_call" | custom-call | flops 4294967296 | bytes 9437184 | tf_op jit(solution)/shard_map/beams/beams/pallas_call | solution.py:118
  20.6 0.0 copy-start.2
  20.6 1.3 %collective-permute-start.6 = (bf16[256,1024]{1,0:T(8,128)(2,1)}, bf16[256,1024]{1,0:T(8,128)(2,1)S(1)}, u32[]{:S(2)}, u32[]{:S(2)}) collective-permute-start(bf16[256,1024]{1,0:T(8,128)(2,1)} %get-tuple-element.37), channel_id=1, source_target_pairs={{0,16},{16,0},{1,17},{17,1},{2,18},{18,2},{3,19},{19,3},{4,20},{20... | collective-permute-start | bytes 1572872 | tf_op jit(solution)/shard_map/tile_sum/ppermute | solution.py:349
  21.9 8.7 %beams.5 = (bf16[256,1024]{1,0:T(8,128)(2,1)}, bf16[256,1024]{1,0:T(8,128)(2,1)}) custom-call(bf16[2,1024,512]{2,1,0:T(8,128)(2,1)} %echoes_hbm.7, f32[1,1024]{1,0:T(1,128)S(1)} %add_add_fusion.power_ref, s32[1,2048]{1,0:T(1,128)S(1)} %bitcast.5, bf16[2,2048,1024]{2,1,0:T(8,128)(2,1)} %steer_hbm.7), custom_call_target="tpu_custom_call" | custom-call | flops 4294967296 | bytes 9437184 | tf_op jit(solution)/shard_map/beams/beams/pallas_call | solution.py:118
  30.6 0.3 collective-permute-start.7
  30.9 1.4 %collective-permute-done.6.rest_1_ = bf16[256,1024]{1,0:T(8,128)(2,1)S(1)} collective-permute-done((bf16[256,1024]{1,0:T(8,128)(2,1)}, bf16[256,1024]{1,0:T(8,128)(2,1)S(1)}, u32[]{:S(2)}, u32[]{:S(2)}) %collective-permute-start.6) | collective-permute-done | bytes 524320 | tf_op jit(solution)/shard_map/tile_sum/ppermute | solution.py:349
  32.3 0.0 copy-done.2
  32.3 3.1 %compress.4 = (bf16[16,256,128]{2,1,0:T(8,128)(2,1)}, bf16[2,112,1024]{2,1,0:T(8,128)(2,1)}) custom-call(f32[2,8]{1,0:T(2,128)S(1)} %convert_element_type.6.code_ref, s32[1]{0:T(128)} %bitcast.at_ref, s32[1,1024]{1,0:T(1,128)S(1)} %and_select_fusion.1.lens_ref, s32[1,1024]{1,0:T(1,128)S(1)} %get-tuple-element.57.limits_ref, bf16[256,1024]{1,0:T(8,128)(2,1)S(1)} %copy-done.2, ...), custom_call_target="tpu_custom_call" | custom-call | flops 8388608 | bytes 1572864 | tf_op jit(solution)/shard_map/compress/compress/pallas_call | solution.py:208
  35.4 0.0 copy-start.3
  35.4 0.0 copy-start.6
  35.4 8.8 %beams.6 = (bf16[256,1024]{1,0:T(8,128)(2,1)}, bf16[256,1024]{1,0:T(8,128)(2,1)}) custom-call(bf16[2,1024,512]{2,1,0:T(8,128)(2,1)} %echoes_hbm.7, f32[1,1024]{1,0:T(1,128)S(1)} %add_add_fusion.power_ref, s32[1,2048]{1,0:T(1,128)S(1)} %bitcast.6, bf16[2,2048,1024]{2,1,0:T(8,128)(2,1)} %steer_hbm.7), custom_call_target="tpu_custom_call" | custom-call | flops 4294967296 | bytes 9437184 | tf_op jit(solution)/shard_map/beams/beams/pallas_call | solution.py:118
  44.2 0.0 copy-start.8
  44.2 0.3 collective-permute-done.7.rest_1_
  44.5 0.0 copy-done.3
  44.5 0.0 copy-done.6
  44.5 3.4 %compress.5 = (bf16[16,256,128]{2,1,0:T(8,128)(2,1)}, bf16[2,112,1024]{2,1,0:T(8,128)(2,1)}) custom-call(f32[2,8]{1,0:T(2,128)S(1)} %convert_element_type.6.code_ref, s32[1]{0:T(128)} %bitcast.at_ref, s32[1,1024]{1,0:T(1,128)S(1)} %and_select_fusion.1.lens_ref, s32[1,1024]{1,0:T(1,128)S(1)} %get-tuple-element.57.limits_ref, ...), custom_call_target="tpu_custom_call", output_to_operand_aliasing={{0}: (7, {})} | custom-call | flops 8388608 | bytes 1572864 | tf_op jit(solution)/shard_map/compress/compress/pallas_call | solution.py:208
  47.9 9.7 %all-to-all-start.1 = ((bf16[16,256,128]{2,1,0:T(8,128)(2,1)}), bf16[16,256,128]{2,1,0:T(8,128)(2,1)S(1)}, u32[]{:S(2)}, u32[]{:S(2)}) async-start(bf16[16,256,128]{2,1,0:T(8,128)(2,1)} %get-tuple-element.56), calls=%async_computation.1 | async-start | bytes 2097152 | tf_op jit(solution)/shard_map/to_owners/all_to_all | solution.py:363
  57.6 0.0 copy-done.8
  57.7 0.0 copy-start.1
  57.7 0.0 copy-start.5
  57.7 2.2 %collective-permute-start.9 = (bf16[256,1024]{1,0:T(8,128)(2,1)S(1)}, bf16[256,1024]{1,0:T(8,128)(2,1)S(1)}, u32[]{:S(2)}, u32[]{:S(2)}) collective-permute-start(bf16[256,1024]{1,0:T(8,128)(2,1)S(1)} %copy-done.8), channel_id=1, source_target_pairs={{0,16},{16,0},{1,17},{17,1},{2,18},{18,2},{3,19},{19,3},{4,20},{20... | collective-permute-start | bytes 1572872 | tf_op jit(solution)/shard_map/tile_sum/ppermute | solution.py:349
  59.8 8.7 %beams.7 = (bf16[256,1024]{1,0:T(8,128)(2,1)}, bf16[256,1024]{1,0:T(8,128)(2,1)}) custom-call(bf16[2,1024,512]{2,1,0:T(8,128)(2,1)} %echoes_hbm.7, f32[1,1024]{1,0:T(1,128)S(1)} %add_add_fusion.power_ref, s32[1,2048]{1,0:T(1,128)S(1)} %bitcast.7, bf16[2,2048,1024]{2,1,0:T(8,128)(2,1)} %steer_hbm.7), custom_call_target="tpu_custom_call" | custom-call | flops 4294967296 | bytes 9437184 | tf_op jit(solution)/shard_map/beams/beams/pallas_call | solution.py:118
  68.5 0.0 copy-start
  68.5 0.1 collective-permute-start.8
  68.7 3.2 %collective-permute-done.9.rest_1_ = bf16[256,1024]{1,0:T(8,128)(2,1)S(1)} collective-permute-done((bf16[256,1024]{1,0:T(8,128)(2,1)S(1)}, bf16[256,1024]{1,0:T(8,128)(2,1)S(1)}, u32[]{:S(2)}, u32[]{:S(2)}) %collective-permute-start.9) | collective-permute-done | bytes 524320 | tf_op jit(solution)/shard_map/tile_sum/ppermute | solution.py:349
  71.8 0.0 copy-done.1
  71.8 0.0 copy-done.5
  71.8 3.4 %compress.6 = (bf16[16,256,128]{2,1,0:T(8,128)(2,1)}, bf16[2,112,1024]{2,1,0:T(8,128)(2,1)}) custom-call(f32[2,8]{1,0:T(2,128)S(1)} %convert_element_type.6.code_ref, s32[1]{0:T(128)} %bitcast.at_ref, s32[1,1024]{1,0:T(1,128)S(1)} %and_select_fusion.1.lens_ref, s32[1,1024]{1,0:T(1,128)S(1)} %get-tuple-element.57.limits_ref, bf16[256,1024]{1,0:T(8,128)(2,1)S(1)} %copy-done.1, ...), custom_call_target="tpu_custom_call" | custom-call | flops 8388608 | bytes 1572864 | tf_op jit(solution)/shard_map/compress/compress/pallas_call | solution.py:208
  75.3 7.8 %collective-permute-done.8.rest_1_ = bf16[256,1024]{1,0:T(8,128)(2,1)S(1)} collective-permute-done((bf16[256,1024]{1,0:T(8,128)(2,1)}, bf16[256,1024]{1,0:T(8,128)(2,1)S(1)}, u32[]{:S(2)}, u32[]{:S(2)}) %collective-permute-start.8) | collective-permute-done | bytes 524320 | tf_op jit(solution)/shard_map/tile_sum/ppermute | solution.py:349
  83.1 0.0 copy-start.4
  83.1 1.0 copy-done.4
  84.1 0.0 copy-start.7
  84.1 1.0 copy-done.7
  85.1 3.3 %compress.7 = bf16[16,256,128]{2,1,0:T(8,128)(2,1)} custom-call(f32[2,8]{1,0:T(2,128)S(1)} %convert_element_type.6.code_ref, s32[1]{0:T(128)} %bitcast.at_ref, s32[1,1024]{1,0:T(1,128)S(1)} %and_select_fusion.1.lens_ref, s32[1,1024]{1,0:T(1,128)S(1)} %get-tuple-element.57.limits_ref, ...), custom_call_target="tpu_custom_call", output_to_operand_aliasing={{}: (7, {})} | custom-call | flops 8388608 | bytes 1572864 | tf_op jit(solution)/shard_map/compress/compress/pallas_call | solution.py:208
  88.4 0.0 all-to-all-done.1.got_ref
  88.4 6.5 %all-to-all-start = ((bf16[16,256,128]{2,1,0:T(8,128)(2,1)}), bf16[16,256,128]{2,1,0:T(8,128)(2,1)S(1)}, u32[]{:S(2)}, u32[]{:S(2)}) async-start(bf16[16,256,128]{2,1,0:T(8,128)(2,1)} %compress.7), calls=%async_computation | async-start | bytes 2097152 | tf_op jit(solution)/shard_map/to_owners/all_to_all | solution.py:363
  94.9 0.0 copy-done
  94.9 3.5 %doppler.2.rest_0_ = f32[64,2,32,256]{3,2,1,0:T(8,128)} custom-call(bf16[16,256,128]{2,1,0:T(8,128)(2,1)S(1)} %all-to-all-done.1.got_ref, bf16[256,512]{1,0:T(8,128)(2,1)S(1)} %copy-done), custom_call_target="tpu_custom_call" | custom-call | flops 536870912 | bytes 3145728 | tf_op jit(solution)/shard_map/doppler/doppler/pallas_call | solution.py:247
  98.4 21.3 %all-to-all-done.got_ref = bf16[16,256,128]{2,1,0:T(8,128)(2,1)S(1)} async-done(((bf16[16,256,128]{2,1,0:T(8,128)(2,1)}), bf16[16,256,128]{2,1,0:T(8,128)(2,1)S(1)}, u32[]{:S(2)}, u32[]{:S(2)}) %all-to-all-start) | async-done | bytes 1048608 | tf_op jit(solution)/shard_map/to_owners/all_to_all | solution.py:363
  119.8 3.5 %doppler.3 = f32[64,2,32,256]{3,2,1,0:T(8,128)} custom-call(bf16[16,256,128]{2,1,0:T(8,128)(2,1)S(1)} %all-to-all-done.got_ref, bf16[256,512]{1,0:T(8,128)(2,1)S(1)} %copy-done, f32[64,2,32,256]{3,2,1,0:T(8,128)} %doppler.2.rest_0_), custom_call_target="tpu_custom_call", output_to_operand_aliasing={{}: (2, {})} | custom-call | flops 536870912 | bytes 3145728 | tf_op jit(solution)/shard_map/doppler/doppler/pallas_call | solution.py:247
  (5 shorter events, 0.1 us)
Async XLA Ops:
  2.1 4.9 %collective-permute-start.2 = (f32[1,1024]{1,0:T(1,128)S(1)}, f32[1,1024]{1,0:T(1,128)S(1)}, u32[]{:S(2)}, u32[]{:S(2)}) collective-permute-start(f32[1,1024]{1,0:T(1,128)S(1)} %bitcast.8), channel_id=1, source_target_pairs={{0,3},{1,2},{2,1},{3,0},{4,7},{5,6},{6,5},{7,4},{8,11},{9,10},{10,... | collective-permute-start | bytes 12296 | tf_op jit(solution)/shard_map/ppermute | solution.py:280
  3.9 3.0 %collective-permute-start.1 = (f32[1,1024]{1,0:T(1,128)S(1)}, f32[1,1024]{1,0:T(1,128)S(1)}, u32[]{:S(2)}, u32[]{:S(2)}) collective-permute-start(f32[1,1024]{1,0:T(1,128)S(1)} %bitcast.9), channel_id=1, source_target_pairs={{0,2},{1,3},{2,0},{3,1},{4,6},{5,7},{6,4},{7,5},{8,10},{9,11},{10,... | collective-permute-start | bytes 12296 | tf_op jit(solution)/shard_map/ppermute | solution.py:280
  4.2 2.8 %collective-permute-start = (f32[1,1024]{1,0:T(1,128)S(1)}, f32[1,1024]{1,0:T(1,128)S(1)}, u32[]{:S(2)}, u32[]{:S(2)}) collective-permute-start(f32[1,1024]{1,0:T(1,128)S(1)} %bitcast.10), channel_id=1, source_target_pairs={{0,1},{1,0},{2,3},{3,2},{4,5},{5,4},{6,7},{7,6},{8,9},{9,8},{10,11... | collective-permute-start | bytes 12296 | tf_op jit(solution)/shard_map/ppermute | solution.py:280
  7.0 4.2 %collective-permute-start.5 = (f32[1,1024]{1,0:T(1,128)S(1)}, f32[1,1024]{1,0:T(1,128)S(1)}, u32[]{:S(2)}, u32[]{:S(2)}) collective-permute-start(f32[1,1024]{1,0:T(1,128)S(1)} %add_add_fusion.1), channel_id=1, source_target_pairs={{0,12},{1,13},{2,14},{3,15},{4,8},{5,9},{6,10},{7,11},{8,4},{9,5},... | collective-permute-start | bytes 12296 | tf_op jit(solution)/shard_map/ppermute | solution.py:280
  8.3 3.4 %collective-permute-start.4 = (f32[1,1024]{1,0:T(1,128)S(1)}, f32[1,1024]{1,0:T(1,128)S(1)}, u32[]{:S(2)}, u32[]{:S(2)}) collective-permute-start(f32[1,1024]{1,0:T(1,128)S(1)} %add_add_fusion.1), channel_id=1, source_target_pairs={{0,8},{1,9},{2,10},{3,11},{4,12},{5,13},{6,14},{7,15},{8,0},{9,1},... | collective-permute-start | bytes 12296 | tf_op jit(solution)/shard_map/ppermute | solution.py:280
  9.4 2.5 %collective-permute-start.3 = (f32[1,1024]{1,0:T(1,128)S(1)}, f32[1,1024]{1,0:T(1,128)S(1)}, u32[]{:S(2)}, u32[]{:S(2)}) collective-permute-start(f32[1,1024]{1,0:T(1,128)S(1)} %add_add_fusion.1), channel_id=1, source_target_pairs={{0,4},{1,5},{2,6},{3,7},{4,0},{5,1},{6,2},{7,3},{8,12},{9,13},{10,... | collective-permute-start | bytes 12296 | tf_op jit(solution)/shard_map/ppermute | solution.py:280
  20.6 11.7 %copy-start.2 = (bf16[256,1024]{1,0:T(8,128)(2,1)S(1)}, bf16[256,1024]{1,0:T(8,128)(2,1)}, u32[]{:S(2)}) copy-start(bf16[256,1024]{1,0:T(8,128)(2,1)} %get-tuple-element.36.rest_0_) | copy-start | bytes 1572868
  20.6 11.7 %collective-permute-start.6 = (bf16[256,1024]{1,0:T(8,128)(2,1)}, bf16[256,1024]{1,0:T(8,128)(2,1)S(1)}, u32[]{:S(2)}, u32[]{:S(2)}) collective-permute-start(bf16[256,1024]{1,0:T(8,128)(2,1)} %get-tuple-element.37), channel_id=1, source_target_pairs={{0,16},{16,0},{1,17},{17,1},{2,18},{18,2},{3,19},{19,3},{4,20},{20... | collective-permute-start | bytes 1572872 | tf_op jit(solution)/shard_map/tile_sum/ppermute | solution.py:349
  30.6 13.9 %collective-permute-start.7 = (bf16[256,1024]{1,0:T(8,128)(2,1)}, bf16[256,1024]{1,0:T(8,128)(2,1)S(1)}, u32[]{:S(2)}, u32[]{:S(2)}) collective-permute-start(bf16[256,1024]{1,0:T(8,128)(2,1)} %get-tuple-element.43), channel_id=1, source_target_pairs={{0,16},{16,0},{1,17},{17,1},{2,18},{18,2},{3,19},{19,3},{4,20},{20... | collective-permute-start | bytes 1572872 | tf_op jit(solution)/shard_map/tile_sum/ppermute | solution.py:349
  35.4 9.1 %copy-start.3 = (bf16[256,1024]{1,0:T(8,128)(2,1)S(1)}, bf16[256,1024]{1,0:T(8,128)(2,1)}, u32[]{:S(2)}) copy-start(bf16[256,1024]{1,0:T(8,128)(2,1)} %get-tuple-element.42.rest_0_) | copy-start | bytes 1572868
  35.4 9.1 %copy-start.6 = (bf16[2,112,1024]{2,1,0:T(8,128)(2,1)S(1)}, bf16[2,112,1024]{2,1,0:T(8,128)(2,1)}, u32[]{:S(2)}) copy-start(bf16[2,112,1024]{2,1,0:T(8,128)(2,1)} %get-tuple-element.44.rest_2_) | copy-start | bytes 1376260
  44.2 13.4 %copy-start.8 = (bf16[256,1024]{1,0:T(8,128)(2,1)S(1)}, bf16[256,1024]{1,0:T(8,128)(2,1)}, u32[]{:S(2)}) copy-start(bf16[256,1024]{1,0:T(8,128)(2,1)} %get-tuple-element.52) | copy-start | bytes 1572868
  47.9 40.5 %all-to-all-start.1 = ((bf16[16,256,128]{2,1,0:T(8,128)(2,1)}), bf16[16,256,128]{2,1,0:T(8,128)(2,1)S(1)}, u32[]{:S(2)}, u32[]{:S(2)}) async-start(bf16[16,256,128]{2,1,0:T(8,128)(2,1)} %get-tuple-element.56), calls=%async_computation.1 | async-start | bytes 2097152 | tf_op jit(solution)/shard_map/to_owners/all_to_all | solution.py:363
  57.7 14.2 %copy-start.1 = (bf16[256,1024]{1,0:T(8,128)(2,1)S(1)}, bf16[256,1024]{1,0:T(8,128)(2,1)}, u32[]{:S(2)}) copy-start(bf16[256,1024]{1,0:T(8,128)(2,1)} %get-tuple-element.51.rest_0_) | copy-start | bytes 1572868
  57.7 14.2 %copy-start.5 = (bf16[2,112,1024]{2,1,0:T(8,128)(2,1)S(1)}, bf16[2,112,1024]{2,1,0:T(8,128)(2,1)}, u32[]{:S(2)}) copy-start(bf16[2,112,1024]{2,1,0:T(8,128)(2,1)} %get-tuple-element.53.rest_2_) | copy-start | bytes 1376260
  57.7 14.2 %collective-permute-start.9 = (bf16[256,1024]{1,0:T(8,128)(2,1)S(1)}, bf16[256,1024]{1,0:T(8,128)(2,1)S(1)}, u32[]{:S(2)}, u32[]{:S(2)}) collective-permute-start(bf16[256,1024]{1,0:T(8,128)(2,1)S(1)} %copy-done.8), channel_id=1, source_target_pairs={{0,16},{16,0},{1,17},{17,1},{2,18},{18,2},{3,19},{19,3},{4,20},{20... | collective-permute-start | bytes 1572872 | tf_op jit(solution)/shard_map/tile_sum/ppermute | solution.py:349
  68.5 26.4 %copy-start = (bf16[256,512]{1,0:T(8,128)(2,1)S(1)}, bf16[256,512]{1,0:T(8,128)(2,1)}, u32[]{:S(2)}) copy-start(bf16[256,512]{1,0:T(8,128)(2,1)} %constant.66.clone.table_ref) | copy-start | bytes 786436
  68.5 14.5 %collective-permute-start.8 = (bf16[256,1024]{1,0:T(8,128)(2,1)}, bf16[256,1024]{1,0:T(8,128)(2,1)S(1)}, u32[]{:S(2)}, u32[]{:S(2)}) collective-permute-start(bf16[256,1024]{1,0:T(8,128)(2,1)} %get-tuple-element.50), channel_id=1, source_target_pairs={{0,16},{16,0},{1,17},{17,1},{2,18},{18,2},{3,19},{19,3},{4,20},{20... | collective-permute-start | bytes 1572872 | tf_op jit(solution)/shard_map/tile_sum/ppermute | solution.py:349
  83.1 1.0 copy-start.4
  84.1 1.0 copy-start.7
  88.4 31.4 %all-to-all-start = ((bf16[16,256,128]{2,1,0:T(8,128)(2,1)}), bf16[16,256,128]{2,1,0:T(8,128)(2,1)S(1)}, u32[]{:S(2)}, u32[]{:S(2)}) async-start(bf16[16,256,128]{2,1,0:T(8,128)(2,1)} %compress.7), calls=%async_computation | async-start | bytes 2097152 | tf_op jit(solution)/shard_map/to_owners/all_to_all | solution.py:363

commit v3 on v2

--- a/solution.py
+++ b/solution.py
@@ -119,7 +119,8 @@
         functools.partial(beam_kernel, samples, gates, gate, count),
         in_specs=[apart, whole, whole, apart],
         out_specs=[whole] * tiles,
-        out_shape=[pltpu.HBM((2 * rows, tile_beams), jnp.bfloat16)] * tiles,
+        out_shape=[pltpu.VMEM((2 * rows, tile_beams), jnp.bfloat16)]
+        + [pltpu.HBM((2 * rows, tile_beams), jnp.bfloat16)] * (tiles - 1),
         scratch_shapes=[
             pltpu.VMEM(echoes.shape, jnp.bfloat16),
             pltpu.VMEM(steer.shape, jnp.bfloat16),
@@ -139,53 +140,66 @@
     )(echoes, power, order, steer)
 
 
-def compress_kernel(pulses, taps, parts_in, halo, shared, keep_ahead, own, code_ref, at_ref, lens_ref, limits_ref, *rest):
+def compress_kernel(pulses, taps, parts_in, halo, shared, keep_ahead, place, code_ref, at_ref, lens_ref, limits_ref, *rest):
     part_refs, rest = rest[:parts_in], rest[parts_in:]
     if halo:
         ahead_ref, rest = rest[0], rest[1:]
-    out_ref, rest = rest[shared], rest[shared + 1 :]
+    out_hbm, rest = rest[shared], rest[shared + 1 :]
     if keep_ahead:
         beams_ref, rest = rest[0], rest[1:]
-    (wide_ref,) = rest
-    rows = part_refs[0].shape[0] // 2
+    wide_ref, laid_ref, sem = rest
+    rows, tile_beams = part_refs[0].shape[0] // 2, part_refs[0].shape[1]
     edge = (taps - 1) * pulses
-    lanes = part_refs[0].shape[1]
-    for part in range(2):
-        total = part_refs[0][part * rows : (part + 1) * rows].astype(jnp.float32)
-        for ref in part_refs[1:]:
-            total += ref[part * rows : (part + 1) * rows].astype(jnp.float32)
-        rounded = total.astype(jnp.bfloat16)
-        if keep_ahead:
-            beams_ref[part] = rounded[:edge]
-        wide_ref[part, :rows] = rounded.astype(jnp.float32)
-        if halo:
-            wide_ref[part, rows:] = ahead_ref[part].astype(jnp.float32)
-        else:
-            wide_ref[part, rows:] = jnp.zeros((edge, lanes), jnp.float32)
-    lens, limits = lens_ref[...], limits_ref[...]
-    pulse = at_ref[0] + lax.broadcasted_iota(jnp.int32, (pulses, lanes), 0)
-    keep = pulse < limits
-    factors = [
-        (jnp.where(tap < lens, code_ref[0, tap], 0.0), jnp.where(tap < lens, code_ref[1, tap], 0.0))
-        for tap in range(taps)
-    ]
-    for gate in range(rows // pulses):
-        real = imag = None
-        for tap, (code_re, code_im) in enumerate(factors):
-            start = (gate + tap) * pulses
-            shift_re = wide_ref[0, start : start + pulses]
-            shift_im = wide_ref[1, start : start + pulses]
-            term_re = code_re * shift_re + code_im * shift_im
-            term_im = code_re * shift_im - code_im * shift_re
-            real = term_re if real is None else real + term_re
-            imag = term_im if imag is None else imag + term_im
-        real = jnp.where(keep, real, 0.0)
-        imag = jnp.where(keep, imag, 0.0)
-        for owner in range(lanes // own):
-            block = jnp.concatenate(
-                [real[:, owner * own : (owner + 1) * own], imag[:, owner * own : (owner + 1) * own]], axis=1
-            )
-            out_ref[owner, gate * pulses : (gate + 1) * pulses] = block.astype(jnp.bfloat16)
+    lanes = wide_ref.shape[2]
+    own = laid_ref.shape[2] // 2
+    some = lanes // own
+
+    def copy(block):
+        at = pl.ds(block * some, some)
+        return pltpu.make_async_copy(
+            laid_ref.at[at], out_hbm.at[at, pl.ds(place * rows, rows)], sem.at[block]
+        )
+
+    for block in range(tile_beams // lanes):
+        at = slice(block * lanes, (block + 1) * lanes)
+        for part in range(2):
+            total = part_refs[0][part * rows : (part + 1) * rows, at].astype(jnp.float32)
+            for ref in part_refs[1:]:
+                total += ref[part * rows : (part + 1) * rows, at].astype(jnp.float32)
+            rounded = total.astype(jnp.bfloat16)
+            if keep_ahead:
+                beams_ref[part, :, at] = rounded[:edge]
+            wide_ref[part, :rows] = rounded.astype(jnp.float32)
+            if halo:
+                wide_ref[part, rows:] = ahead_ref[part, :, at].astype(jnp.float32)
+            else:
+                wide_ref[part, rows:] = jnp.zeros((edge, lanes), jnp.float32)
+        lens, limits = lens_ref[:, at], limits_ref[:, at]
+        pulse = at_ref[0] + lax.broadcasted_iota(jnp.int32, (pulses, lanes), 0)
+        keep = pulse < limits
+        factors = [
+            (jnp.where(tap < lens, code_ref[0, tap], 0.0), jnp.where(tap < lens, code_ref[1, tap], 0.0))
+            for tap in range(taps)
+        ]
+        for gate in range(rows // pulses):
+            real = imag = None
+            for tap, (code_re, code_im) in enumerate(factors):
+                start = (gate + tap) * pulses
+                shift_re = wide_ref[0, start : start + pulses]
+                shift_im = wide_ref[1, start : start + pulses]
+                term_re = code_re * shift_re + code_im * shift_im
+                term_im = code_re * shift_im - code_im * shift_re
+                real = term_re if real is None else real + term_re
+                imag = term_im if imag is None else imag + term_im
+            real = jnp.where(keep, real, 0.0)
+            imag = jnp.where(keep, imag, 0.0)
+            for owner in range(some):
+                line = slice(owner * own, (owner + 1) * own)
+                joined = jnp.concatenate([real[:, line], imag[:, line]], axis=1).astype(jnp.bfloat16)
+                laid_ref[block * some + owner, gate * pulses : (gate + 1) * pulses] = joined
+        copy(block).start()
+    for block in range(tile_beams // lanes):
+        copy(block).wait()
 
 
 def compress(parts, ahead, code, at, lens, limits, pulses, owners, keep_ahead, ready, place, places):
@@ -194,33 +208,29 @@
     own = tile_beams // owners
     lanes = block_of(tile_beams, 256)
     edge = (taps - 1) * pulses
-    flat = pl.BlockSpec((2 * rows, lanes), lambda i: (0, i))
-    line = pl.BlockSpec((1, lanes), lambda i: (0, i))
-    edges = pl.BlockSpec((2, edge, lanes), lambda i: (0, 0, i))
+    whole, apart = pl.BlockSpec(memory_space=pltpu.VMEM), pl.BlockSpec(memory_space=pl.ANY)
     scalars = pl.BlockSpec(memory_space=pltpu.SMEM)
-    out_specs = [pl.BlockSpec((lanes // own, rows, 2 * own), lambda i: (i, place, 0))]
     out_shape = [pltpu.HBM((owners, places * rows, 2 * own), jnp.bfloat16)]
     if keep_ahead:
-        out_specs.append(edges)
-        out_shape.append(pltpu.HBM((2, edge, tile_beams), jnp.bfloat16))
-    halo = [] if ahead is None else [ahead]
-    shared = [] if ready is None else [ready]
+        out_shape.append(pltpu.VMEM((2, edge, tile_beams), jnp.bfloat16))
+    near = [pltpu.with_memory_space_constraint(x, pltpu.VMEM) for x in parts + ([] if ahead is None else [ahead])]
+    shared = [] if ready is None else in_hbm(ready)
     done = pl.pallas_call(
-        functools.partial(compress_kernel, pulses, taps, len(parts), len(halo), len(shared), keep_ahead, own),
-        grid=(tile_beams // lanes,),
-        in_specs=[scalars, scalars, line, line] + [flat] * len(parts)
-        + [edges] * len(halo)
-        + [pl.BlockSpec(memory_space=pl.ANY)] * len(shared),
-        out_specs=out_specs,
+        functools.partial(
+            compress_kernel, pulses, taps, len(parts), ahead is not None, len(shared), keep_ahead, place
+        ),
+        in_specs=[scalars, scalars, whole, whole] + [whole] * len(near) + [apart] * len(shared),
+        out_specs=[apart] + [whole] * keep_ahead,
         out_shape=out_shape,
-        scratch_shapes=[pltpu.VMEM((2, rows + edge, lanes), jnp.float32)],
-        input_output_aliases={4 + len(parts) + len(halo): 0} if shared else {},
+        scratch_shapes=[
+            pltpu.VMEM((2, rows + edge, lanes), jnp.float32),
+            pltpu.VMEM((owners, rows, 2 * own), jnp.bfloat16),
+            pltpu.SemaphoreType.DMA((tile_beams // lanes,)),
+        ],
+        input_output_aliases={4 + len(near): 0} if shared else {},
         compiler_params=params(16),
-        cost_estimate=pl.CostEstimate(
-            flops=rows * tile_beams * 8 * taps, bytes_accessed=rows * tile_beams * 12, transcendentals=0
-        ),
         name="compress",
-    )(code, at, lens, limits, *parts, *halo, *shared)
+    )(code, at, lens, limits, *near, *shared)
     return done if keep_ahead else (done[0], None)
 
 
@@ -229,14 +239,26 @@
     owners, rows, lanes = got_ref.shape
     own, bins = lanes // 2, table_ref.shape[1] // 2
     gates = rows // pulses
-    for gate in range(gates):
-        values = got_ref[:, gate * pulses : (gate + 1) * pulses].reshape(owners * pulses, lanes)
+    some = block_of(gates, max(1, 512 // lanes))
+    for first in range(0, gates, some):
+        values = jnp.concatenate(
+            [
+                got_ref[:, gate * pulses : (gate + 1) * pulses].reshape(owners * pulses, lanes)
+                for gate in range(first, first + some)
+            ],
+            axis=1,
+        )
         both = lax.dot_general(values, table_ref[...], TN, preferred_element_type=jnp.float32)
-        real = both[:own, :bins] - both[own:, bins:]
-        imag = both[own:, :bins] + both[:own, bins:]
-        for part, values in enumerate((real, imag)):
-            for at in range(lines_ref.shape[0]):
-                lines_ref[at, pl.ds(part * gates + gate, own, stride=2 * gates), :] = values[:, at * 128 : (at + 1) * 128]
+        for index in range(some):
+            gate, start = first + index, index * lanes
+            upper, lower = both[start : start + own], both[start + own : start + lanes]
+            real = upper[:, :bins] - lower[:, bins:]
+            imag = lower[:, :bins] + upper[:, bins:]
+            for part, line in enumerate((real, imag)):
+                for at in range(lines_ref.shape[0]):
+                    lines_ref[at, pl.ds(part * gates + gate, own, stride=2 * gates), :] = line[
+                        :, at * 128 : (at + 1) * 128
+                    ]
     for at in range(lines_ref.shape[0]):
         out_ref[:, :, :, at * 128 : (at + 1) * 128] = lines_ref[at].reshape(own, 2, gates, 128)
 
@@ -244,22 +266,20 @@
 def doppler(got, table, out, first, pulses):
     owners, rows, lanes = got.shape
     own, bins, gates = lanes // 2, table.shape[1] // 2, rows // pulses
+    some = CHUNK if gates % CHUNK == 0 else gates
     return pl.pallas_call(
         functools.partial(doppler_kernel, pulses),
-        grid=(1,),
+        grid=(gates // some,),
         in_specs=[
-            pl.BlockSpec(got.shape, lambda i: (0, 0, 0)),
+            pl.BlockSpec((owners, some * pulses, lanes), lambda i: (0, i, 0)),
             pl.BlockSpec(table.shape, lambda i: (0, 0)),
         ]
         + ([] if out is None else [pl.BlockSpec(memory_space=pl.ANY)]),
-        out_specs=pl.BlockSpec((own, 2, gates, bins), lambda i: (0, 0, first // gates, 0)),
+        out_specs=pl.BlockSpec((own, 2, some, bins), lambda i: (0, 0, first // some + i, 0)),
         out_shape=jax.ShapeDtypeStruct((own, 2, G, bins), jnp.float32),
-        scratch_shapes=[pltpu.VMEM((bins // 128, own * 2 * gates, 128), jnp.float32)],
+        scratch_shapes=[pltpu.VMEM((bins // 128, own * 2 * some, 128), jnp.float32)],
         input_output_aliases={} if out is None else {2: 0},
         compiler_params=params(24),
-        cost_estimate=pl.CostEstimate(
-            flops=rows * lanes * owners * bins * 4, bytes_accessed=got.size * 2 + own * 8 * gates * bins, transcendentals=0
-        ),
         name="doppler",
     )(got, table, *([] if out is None else [out]))
 
@@ -291,11 +311,10 @@
         ("beams", 0),
         ("beams<beams", 0),
         ("beams", 1),
-        ("beams<compress", (1, 0)),
+        ("beams<beams", 1),
+        ("beams", 2),
+        ("beams<compress", (2, 0)),
         ("compress", 0),
-        ("compress<beams", 0),
-        ("beams", 2),
-        ("beams<compress", (2, 1)),
         ("compress", 1),
         ("compress<beams", 1),
         ("send", 0),

time: 124 us -> 117 us (0.944)
  Pallas kernels: 55.1 us -> 51.2 us
  starting transfers between devices: 26 us -> 23.7 us
  local copies, waits for them, and re-layouts: 2.09 us -> 0.01 us
  waiting for transfers between devices: 34.7 us -> 36.3 us
    pallas_call x4, Pallas kernels: 13.2 us -> 10.8 us  [compress(): pl.pallas_call(functools.partial(compress_kernel, pulses, taps, len(parts...]
    unnamed x18 -> x4, local copies, waits for them, and re-layouts: 2.09 us -> 0.01 us
    all_to_all x2, starting transfers between devices: 16.3 us -> 14.6 us  [on_device(): lax.all_to_all(ready[number], 'beam', split_axis=0, concat_axis=0)]
    pallas_call x2, Pallas kernels: 7.01 us -> 5.38 us  [doppler(): pl.pallas_call(functools.partial(doppler_kernel, pulses), grid=(gates //...]
  transfers between devices with their start and end apart: 12 -> 12, of which waited for: 7 -> 6; matrix products, arithmetic and copies ran while one was open for 3% -> 3% of each run, Pallas kernels for 32% -> 32%
where the time goes in v3:
time: 117 us
  Pallas kernels  51.2 us (44%)
  waiting for transfers between devices  36.3 us (31%)
  starting transfers between devices  23.7 us (20%)
  other arithmetic  5.28 us (5%)
    pallas_call x4, Pallas kernels, form_beams(): pl.pallas_call(functools.partial(beam_kernel, samples, gates, gate, count...  35 us
    all_to_all x2, waiting for transfers between devices, on_device(): lax.all_to_all(ready[number], 'beam', split_axis=0, concat_axis=0)  22.1 us
    all_to_all x2, starting transfers between devices, on_device(): lax.all_to_all(ready[number], 'beam', split_axis=0, concat_axis=0)  14.6 us
    ppermute x4, waiting for transfers between devices, on_device(): lax.ppermute(part, 'tile', [(i, (i + away) % tiles) for i in range(tiles)])  13.5 us
    pallas_call x4, Pallas kernels, compress(): pl.pallas_call(functools.partial(compress_kernel, pulses, taps, len(parts...  10.8 us
    ppermute x6, starting transfers between devices, sum_over(): lax.ppermute(values, axis, [(i, i ^ away) for i in range(size)])  5.9 us
    pallas_call x2, Pallas kernels, doppler(): pl.pallas_call(functools.partial(doppler_kernel, pulses), grid=(gates //...  5.38 us
    ppermute x4, starting transfers between devices, on_device(): lax.ppermute(part, 'tile', [(i, (i + away) % tiles) for i in range(tiles)])  3.21 us
  transfers between devices with their start and end apart: 12, of which 6 were waited for; matrix products, arithmetic and copies ran while one was open for 3% of the time, Pallas kernels for 32%

profile of v3, /device:TPU:9, one launch (start us, length us, event | category | flops | bytes accessed | tf_op | source)
XLA Modules:
  0.0 116.7 jit_solution(10666029911729613305)
XLA Ops:
  0.0 2.1 %multiply_reduce_fusion = f32[1024]{0:T(1024)S(1)} fusion(bf16[2,1024,512]{2,1,0:T(8,128)(2,1)} %echoes_hbm.7), kind=kLoop, calls=%fused_computation.2 | loop fusion | flops 3144704 | bytes 2101248 | tf_op jit(solution)/shard_map/reduce_sum | solution.py:341
  2.1 1.9 %collective-permute-start.2 = (f32[1,1024]{1,0:T(1,128)S(1)}, f32[1,1024]{1,0:T(1,128)S(1)}, u32[]{:S(2)}, u32[]{:S(2)}) collective-permute-start(f32[1,1024]{1,0:T(1,128)S(1)} %bitcast.8), channel_id=1, source_target_pairs={{0,3},{1,2},{2,1},{3,0},{4,7},{5,6},{6,5},{7,4},{8,11},{9,10},{10,... | collective-permute-start | bytes 12296 | tf_op jit(solution)/shard_map/ppermute | solution.py:300
  3.9 0.2 collective-permute-start.1
  4.2 0.2 collective-permute-start
  4.4 0.7 fusion
  5.1 0.7 multiply_add_fusion
  5.8 1.1 select_reduce_fusion
  6.9 0.0 collective-permute-done.2
  6.9 0.0 collective-permute-done.1
  6.9 0.0 collective-permute-done
  7.0 1.4 %collective-permute-start.5 = (f32[1,1024]{1,0:T(1,128)S(1)}, f32[1,1024]{1,0:T(1,128)S(1)}, u32[]{:S(2)}, u32[]{:S(2)}) collective-permute-start(f32[1,1024]{1,0:T(1,128)S(1)} %add_add_fusion.1), channel_id=1, source_target_pairs={{0,12},{1,13},{2,14},{3,15},{4,8},{5,9},{6,10},{7,11},{8,4},{9,5},... | collective-permute-start | bytes 12296 | tf_op jit(solution)/shard_map/ppermute | solution.py:300
  8.3 1.1 collective-permute-start.4
  9.4 1.1 collective-permute-start.3
  10.6 0.7 convert_element_type.6.code_ref
  11.2 0.0 collective-permute-done.5
  11.2 0.5 collective-permute-done.4
  11.7 0.2 collective-permute-done.3
  11.9 8.7 %beams.4 = (bf16[256,1024]{1,0:T(8,128)(2,1)S(1)}, bf16[256,1024]{1,0:T(8,128)(2,1)}) custom-call(bf16[2,1024,512]{2,1,0:T(8,128)(2,1)} %echoes_hbm.7, f32[1,1024]{1,0:T(1,128)S(1)} %add_add_fusion.power_ref, s32[1,2048]{1,0:T(1,128)S(1)} %bitcast.4, bf16[2,2048,1024]{2,1,0:T(8,128)(2,1)} %steer_hbm.7), custom_call_target="tpu_custom_call" | custom-call | flops 4294967296 | bytes 9437184 | tf_op jit(solution)/shard_map/beams/beams/pallas_call | solution.py:118
  20.6 1.3 %collective-permute-start.7 = (bf16[256,1024]{1,0:T(8,128)(2,1)}, bf16[256,1024]{1,0:T(8,128)(2,1)S(1)}, u32[]{:S(2)}, u32[]{:S(2)}) collective-permute-start(bf16[256,1024]{1,0:T(8,128)(2,1)} %get-tuple-element.39), channel_id=1, source_target_pairs={{0,16},{16,0},{1,17},{17,1},{2,18},{18,2},{3,19},{19,3},{4,20},{20... | collective-permute-start | bytes 1572872 | tf_op jit(solution)/shard_map/tile_sum/ppermute | solution.py:368
  21.9 8.7 %beams.5 = (bf16[256,1024]{1,0:T(8,128)(2,1)S(1)}, bf16[256,1024]{1,0:T(8,128)(2,1)}) custom-call(bf16[2,1024,512]{2,1,0:T(8,128)(2,1)} %echoes_hbm.7, f32[1,1024]{1,0:T(1,128)S(1)} %add_add_fusion.power_ref, s32[1,2048]{1,0:T(1,128)S(1)} %bitcast.5, bf16[2,2048,1024]{2,1,0:T(8,128)(2,1)} %steer_hbm.7), custom_call_target="tpu_custom_call" | custom-call | flops 4294967296 | bytes 9437184 | tf_op jit(solution)/shard_map/beams/beams/pallas_call | solution.py:118
  30.6 0.3 collective-permute-start.6
  30.9 8.9 %beams.6 = (bf16[256,1024]{1,0:T(8,128)(2,1)S(1)}, bf16[256,1024]{1,0:T(8,128)(2,1)}) custom-call(bf16[2,1024,512]{2,1,0:T(8,128)(2,1)} %echoes_hbm.7, f32[1,1024]{1,0:T(1,128)S(1)} %add_add_fusion.power_ref, s32[1,2048]{1,0:T(1,128)S(1)} %bitcast.6, bf16[2,2048,1024]{2,1,0:T(8,128)(2,1)} %steer_hbm.7), custom_call_target="tpu_custom_call" | custom-call | flops 4294967296 | bytes 9437184 | tf_op jit(solution)/shard_map/beams/beams/pallas_call | solution.py:118
  39.8 0.0 copy-start.1
  39.8 0.0 collective-permute-done.7.rest_1_
  39.9 2.4 %compress.4 = (bf16[16,256,128]{2,1,0:T(8,128)(2,1)}, bf16[2,112,1024]{2,1,0:T(8,128)(2,1)S(1)}) custom-call(f32[2,8]{1,0:T(2,128)S(1)} %convert_element_type.6.code_ref, s32[1]{0:T(128)} %bitcast.at_ref, s32[1,1024]{1,0:T(1,128)S(1)} %and_select_fusion.1.lens_ref, s32[1,1024]{1,0:T(1,128)S(1)} %get-tuple-element.53.limits_ref, ...), custom_call_target="tpu_custom_call" | custom-call | tf_op jit(solution)/shard_map/compress/compress/pallas_call | solution.py:218
  42.3 2.2 %collective-permute-done.6.rest_1_ = bf16[256,1024]{1,0:T(8,128)(2,1)S(1)} collective-permute-done((bf16[256,1024]{1,0:T(8,128)(2,1)}, bf16[256,1024]{1,0:T(8,128)(2,1)S(1)}, u32[]{:S(2)}, u32[]{:S(2)}) %collective-permute-start.6) | collective-permute-done | bytes 524320 | tf_op jit(solution)/shard_map/tile_sum/ppermute | solution.py:368
  44.5 2.8 %compress.5 = (bf16[16,256,128]{2,1,0:T(8,128)(2,1)}, bf16[2,112,1024]{2,1,0:T(8,128)(2,1)S(1)}) custom-call(f32[2,8]{1,0:T(2,128)S(1)} %convert_element_type.6.code_ref, s32[1]{0:T(128)} %bitcast.at_ref, s32[1,1024]{1,0:T(1,128)S(1)} %and_select_fusion.1.lens_ref, s32[1,1024]{1,0:T(1,128)S(1)} %get-tuple-element.53.limits_ref, ...), custom_call_target="tpu_custom_call", output_to_operand_aliasing={{0}: (7, {})} | custom-call | tf_op jit(solution)/shard_map/compress/compress/pallas_call | solution.py:218
  47.3 7.7 %all-to-all-start.1 = ((bf16[16,256,128]{2,1,0:T(8,128)(2,1)}), bf16[16,256,128]{2,1,0:T(8,128)(2,1)S(1)}, u32[]{:S(2)}, u32[]{:S(2)}) async-start(bf16[16,256,128]{2,1,0:T(8,128)(2,1)} %get-tuple-element.52), calls=%async_computation.1 | async-start | bytes 2097152 | tf_op jit(solution)/shard_map/to_owners/all_to_all | solution.py:382
  55.0 0.0 copy-done.1
  55.1 1.3 %collective-permute-start.9 = (bf16[256,1024]{1,0:T(8,128)(2,1)S(1)}, bf16[256,1024]{1,0:T(8,128)(2,1)S(1)}, u32[]{:S(2)}, u32[]{:S(2)}) collective-permute-start(bf16[256,1024]{1,0:T(8,128)(2,1)S(1)} %copy-done.1), channel_id=1, source_target_pairs={{0,16},{16,0},{1,17},{17,1},{2,18},{18,2},{3,19},{19,3},{4,20},{20... | collective-permute-start | bytes 1572872 | tf_op jit(solution)/shard_map/tile_sum/ppermute | solution.py:368
  56.4 8.7 %beams.7 = (bf16[256,1024]{1,0:T(8,128)(2,1)S(1)}, bf16[256,1024]{1,0:T(8,128)(2,1)}) custom-call(bf16[2,1024,512]{2,1,0:T(8,128)(2,1)} %echoes_hbm.7, f32[1,1024]{1,0:T(1,128)S(1)} %add_add_fusion.power_ref, s32[1,2048]{1,0:T(1,128)S(1)} %bitcast.7, bf16[2,2048,1024]{2,1,0:T(8,128)(2,1)} %steer_hbm.7), custom_call_target="tpu_custom_call" | custom-call | flops 4294967296 | bytes 9437184 | tf_op jit(solution)/shard_map/beams/beams/pallas_call | solution.py:118
  65.1 0.0 copy-start
  65.1 0.3 collective-permute-start.8
  65.4 2.9 %collective-permute-done.9.rest_1_ = bf16[256,1024]{1,0:T(8,128)(2,1)S(1)} collective-permute-done((bf16[256,1024]{1,0:T(8,128)(2,1)S(1)}, bf16[256,1024]{1,0:T(8,128)(2,1)S(1)}, u32[]{:S(2)}, u32[]{:S(2)}) %collective-permute-start.9) | collective-permute-done | bytes 524320 | tf_op jit(solution)/shard_map/tile_sum/ppermute | solution.py:368
  68.3 2.8 %compress.6 = (bf16[16,256,128]{2,1,0:T(8,128)(2,1)}, bf16[2,112,1024]{2,1,0:T(8,128)(2,1)S(1)}) custom-call(f32[2,8]{1,0:T(2,128)S(1)} %convert_element_type.6.code_ref, s32[1]{0:T(128)} %bitcast.at_ref, s32[1,1024]{1,0:T(1,128)S(1)} %and_select_fusion.1.lens_ref, s32[1,1024]{1,0:T(1,128)S(1)} %get-tuple-element.53.limits_ref, ...), custom_call_target="tpu_custom_call" | custom-call | tf_op jit(solution)/shard_map/compress/compress/pallas_call | solution.py:218
  71.1 8.4 %collective-permute-done.8.rest_1_ = bf16[256,1024]{1,0:T(8,128)(2,1)S(1)} collective-permute-done((bf16[256,1024]{1,0:T(8,128)(2,1)}, bf16[256,1024]{1,0:T(8,128)(2,1)S(1)}, u32[]{:S(2)}, u32[]{:S(2)}) %collective-permute-start.8) | collective-permute-done | bytes 524320 | tf_op jit(solution)/shard_map/tile_sum/ppermute | solution.py:368
  79.5 2.8 %compress.7 = bf16[16,256,128]{2,1,0:T(8,128)(2,1)} custom-call(f32[2,8]{1,0:T(2,128)S(1)} %convert_element_type.6.code_ref, s32[1]{0:T(128)} %bitcast.at_ref, s32[1,1024]{1,0:T(1,128)S(1)} %and_select_fusion.1.lens_ref, s32[1,1024]{1,0:T(1,128)S(1)} %get-tuple-element.53.limits_ref, ...), custom_call_target="tpu_custom_call", output_to_operand_aliasing={{}: (7, {})} | custom-call | tf_op jit(solution)/shard_map/compress/compress/pallas_call | solution.py:218
  82.3 0.0 all-to-all-done.1.got_ref
  82.3 6.9 %all-to-all-start = ((bf16[16,256,128]{2,1,0:T(8,128)(2,1)}), bf16[16,256,128]{2,1,0:T(8,128)(2,1)S(1)}, u32[]{:S(2)}, u32[]{:S(2)}) async-start(bf16[16,256,128]{2,1,0:T(8,128)(2,1)} %compress.7), calls=%async_computation | async-start | bytes 2097152 | tf_op jit(solution)/shard_map/to_owners/all_to_all | solution.py:382
  89.2 0.0 copy-done
  89.2 2.7 %doppler.2.rest_0_ = f32[64,2,32,256]{3,2,1,0:T(8,128)} custom-call(bf16[16,256,128]{2,1,0:T(8,128)(2,1)S(1)} %all-to-all-done.1.got_ref, bf16[256,512]{1,0:T(8,128)(2,1)S(1)} %copy-done), custom_call_target="tpu_custom_call" | custom-call | tf_op jit(solution)/shard_map/doppler/doppler/pallas_call | solution.py:270
  91.9 22.1 %all-to-all-done.got_ref = bf16[16,256,128]{2,1,0:T(8,128)(2,1)S(1)} async-done(((bf16[16,256,128]{2,1,0:T(8,128)(2,1)}), bf16[16,256,128]{2,1,0:T(8,128)(2,1)S(1)}, u32[]{:S(2)}, u32[]{:S(2)}) %all-to-all-start) | async-done | bytes 1048608 | tf_op jit(solution)/shard_map/to_owners/all_to_all | solution.py:382
  114.0 2.7 %doppler.3 = f32[64,2,32,256]{3,2,1,0:T(8,128)} custom-call(bf16[16,256,128]{2,1,0:T(8,128)(2,1)S(1)} %all-to-all-done.got_ref, bf16[256,512]{1,0:T(8,128)(2,1)S(1)} %copy-done, f32[64,2,32,256]{3,2,1,0:T(8,128)} %doppler.2.rest_0_), custom_call_target="tpu_custom_call", output_to_operand_aliasing={{}: (2, {})} | custom-call | tf_op jit(solution)/shard_map/doppler/doppler/pallas_call | solution.py:270
  (5 shorter events, 0.1 us)
Async XLA Ops:
  2.1 4.9 %collective-permute-start.2 = (f32[1,1024]{1,0:T(1,128)S(1)}, f32[1,1024]{1,0:T(1,128)S(1)}, u32[]{:S(2)}, u32[]{:S(2)}) collective-permute-start(f32[1,1024]{1,0:T(1,128)S(1)} %bitcast.8), channel_id=1, source_target_pairs={{0,3},{1,2},{2,1},{3,0},{4,7},{5,6},{6,5},{7,4},{8,11},{9,10},{10,... | collective-permute-start | bytes 12296 | tf_op jit(solution)/shard_map/ppermute | solution.py:300
  3.9 3.0 %collective-permute-start.1 = (f32[1,1024]{1,0:T(1,128)S(1)}, f32[1,1024]{1,0:T(1,128)S(1)}, u32[]{:S(2)}, u32[]{:S(2)}) collective-permute-start(f32[1,1024]{1,0:T(1,128)S(1)} %bitcast.9), channel_id=1, source_target_pairs={{0,2},{1,3},{2,0},{3,1},{4,6},{5,7},{6,4},{7,5},{8,10},{9,11},{10,... | collective-permute-start | bytes 12296 | tf_op jit(solution)/shard_map/ppermute | solution.py:300
  4.2 2.8 %collective-permute-start = (f32[1,1024]{1,0:T(1,128)S(1)}, f32[1,1024]{1,0:T(1,128)S(1)}, u32[]{:S(2)}, u32[]{:S(2)}) collective-permute-start(f32[1,1024]{1,0:T(1,128)S(1)} %bitcast.10), channel_id=1, source_target_pairs={{0,1},{1,0},{2,3},{3,2},{4,5},{5,4},{6,7},{7,6},{8,9},{9,8},{10,11... | collective-permute-start | bytes 12296 | tf_op jit(solution)/shard_map/ppermute | solution.py:300
  7.0 4.2 %collective-permute-start.5 = (f32[1,1024]{1,0:T(1,128)S(1)}, f32[1,1024]{1,0:T(1,128)S(1)}, u32[]{:S(2)}, u32[]{:S(2)}) collective-permute-start(f32[1,1024]{1,0:T(1,128)S(1)} %add_add_fusion.1), channel_id=1, source_target_pairs={{0,12},{1,13},{2,14},{3,15},{4,8},{5,9},{6,10},{7,11},{8,4},{9,5},... | collective-permute-start | bytes 12296 | tf_op jit(solution)/shard_map/ppermute | solution.py:300
  8.3 3.4 %collective-permute-start.4 = (f32[1,1024]{1,0:T(1,128)S(1)}, f32[1,1024]{1,0:T(1,128)S(1)}, u32[]{:S(2)}, u32[]{:S(2)}) collective-permute-start(f32[1,1024]{1,0:T(1,128)S(1)} %add_add_fusion.1), channel_id=1, source_target_pairs={{0,8},{1,9},{2,10},{3,11},{4,12},{5,13},{6,14},{7,15},{8,0},{9,1},... | collective-permute-start | bytes 12296 | tf_op jit(solution)/shard_map/ppermute | solution.py:300
  9.4 2.5 %collective-permute-start.3 = (f32[1,1024]{1,0:T(1,128)S(1)}, f32[1,1024]{1,0:T(1,128)S(1)}, u32[]{:S(2)}, u32[]{:S(2)}) collective-permute-start(f32[1,1024]{1,0:T(1,128)S(1)} %add_add_fusion.1), channel_id=1, source_target_pairs={{0,4},{1,5},{2,6},{3,7},{4,0},{5,1},{6,2},{7,3},{8,12},{9,13},{10,... | collective-permute-start | bytes 12296 | tf_op jit(solution)/shard_map/ppermute | solution.py:300
  20.6 19.3 %collective-permute-start.7 = (bf16[256,1024]{1,0:T(8,128)(2,1)}, bf16[256,1024]{1,0:T(8,128)(2,1)S(1)}, u32[]{:S(2)}, u32[]{:S(2)}) collective-permute-start(bf16[256,1024]{1,0:T(8,128)(2,1)} %get-tuple-element.39), channel_id=1, source_target_pairs={{0,16},{16,0},{1,17},{17,1},{2,18},{18,2},{3,19},{19,3},{4,20},{20... | collective-permute-start | bytes 1572872 | tf_op jit(solution)/shard_map/tile_sum/ppermute | solution.py:368
  30.6 13.9 %collective-permute-start.6 = (bf16[256,1024]{1,0:T(8,128)(2,1)}, bf16[256,1024]{1,0:T(8,128)(2,1)S(1)}, u32[]{:S(2)}, u32[]{:S(2)}) collective-permute-start(bf16[256,1024]{1,0:T(8,128)(2,1)} %get-tuple-element.37), channel_id=1, source_target_pairs={{0,16},{16,0},{1,17},{17,1},{2,18},{18,2},{3,19},{19,3},{4,20},{20... | collective-permute-start | bytes 1572872 | tf_op jit(solution)/shard_map/tile_sum/ppermute | solution.py:368
  39.8 15.2 %copy-start.1 = (bf16[256,1024]{1,0:T(8,128)(2,1)S(1)}, bf16[256,1024]{1,0:T(8,128)(2,1)}, u32[]{:S(2)}) copy-start(bf16[256,1024]{1,0:T(8,128)(2,1)} %get-tuple-element.48) | copy-start | bytes 1572868
  47.3 35.0 %all-to-all-start.1 = ((bf16[16,256,128]{2,1,0:T(8,128)(2,1)}), bf16[16,256,128]{2,1,0:T(8,128)(2,1)S(1)}, u32[]{:S(2)}, u32[]{:S(2)}) async-start(bf16[16,256,128]{2,1,0:T(8,128)(2,1)} %get-tuple-element.52), calls=%async_computation.1 | async-start | bytes 2097152 | tf_op jit(solution)/shard_map/to_owners/all_to_all | solution.py:382
  55.1 13.2 %collective-permute-start.9 = (bf16[256,1024]{1,0:T(8,128)(2,1)S(1)}, bf16[256,1024]{1,0:T(8,128)(2,1)S(1)}, u32[]{:S(2)}, u32[]{:S(2)}) collective-permute-start(bf16[256,1024]{1,0:T(8,128)(2,1)S(1)} %copy-done.1), channel_id=1, source_target_pairs={{0,16},{16,0},{1,17},{17,1},{2,18},{18,2},{3,19},{19,3},{4,20},{20... | collective-permute-start | bytes 1572872 | tf_op jit(solution)/shard_map/tile_sum/ppermute | solution.py:368
  65.1 24.1 %copy-start = (bf16[256,512]{1,0:T(8,128)(2,1)S(1)}, bf16[256,512]{1,0:T(8,128)(2,1)}, u32[]{:S(2)}) copy-start(bf16[256,512]{1,0:T(8,128)(2,1)} %constant.66.clone.table_ref) | copy-start | bytes 786436
  65.1 14.4 %collective-permute-start.8 = (bf16[256,1024]{1,0:T(8,128)(2,1)}, bf16[256,1024]{1,0:T(8,128)(2,1)S(1)}, u32[]{:S(2)}, u32[]{:S(2)}) collective-permute-start(bf16[256,1024]{1,0:T(8,128)(2,1)} %get-tuple-element.46), channel_id=1, source_target_pairs={{0,16},{16,0},{1,17},{17,1},{2,18},{18,2},{3,19},{19,3},{4,20},{20... | collective-permute-start | bytes 1572872 | tf_op jit(solution)/shard_map/tile_sum/ppermute | solution.py:368
  82.3 31.7 %all-to-all-start = ((bf16[16,256,128]{2,1,0:T(8,128)(2,1)}), bf16[16,256,128]{2,1,0:T(8,128)(2,1)S(1)}, u32[]{:S(2)}, u32[]{:S(2)}) async-start(bf16[16,256,128]{2,1,0:T(8,128)(2,1)} %compress.7), calls=%async_computation | async-start | bytes 2097152 | tf_op jit(solution)/shard_map/to_owners/all_to_all | solution.py:382

commit v4 on v3

--- a/solution.py
+++ b/solution.py
@@ -13,6 +13,7 @@
 EPS = 1e-05
 CHUNK = 8
 TOGETHER = (2, 2)
+STREAMED = (0, 1, 3)
 NT = (((1,), (1,)), ((), ()))
 TN = (((0,), (0,)), ((), ()))
 MIB = 1024 * 1024
@@ -20,6 +21,10 @@
 
 def params(mib):
     return pltpu.CompilerParams(vmem_limit_bytes=mib * MIB)
+
+
+def busy(micros):
+    return pl.CostEstimate(flops=int(micros * 1.15e9), bytes_accessed=1, transcendentals=0)
 
 
 def block_of(size, most):
@@ -40,60 +45,111 @@
     return [pltpu.with_memory_space_constraint(x, pltpu.HBM) for x in values]
 
 
-def beam_kernel(samples, gates, gate, count, echoes_hbm, power_ref, order_ref, steer_hbm, *rest):
-    out_refs = rest[:-7]
-    echoes_ref, steer_ref, scaled_ref, row_ref, picked_ref, echoes_sem, steer_sem = rest[-7:]
+def lookup_kernel(order_ref, lens_ref, limits_ref, near_ref, len_ref, limit_ref):
+    tiles, mine = lax.axis_size("tile"), lax.axis_index("tile")
+    beam_total, slots = order_ref.shape[1], len_ref.shape[1]
+    for away in range(tiles):
+        start = pl.multiple_of(lax.rem(mine + away, tiles) * slots, slots)
+        near_ref[:, away * slots : (away + 1) * slots] = order_ref[:, pl.ds(start, slots)]
+    wide = block_of(beam_total, 512)
+    found = jnp.zeros((8, slots), jnp.float32)
+    for first in range(0, beam_total, wide):
+        at = slice(first, first + wide)
+        lens, limits = lens_ref[:, at], limits_ref[:, at]
+        row = lax.broadcasted_iota(jnp.int32, (8, wide), 0)
+        values = jnp.where(row == 0, lens, jnp.where(row == 1, limits >> 5, limits & 31))
+        beam = first + lax.broadcasted_iota(jnp.int32, (wide, slots), 0)
+        pick = jnp.where(beam == near_ref[:, :slots], 1.0, 0.0).astype(jnp.bfloat16)
+        found += jnp.dot(
+            values.astype(jnp.float32).astype(jnp.bfloat16), pick, preferred_element_type=jnp.float32
+        )
+    found = found.astype(jnp.int32)
+    len_ref[...] = found[0:1]
+    limit_ref[...] = found[1:2] * 32 + found[2:3]
+
+
+def lookup(order, code_len, dwell, slots):
+    whole = pl.BlockSpec(memory_space=pltpu.VMEM)
+    return pl.pallas_call(
+        lookup_kernel,
+        in_specs=[whole] * 3,
+        out_specs=[whole] * 3,
+        out_shape=[jax.ShapeDtypeStruct((1, size), jnp.int32) for size in (order.shape[0], slots, slots)],
+        compiler_params=params(8),
+        cost_estimate=busy(20),
+        name="lookup",
+    )(order[None, :], code_len[None, :], dwell[None, :])
+
+
+def add_kernel(*refs):
+    total = refs[0][...]
+    for ref in refs[1:-1]:
+        total = total + ref[...]
+    refs[-1][...] = total
+
+
+def add(*values):
+    whole = pl.BlockSpec(memory_space=pltpu.VMEM)
+    return pl.pallas_call(
+        add_kernel,
+        in_specs=[whole] * len(values),
+        out_specs=whole,
+        out_shape=jax.ShapeDtypeStruct(values[0].shape, values[0].dtype),
+        compiler_params=params(1),
+        cost_estimate=busy(1),
+        name="add",
+    )(*values)
+
+
+def beam_kernel(samples, gates, gate, count, streamed, tiles, picks, echoes_ref, power_ref, order_ref, steer_ref, *rest):
+    if streamed:
+        steer_hbm, steer_ref, sem = steer_ref, rest[-2], rest[-1]
+        rest = rest[:-2]
+    out_refs, (scaled_ref, row_ref, picked_ref) = rest[:-3], rest[-3:]
+    if len(picks) < tiles:
+        *out_refs, beams_ref = out_refs
     _, chans, columns = echoes_ref.shape
     beam_total, wide = steer_ref.shape[1], row_ref.shape[0]
+    steps = beam_total // wide
+
+    def copy(part, step):
+        at = pl.ds(step * wide, wide)
+        return pltpu.make_async_copy(steer_hbm.at[part, at], steer_ref.at[part, at], sem.at[part, step])
+
+    if streamed:
+        for step in range(min(2, steps)):
+            for part in range(2):
+                copy(part, step).start()
     pulses = columns // gates
     rows = count * pulses
-
-    def echoes_copy(part):
-        return pltpu.make_async_copy(echoes_hbm.at[part], echoes_ref.at[part], echoes_sem.at[part])
-
-    def steer_copy(part, step):
-        at = pl.ds(step * wide, wide)
-        return pltpu.make_async_copy(
-            steer_hbm.at[part, at], steer_ref.at[part, at], steer_sem.at[part, step]
-        )
-
-    def begin(step):
-        for part in range(2):
-            steer_copy(part, step).start()
-
-    steps = beam_total // wide
-    for part in range(2):
-        echoes_copy(part).start()
-    begin(0)
     row = lax.broadcasted_iota(jnp.int32, (rows, columns), 0)
     col = lax.broadcasted_iota(jnp.int32, (rows, columns), 1)
     source = (row % pulses) * gates + row // pulses + gate
     moved = jnp.where(source == col, 1.0, 0.0).astype(jnp.bfloat16)
     row_ref[...] = lax.broadcasted_iota(jnp.int32, row_ref.shape, 0)
     gain = lax.rsqrt(power_ref[...] / samples + EPS)
-    for part in range(2):
-        echoes_copy(part).wait()
-        if part == 0 and steps > 1:
-            begin(1)
-        turned = lax.dot_general(moved, echoes_ref[part], NT, preferred_element_type=jnp.float32) * gain
-        if part == 0:
-            scaled_ref[:rows, :chans] = turned.astype(jnp.bfloat16)
-            scaled_ref[rows:, chans:] = turned.astype(jnp.bfloat16)
-        else:
-            scaled_ref[:rows, chans:] = (-turned).astype(jnp.bfloat16)
-            scaled_ref[rows:, :chans] = turned.astype(jnp.bfloat16)
-
-    slots = row_ref.shape[1]
+    real = lax.dot_general(moved, echoes_ref[0], NT, preferred_element_type=jnp.float32) * gain
+    imag = lax.dot_general(moved, echoes_ref[1], NT, preferred_element_type=jnp.float32) * gain
+    scaled_ref[:rows, :chans] = real.astype(jnp.bfloat16)
+    scaled_ref[:rows, chans:] = (-imag).astype(jnp.bfloat16)
+    scaled_ref[rows:, :chans] = imag.astype(jnp.bfloat16)
+    scaled_ref[rows:, chans:] = real.astype(jnp.bfloat16)
+
+    slots, tile_beams = row_ref.shape[1], beam_total // tiles
+    starts = [start for tile in picks for start in range(tile * tile_beams, (tile + 1) * tile_beams, slots)]
     for step in range(steps):
         at = slice(step * wide, (step + 1) * wide)
-        for part in range(2):
-            steer_copy(part, step).wait()
-        if step + 2 < steps:
-            begin(step + 2)
+        if streamed:
+            for part in range(2):
+                copy(part, step).wait()
+                if step + 2 < steps:
+                    copy(part, step + 2).start()
         beams = lax.dot_general(scaled_ref[:, :chans], steer_ref[0, at], NT, preferred_element_type=jnp.float32)
         beams += lax.dot_general(scaled_ref[:, chans:], steer_ref[1, at], NT, preferred_element_type=jnp.float32)
         beams = beams.astype(jnp.bfloat16)
-        for start in range(0, beam_total, slots):
+        if len(picks) < tiles:
+            beams_ref[:, at] = beams
+        for start in starts:
             wanted = order_ref[:, start : start + slots] - step * wide
             pick = jnp.where(row_ref[...] == wanted, 1.0, 0.0).astype(jnp.bfloat16)
             picked = jnp.dot(beams, pick, preferred_element_type=jnp.float32)
@@ -101,41 +157,66 @@
                 picked += picked_ref[:, start : start + slots]
             picked_ref[:, start : start + slots] = picked
 
-    for index, out_ref in enumerate(out_refs):
-        slots = out_ref.shape[1]
-        out_ref[...] = picked_ref[:, index * slots : (index + 1) * slots].astype(jnp.bfloat16)
-
-
-def form_beams(echoes, power, order, steer, gates, gate, count, samples, tiles):
+    for tile, out_ref in zip(picks, out_refs):
+        out_ref[...] = picked_ref[:, tile * tile_beams : (tile + 1) * tile_beams].astype(jnp.bfloat16)
+
+
+def own_kernel(beams_ref, order_ref, out_ref, row_ref):
+    beam_total, slots = beams_ref.shape[1], out_ref.shape[1]
+    wide, some = row_ref.shape
+    row_ref[...] = lax.broadcasted_iota(jnp.int32, row_ref.shape, 0)
+    for start in range(0, slots, some):
+        picked = None
+        for first in range(0, beam_total, wide):
+            wanted = order_ref[:, start : start + some] - first
+            pick = jnp.where(row_ref[...] == wanted, 1.0, 0.0).astype(jnp.bfloat16)
+            term = jnp.dot(beams_ref[:, first : first + wide], pick, preferred_element_type=jnp.float32)
+            picked = term if picked is None else picked + term
+        out_ref[:, start : start + some] = picked.astype(jnp.bfloat16)
+
+
+def pick_own(beams, order, tiles):
+    rows, beam_total = beams.shape
+    slots = beam_total // tiles
+    whole = pl.BlockSpec(memory_space=pltpu.VMEM)
+    return pl.pallas_call(
+        own_kernel,
+        in_specs=[whole] * 2,
+        out_specs=whole,
+        out_shape=pltpu.VMEM((rows, slots), jnp.bfloat16),
+        scratch_shapes=[pltpu.VMEM((block_of(beam_total, 512), block_of(slots, 512)), jnp.int32)],
+        compiler_params=params(16),
+        cost_estimate=busy(2),
+        name="own",
+    )(pltpu.with_memory_space_constraint(beams, pltpu.VMEM), order)
+
+
+def form_beams(echoes, power, order, steer, gates, gate, count, samples, tiles, streamed, picks):
     _, chans, columns = echoes.shape
     beam_total = steer.shape[1]
     tile_beams = beam_total // tiles
     rows = columns // gates * count
     wide = block_of(beam_total, 512)
-    echoes, steer = in_hbm(echoes, steer)
+    echoes = pltpu.with_memory_space_constraint(echoes, pltpu.VMEM)
+    steer = pltpu.with_memory_space_constraint(steer, pltpu.HBM if streamed else pltpu.VMEM)
     whole = pl.BlockSpec(memory_space=pltpu.VMEM)
-    apart = pl.BlockSpec(memory_space=pl.ANY)
+    spaces = [pltpu.HBM if tile else pltpu.VMEM for tile in picks]
+    out_shape = [space((2 * rows, tile_beams), jnp.bfloat16) for space in spaces]
+    if len(picks) < tiles:
+        out_shape.append(pltpu.VMEM((2 * rows, beam_total), jnp.bfloat16))
     return pl.pallas_call(
-        functools.partial(beam_kernel, samples, gates, gate, count),
-        in_specs=[apart, whole, whole, apart],
-        out_specs=[whole] * tiles,
-        out_shape=[pltpu.VMEM((2 * rows, tile_beams), jnp.bfloat16)]
-        + [pltpu.HBM((2 * rows, tile_beams), jnp.bfloat16)] * (tiles - 1),
+        functools.partial(beam_kernel, samples, gates, gate, count, streamed, tiles, picks),
+        in_specs=[whole] * 3 + [pl.BlockSpec(memory_space=pl.ANY) if streamed else whole],
+        out_specs=[whole] * len(out_shape),
+        out_shape=out_shape,
         scratch_shapes=[
-            pltpu.VMEM(echoes.shape, jnp.bfloat16),
-            pltpu.VMEM(steer.shape, jnp.bfloat16),
             pltpu.VMEM((2 * rows, 2 * chans), jnp.bfloat16),
-            pltpu.VMEM((wide, block_of(beam_total, 512)), jnp.int32),
+            pltpu.VMEM((wide, block_of(tile_beams, 512)), jnp.int32),
             pltpu.VMEM((2 * rows, beam_total), jnp.float32),
-            pltpu.SemaphoreType.DMA((2,)),
-            pltpu.SemaphoreType.DMA((2, beam_total // wide)),
-        ],
-        compiler_params=params(40),
-        cost_estimate=pl.CostEstimate(
-            flops=4 * rows * beam_total * (2 * chans + beam_total),
-            bytes_accessed=steer.size * 2 + 4 * rows * beam_total,
-            transcendentals=0,
-        ),
+        ]
+        + ([pltpu.VMEM(steer.shape, steer.dtype), pltpu.SemaphoreType.DMA((2, beam_total // wide))] if streamed else []),
+        compiler_params=params(24),
+        cost_estimate=busy(9),
         name="beams",
     )(echoes, power, order, steer)
 
@@ -145,7 +226,10 @@
     if halo:
         ahead_ref, rest = rest[0], rest[1:]
     out_hbm, rest = rest[shared], rest[shared + 1 :]
-    if keep_ahead:
+    away = keep_ahead and place == 0
+    if away:
+        beams_hbm, beams_ref, beams_sem, rest = rest[0], rest[-2], rest[-1], rest[1:-2]
+    elif keep_ahead:
         beams_ref, rest = rest[0], rest[1:]
     wide_ref, laid_ref, sem = rest
     rows, tile_beams = part_refs[0].shape[0] // 2, part_refs[0].shape[1]
@@ -159,6 +243,10 @@
         return pltpu.make_async_copy(
             laid_ref.at[at], out_hbm.at[at, pl.ds(place * rows, rows)], sem.at[block]
         )
+
+    def beams_copy(block):
+        at = pl.ds(block * lanes, lanes)
+        return pltpu.make_async_copy(beams_ref.at[:, :, at], beams_hbm.at[:, :, at], beams_sem.at[block])
 
     for block in range(tile_beams // lanes):
         at = slice(block * lanes, (block + 1) * lanes)
@@ -174,11 +262,16 @@
                 wide_ref[part, rows:] = ahead_ref[part, :, at].astype(jnp.float32)
             else:
                 wide_ref[part, rows:] = jnp.zeros((edge, lanes), jnp.float32)
+        if away:
+            beams_copy(block).start()
         lens, limits = lens_ref[:, at], limits_ref[:, at]
         pulse = at_ref[0] + lax.broadcasted_iota(jnp.int32, (pulses, lanes), 0)
         keep = pulse < limits
         factors = [
-            (jnp.where(tap < lens, code_ref[0, tap], 0.0), jnp.where(tap < lens, code_ref[1, tap], 0.0))
+            tuple(
+                jnp.where(tap < lens, code_ref[part : part + 1, tap : tap + 1].astype(jnp.float32), 0.0)
+                for part in range(2)
+            )
             for tap in range(taps)
         ]
         for gate in range(rows // pulses):
@@ -200,6 +293,8 @@
         copy(block).start()
     for block in range(tile_beams // lanes):
         copy(block).wait()
+        if away:
+            beams_copy(block).wait()
 
 
 def compress(parts, ahead, code, at, lens, limits, pulses, owners, keep_ahead, ready, place, places):
@@ -212,23 +307,29 @@
     scalars = pl.BlockSpec(memory_space=pltpu.SMEM)
     out_shape = [pltpu.HBM((owners, places * rows, 2 * own), jnp.bfloat16)]
     if keep_ahead:
-        out_shape.append(pltpu.VMEM((2, edge, tile_beams), jnp.bfloat16))
+        out_shape.append((pltpu.VMEM if place else pltpu.HBM)((2, edge, tile_beams), jnp.bfloat16))
     near = [pltpu.with_memory_space_constraint(x, pltpu.VMEM) for x in parts + ([] if ahead is None else [ahead])]
     shared = [] if ready is None else in_hbm(ready)
     done = pl.pallas_call(
         functools.partial(
             compress_kernel, pulses, taps, len(parts), ahead is not None, len(shared), keep_ahead, place
         ),
-        in_specs=[scalars, scalars, whole, whole] + [whole] * len(near) + [apart] * len(shared),
-        out_specs=[apart] + [whole] * keep_ahead,
+        in_specs=[whole, scalars, whole, whole] + [whole] * len(near) + [apart] * len(shared),
+        out_specs=[apart] + [whole if place else apart] * keep_ahead,
         out_shape=out_shape,
         scratch_shapes=[
             pltpu.VMEM((2, rows + edge, lanes), jnp.float32),
             pltpu.VMEM((owners, rows, 2 * own), jnp.bfloat16),
             pltpu.SemaphoreType.DMA((tile_beams // lanes,)),
-        ],
+        ]
+        + (
+            [pltpu.VMEM((2, edge, tile_beams), jnp.bfloat16), pltpu.SemaphoreType.DMA((tile_beams // lanes,))]
+            if keep_ahead and place == 0
+            else []
+        ),
         input_output_aliases={4 + len(near): 0} if shared else {},
         compiler_params=params(16),
+        cost_estimate=busy(3),
         name="compress",
     )(code, at, lens, limits, *near, *shared)
     return done if keep_ahead else (done[0], None)
@@ -280,6 +381,7 @@
         scratch_shapes=[pltpu.VMEM((bins // 128, own * 2 * some, 128), jnp.float32)],
         input_output_aliases={} if out is None else {2: 0},
         compiler_params=params(24),
+        cost_estimate=busy(3),
         name="doppler",
     )(got, table, *([] if out is None else [out]))
 
@@ -296,8 +398,8 @@
     step = 1
     while step < size:
         steps = [step * i for i in (1, 2, 3) if step * i < size] if step * 2 < size else [step]
-        values = values + sum(
-            lax.ppermute(values, axis, [(i, i ^ away) for i in range(size)]) for away in steps
+        values = add(
+            values, *(lax.ppermute(values, axis, [(i, i ^ away) for i in range(size)]) for away in steps)
         )
         step *= len(steps) + 1
     return values
@@ -306,19 +408,25 @@
 def order_of(groups):
     count = sum(len(group) for group in groups)
     if count == 1:
-        return [("beams", 0), ("compress", 0), ("send", 0), ("doppler", 0)]
+        return [("beams", 0), ("exchange", 0), ("own", 0), ("compress", 0), ("send", 0), ("doppler", 0)]
     return [
         ("beams", 0),
+        ("exchange", 0),
         ("beams<beams", 0),
         ("beams", 1),
+        ("exchange", 1),
+        ("beams<compress", (1, 0)),
+        ("own", 0),
         ("beams<beams", 1),
         ("beams", 2),
+        ("exchange", 2),
         ("beams<compress", (2, 0)),
         ("compress", 0),
         ("compress", 1),
         ("compress<beams", 1),
         ("send", 0),
         ("beams", 3),
+        ("exchange", 3),
         ("beams<compress", (3, 2)),
         ("compress", 2),
         ("compress", 3),
@@ -340,14 +448,8 @@
     values = echoes.astype(jnp.float32)
     power = sum_over(jnp.sum(values * values, axis=(0, 2))[None, :], "beam")
 
-    mine = lax.axis_index("tile")
-    order = jnp.roll(beam_order, -mine * tile_beams)
-    here = order[:tile_beams]
-    match = jnp.arange(beam_total, dtype=jnp.int32)[:, None] == here[None, :]
-    both = jnp.sum(jnp.where(match, (dwell * 16 + code_len)[:, None], 0), axis=0)
-    lens, limits = (both % 16)[None, :], (both // 16)[None, :]
+    order, lens, limits = lookup(beam_order, code_len, dwell, tile_beams)
     at = (lax.axis_index("beam") * pulses)[None]
-    taps = code.astype(jnp.float32)
     table = jnp.asarray(phase_table(total).astype(jnp.bfloat16))
 
     groups = groups_of(G)
@@ -359,22 +461,34 @@
         if kind == "beams":
             gate, gates = chunks[number]
             with jax.named_scope("beams"):
+                picks = tuple(range(1 if number == 0 and tiles > 1 else 0, tiles))
                 parts = form_beams(
-                    echoes, power, order[None, :], steer, G, gate, gates, total * G, tiles
+                    echoes, power, order, steer, G, gate, gates, total * G, tiles, number in STREAMED, picks
                 )
-            own_parts[number] = parts[0]
+            if len(picks) < tiles:
+                parts = [parts[-1], *parts[:-1]]
+            own_parts[number], *others[number] = parts
+        elif kind == "own":
+            if tiles > 1:
+                with jax.named_scope("beams"):
+                    own_parts[number] = pick_own(own_parts[number], order, tiles)
+        elif kind == "exchange":
             with jax.named_scope("tile_sum"):
                 others[number] = [
                     lax.ppermute(part, "tile", [(i, (i + away) % tiles) for i in range(tiles)])
-                    for away, part in enumerate(parts[1:], 1)
+                    for away, part in enumerate(others[number], 1)
                 ]
+        elif kind == "arrived<exchange":
+            others[number[0]][0], others[number[1]][0] = lax.optimization_barrier(
+                (others[number[0]][0], others[number[1]][0])
+            )
         elif kind == "compress":
             index = owner_of[number]
             place = number - firsts[index]
             with jax.named_scope("compress"):
                 ready[index], ahead[number] = compress(
                     [own_parts[number]] + others[number],
-                    ahead.get(number - 1), taps, at, lens, limits, pulses, owners, number < len(chunks) - 1,
+                    ahead.get(number - 1), code, at, lens, limits, pulses, owners, number < len(chunks) - 1,
                     ready.get(index), len(groups[index]) - 1 - place, len(groups[index]),
                 )
         elif kind == "send":
@@ -393,6 +507,9 @@
             power, others[number][0] = lax.optimization_barrier((power, others[number][0]))
         elif kind == "arrived<doppler":
             table, others[number][0] = lax.optimization_barrier((table, others[number][0]))
+        elif kind == "compress<exchange":
+            index = owner_of[number[0]]
+            others[number[1]][0], ready[index] = lax.optimization_barrier((others[number[1]][0], ready[index]))
         elif kind == "compress<beams":
             index = owner_of[number]
             power, ready[index] = lax.optimization_barrier((power, ready[index]))

time: 117 us -> 114 us (0.974)
  waiting for transfers between devices: 36.3 us -> 40.6 us
  Pallas kernels: 51.2 us -> 47.6 us
  other arithmetic: 5.28 us -> 2.11 us
    pallas_call x4, Pallas kernels: 35 us -> 31.4 us  [form_beams(): pl.pallas_call(functools.partial(beam_kernel, samples, gates, gate, count...]
    ppermute x4, waiting for transfers between devices: 13.5 us -> 15.8 us  [on_device(): lax.ppermute(part, 'tile', [(i, (i + away) % tiles) for i in range(tiles)])]
    pallas_call x0 -> x4, Pallas kernels: none -> 1.99 us  [the longest x1 1.3 us: pick_own(): pl.pallas_call(own_kernel, in_specs=[whole] * 2, out_specs=whole, out_sha...]
    ppermute x6, waiting for transfers between devices: 0.67 us -> 2.62 us  [sum_over(): lax.ppermute(values, axis, [(i, i ^ away) for i in range(size)])]
    pallas_call x4, Pallas kernels: 10.8 us -> 8.9 us  [compress(): pl.pallas_call(functools.partial(compress_kernel, pulses, taps, len(parts...]
  transfers between devices with their start and end apart: 12 -> 12, of which waited for: 6 -> 8; matrix products, arithmetic and copies ran while one was open for 3% -> 0% of each run, Pallas kernels for 32% -> 31%
where the time goes in v4:
time: 114 us
  Pallas kernels  47.6 us (42%)
  waiting for transfers between devices  40.6 us (36%)
  starting transfers between devices  22.7 us (20%)
  other arithmetic  2.11 us (2%)
    pallas_call x4, Pallas kernels, form_beams(): pl.pallas_call(functools.partial(beam_kernel, samples, gates, gate, count...  31.4 us
    all_to_all x2, waiting for transfers between devices, on_device(): lax.all_to_all(ready[number], 'beam', split_axis=0, concat_axis=0)  22.1 us
    ppermute x4, waiting for transfers between devices, on_device(): lax.ppermute(part, 'tile', [(i, (i + away) % tiles) for i in range(tiles)])  15.8 us
    all_to_all x2, starting transfers between devices, on_device(): lax.all_to_all(ready[number], 'beam', split_axis=0, concat_axis=0)  13.6 us
    pallas_call x4, Pallas kernels, compress(): pl.pallas_call(functools.partial(compress_kernel, pulses, taps, len(parts...  8.9 us
    ppermute x6, starting transfers between devices, sum_over(): lax.ppermute(values, axis, [(i, i ^ away) for i in range(size)])  5.9 us
    pallas_call x2, Pallas kernels, doppler(): pl.pallas_call(functools.partial(doppler_kernel, pulses), grid=(gates //...  5.38 us
    ppermute x4, starting transfers between devices, on_device(): lax.ppermute(part, 'tile', [(i, (i + away) % tiles) for i in range(tiles)])  3.18 us
  transfers between devices with their start and end apart: 12, of which 8 were waited for; matrix products, arithmetic and copies ran while one was open for 0% of the time, Pallas kernels for 31%

profile of v4, /device:TPU:9, one launch (start us, length us, event | category | flops | bytes accessed | tf_op | source)
XLA Modules:
  0.0 114.2 jit_solution(465917209420550323)
XLA Ops:
  0.0 0.0 copy-start.2
  0.0 0.0 copy-start.3
  0.0 0.0 copy-start.1
  0.0 2.1 %multiply_reduce_fusion = f32[1024]{0:T(1024)S(1)} fusion(bf16[2,1024,512]{2,1,0:T(8,128)(2,1)} %echoes_ref.7), kind=kLoop, calls=%fused_computation | loop fusion | flops 3144704 | bytes 2101248 | tf_op jit(solution)/shard_map/reduce_sum | solution.py:449
  2.1 1.9 %collective-permute-start.2 = (f32[1,1024]{1,0:T(1,128)S(1)}, f32[1,1024]{1,0:T(1,128)S(1)}, u32[]{:S(2)}, u32[]{:S(2)}) collective-permute-start(f32[1,1024]{1,0:T(1,128)S(1)} %bitcast.5), channel_id=1, source_target_pairs={{0,3},{1,2},{2,1},{3,0},{4,7},{5,6},{6,5},{7,4},{8,11},{9,10},{10,... | collective-permute-start | bytes 12296 | tf_op jit(solution)/shard_map/ppermute | solution.py:402
  4.0 0.2 collective-permute-start.1
  4.2 0.2 collective-permute-start
  4.5 1.0 collective-permute-done.2.refs_3_
  5.5 0.9 collective-permute-done.1.refs_2_
  6.4 0.0 collective-permute-done.refs_1_
  6.5 1.4 %collective-permute-start.5 = (f32[1,1024]{1,0:T(1,128)S(1)}, f32[1,1024]{1,0:T(1,128)S(1)}, u32[]{:S(2)}, u32[]{:S(2)}) collective-permute-start(f32[1,1024]{1,0:T(1,128)S(1)} %add.2.refs_0_), channel_id=1, source_target_pairs={{0,12},{1,13},{2,14},{3,15},{4,8},{5,9},{6,10},{7,11},{8,4},{9,5},... | collective-permute-start | bytes 12296 | tf_op jit(solution)/shard_map/ppermute | solution.py:402
  7.8 1.1 collective-permute-start.4
  8.9 1.1 collective-permute-start.3
  10.0 0.0 copy-done.2
  10.0 0.0 copy-done.3
  10.0 0.0 copy-done.1
  10.0 0.7 lookup.1
  10.7 0.0 copy-start
  10.7 0.0 collective-permute-done.5.refs_3_
  10.7 0.4 collective-permute-done.4.refs_2_
  11.2 0.2 collective-permute-done.3.refs_1_
  11.4 0.9 copy-done
  12.3 7.1 %beams.4 = (bf16[256,1024]{1,0:T(8,128)(2,1)}, bf16[256,2048]{1,0:T(8,128)(2,1)S(1)}) custom-call(bf16[2,1024,512]{2,1,0:T(8,128)(2,1)S(1)} %copy-done, f32[1,1024]{1,0:T(1,128)S(1)} %add.3.power_ref, s32[1,2048]{1,0:T(1,128)S(1)} %get-tuple-element.36.order_ref, bf16[2,2048,1024]{2,1,0:T(8,128)(2,1)} %steer_ref.7), custom_call_target="tpu_custom_call" | custom-call | flops 10350000128 | bytes 1 | tf_op jit(solution)/shard_map/beams/beams/pallas_call | solution.py:207
  19.4 0.0 slice-start
  19.5 0.0 slice-start.1
  19.5 1.3 %collective-permute-start.7 = (bf16[256,1024]{1,0:T(8,128)(2,1)}, bf16[256,1024]{1,0:T(8,128)(2,1)S(1)}, u32[]{:S(2)}, u32[]{:S(2)}) collective-permute-start(bf16[256,1024]{1,0:T(8,128)(2,1)} %get-tuple-element.49), channel_id=1, source_target_pairs={{0,16},{16,0},{1,17},{17,1},{2,18},{18,2},{3,19},{19,3},{4,20},{20... | collective-permute-start | bytes 1572872 | tf_op jit(solution)/shard_map/tile_sum/ppermute | solution.py:478
  20.7 9.1 %beams.5 = (bf16[256,1024]{1,0:T(8,128)(2,1)S(1)}, bf16[256,1024]{1,0:T(8,128)(2,1)}) custom-call(bf16[2,1024,512]{2,1,0:T(8,128)(2,1)S(1)} %copy-done, f32[1,1024]{1,0:T(1,128)S(1)} %add.3.power_ref, s32[1,2048]{1,0:T(1,128)S(1)} %get-tuple-element.36.order_ref, bf16[2,2048,1024]{2,1,0:T(8,128)(2,1)} %steer_ref.7), custom_call_target="tpu_custom_call" | custom-call | flops 10350000128 | bytes 1 | tf_op jit(solution)/shard_map/beams/beams/pallas_call | solution.py:207
  29.8 0.3 collective-permute-start.6
  30.1 0.0 slice-done
  30.1 0.0 slice-done.1
  30.1 6.6 %beams.6 = (bf16[256,1024]{1,0:T(8,128)(2,1)S(1)}, bf16[256,1024]{1,0:T(8,128)(2,1)}) custom-call(bf16[2,1024,512]{2,1,0:T(8,128)(2,1)S(1)} %copy-done, f32[1,1024]{1,0:T(1,128)S(1)} %add.3.power_ref, s32[1,2048]{1,0:T(1,128)S(1)} %get-tuple-element.36.order_ref, bf16[2,2048,1024]{2,1,0:T(8,128)(2,1)S(1)} %bitcast.10), custom_call_target="tpu_custom_call" | custom-call | flops 10350000128 | bytes 1 | tf_op jit(solution)/shard_map/beams/beams/pallas_call | solution.py:207
  36.7 0.0 copy-start.7
  36.7 0.0 copy-start.4
  36.7 1.3 %own.1.rest_0_ = bf16[256,1024]{1,0:T(8,128)(2,1)S(1)} custom-call(bf16[256,2048]{1,0:T(8,128)(2,1)S(1)} %get-tuple-element.41.beams_ref, s32[1,2048]{1,0:T(1,128)S(1)} %get-tuple-element.36.order_ref), custom_call_target="tpu_custom_call" | custom-call | flops 2300000000 | bytes 1 | tf_op jit(solution)/shard_map/beams/own/pallas_call | solution.py:182
  38.0 0.0 copy-done.7
  38.1 0.0 collective-permute-done.7.rest_1_
  38.1 0.0 copy-done.4
  38.1 1.9 %compress.4 = (bf16[16,256,128]{2,1,0:T(8,128)(2,1)}, bf16[2,112,1024]{2,1,0:T(8,128)(2,1)S(1)}) custom-call(bf16[2,8]{1,0:T(2,128)(2,1)S(1)} %copy-done.4, s32[1]{0:T(128)} %bitcast.at_ref, s32[1,1024]{1,0:T(1,128)S(1)} %get-tuple-element.34.lens_ref, s32[1,1024]{1,0:T(1,128)S(1)} %get-tuple-element.35.limits_ref, bf16[256,1024]{1,0:T(8,128)(2,1)S(1)} %own.1.rest_0_, ...), custom_call_target="tpu_custom_call" | custom-call | flops 3449999872 | bytes 1 | tf_op jit(solution)/shard_map/compress/compress/pallas_call | solution.py:313
  40.0 3.7 %collective-permute-done.6.rest_1_ = bf16[256,1024]{1,0:T(8,128)(2,1)S(1)} collective-permute-done((bf16[256,1024]{1,0:T(8,128)(2,1)}, bf16[256,1024]{1,0:T(8,128)(2,1)S(1)}, u32[]{:S(2)}, u32[]{:S(2)}) %collective-permute-start.6) | collective-permute-done | bytes 524320 | tf_op jit(solution)/shard_map/tile_sum/ppermute | solution.py:478
  43.7 2.4 %compress.5 = (bf16[16,256,128]{2,1,0:T(8,128)(2,1)}, bf16[2,112,1024]{2,1,0:T(8,128)(2,1)}) custom-call(bf16[2,8]{1,0:T(2,128)(2,1)S(1)} %copy-done.4, s32[1]{0:T(128)} %bitcast.at_ref, s32[1,1024]{1,0:T(1,128)S(1)} %get-tuple-element.34.lens_ref, s32[1,1024]{1,0:T(1,128)S(1)} %get-tuple-element.35.limits_ref, ...), custom_call_target="tpu_custom_call", output_to_operand_aliasing={{0}: (7, {})} | custom-call | flops 3449999872 | bytes 1 | tf_op jit(solution)/shard_map/compress/compress/pallas_call | solution.py:313
  46.0 6.7 %all-to-all-start.1 = ((bf16[16,256,128]{2,1,0:T(8,128)(2,1)}), bf16[16,256,128]{2,1,0:T(8,128)(2,1)S(1)}, u32[]{:S(2)}, u32[]{:S(2)}) async-start(bf16[16,256,128]{2,1,0:T(8,128)(2,1)} %get-tuple-element.62), calls=%async_computation.1 | async-start | bytes 2097152 | tf_op jit(solution)/shard_map/to_owners/all_to_all | solution.py:496
  52.8 0.0 copy-start.6
  52.8 0.0 copy-start.8
  52.8 1.3 %collective-permute-start.9 = (bf16[256,1024]{1,0:T(8,128)(2,1)}, bf16[256,1024]{1,0:T(8,128)(2,1)S(1)}, u32[]{:S(2)}, u32[]{:S(2)}) collective-permute-start(bf16[256,1024]{1,0:T(8,128)(2,1)} %get-tuple-element.58), channel_id=1, source_target_pairs={{0,16},{16,0},{1,17},{17,1},{2,18},{18,2},{3,19},{19,3},{4,20},{20... | collective-permute-start | bytes 1572872 | tf_op jit(solution)/shard_map/tile_sum/ppermute | solution.py:478
  54.1 8.5 %beams.7 = (bf16[256,1024]{1,0:T(8,128)(2,1)S(1)}, bf16[256,1024]{1,0:T(8,128)(2,1)}) custom-call(bf16[2,1024,512]{2,1,0:T(8,128)(2,1)S(1)} %copy-done, f32[1,1024]{1,0:T(1,128)S(1)} %add.3.power_ref, s32[1,2048]{1,0:T(1,128)S(1)} %get-tuple-element.36.order_ref, bf16[2,2048,1024]{2,1,0:T(8,128)(2,1)} %steer_ref.7), custom_call_target="tpu_custom_call" | custom-call | flops 10350000128 | bytes 1 | tf_op jit(solution)/shard_map/beams/beams/pallas_call | solution.py:207
  62.6 0.3 collective-permute-start.8
  63.0 3.3 %collective-permute-done.9.rest_1_ = bf16[256,1024]{1,0:T(8,128)(2,1)S(1)} collective-permute-done((bf16[256,1024]{1,0:T(8,128)(2,1)}, bf16[256,1024]{1,0:T(8,128)(2,1)S(1)}, u32[]{:S(2)}, u32[]{:S(2)}) %collective-permute-start.9) | collective-permute-done | bytes 524320 | tf_op jit(solution)/shard_map/tile_sum/ppermute | solution.py:478
  66.2 0.0 copy-done.6
  66.2 0.0 copy-done.8
  66.2 2.3 %compress.6 = (bf16[16,256,128]{2,1,0:T(8,128)(2,1)}, bf16[2,112,1024]{2,1,0:T(8,128)(2,1)S(1)}) custom-call(bf16[2,8]{1,0:T(2,128)(2,1)S(1)} %copy-done.4, s32[1]{0:T(128)} %bitcast.at_ref, s32[1,1024]{1,0:T(1,128)S(1)} %get-tuple-element.34.lens_ref, s32[1,1024]{1,0:T(1,128)S(1)} %get-tuple-element.35.limits_ref, bf16[256,1024]{1,0:T(8,128)(2,1)S(1)} %copy-done.8, ...), custom_call_target="tpu_custom_call" | custom-call | flops 3449999872 | bytes 1 | tf_op jit(solution)/shard_map/compress/compress/pallas_call | solution.py:313
  68.6 8.9 %collective-permute-done.8.rest_1_ = bf16[256,1024]{1,0:T(8,128)(2,1)S(1)} collective-permute-done((bf16[256,1024]{1,0:T(8,128)(2,1)}, bf16[256,1024]{1,0:T(8,128)(2,1)S(1)}, u32[]{:S(2)}, u32[]{:S(2)}) %collective-permute-start.8) | collective-permute-done | bytes 524320 | tf_op jit(solution)/shard_map/tile_sum/ppermute | solution.py:478
  77.5 0.0 copy-start.5
  77.5 2.3 %compress.7 = bf16[16,256,128]{2,1,0:T(8,128)(2,1)} custom-call(bf16[2,8]{1,0:T(2,128)(2,1)S(1)} %copy-done.4, s32[1]{0:T(128)} %bitcast.at_ref, s32[1,1024]{1,0:T(1,128)S(1)} %get-tuple-element.34.lens_ref, s32[1,1024]{1,0:T(1,128)S(1)} %get-tuple-element.35.limits_ref, ...), custom_call_target="tpu_custom_call", output_to_operand_aliasing={{}: (7, {})} | custom-call | flops 3449999872 | bytes 1 | tf_op jit(solution)/shard_map/compress/compress/pallas_call | solution.py:313
  79.8 0.0 all-to-all-done.1.got_ref
  79.8 6.9 %all-to-all-start = ((bf16[16,256,128]{2,1,0:T(8,128)(2,1)}), bf16[16,256,128]{2,1,0:T(8,128)(2,1)S(1)}, u32[]{:S(2)}, u32[]{:S(2)}) async-start(bf16[16,256,128]{2,1,0:T(8,128)(2,1)} %compress.7), calls=%async_computation | async-start | bytes 2097152 | tf_op jit(solution)/shard_map/to_owners/all_to_all | solution.py:496
  86.6 0.0 copy-done.5
  86.6 2.7 %doppler.2.rest_0_ = f32[64,2,32,256]{3,2,1,0:T(8,128)} custom-call(bf16[16,256,128]{2,1,0:T(8,128)(2,1)S(1)} %all-to-all-done.1.got_ref, bf16[256,512]{1,0:T(8,128)(2,1)S(1)} %copy-done.5), custom_call_target="tpu_custom_call" | custom-call | flops 3449999872 | bytes 1 | tf_op jit(solution)/shard_map/doppler/doppler/pallas_call | solution.py:371
  89.3 22.1 %all-to-all-done.got_ref = bf16[16,256,128]{2,1,0:T(8,128)(2,1)S(1)} async-done(((bf16[16,256,128]{2,1,0:T(8,128)(2,1)}), bf16[16,256,128]{2,1,0:T(8,128)(2,1)S(1)}, u32[]{:S(2)}, u32[]{:S(2)}) %all-to-all-start) | async-done | bytes 1048608 | tf_op jit(solution)/shard_map/to_owners/all_to_all | solution.py:496
  111.5 2.7 %doppler.3 = f32[64,2,32,256]{3,2,1,0:T(8,128)} custom-call(bf16[16,256,128]{2,1,0:T(8,128)(2,1)S(1)} %all-to-all-done.got_ref, bf16[256,512]{1,0:T(8,128)(2,1)S(1)} %copy-done.5, f32[64,2,32,256]{3,2,1,0:T(8,128)} %doppler.2.rest_0_), custom_call_target="tpu_custom_call", output_to_operand_aliasing={{}: (2, {})} | custom-call | flops 3449999872 | bytes 1 | tf_op jit(solution)/shard_map/doppler/doppler/pallas_call | solution.py:371
  (3 shorter events, 0.0 us)
Async XLA Ops:
  0.0 10.0 %copy-start.2 = (s32[2048]{0:T(1024)S(1)}, s32[2048]{0:T(1024)}, u32[]{:S(2)}) copy-start(s32[2048]{0:T(1024)} %param.12) | copy-start | bytes 24580
  0.0 10.0 %copy-start.3 = (s32[2048]{0:T(1024)S(1)}, s32[2048]{0:T(1024)}, u32[]{:S(2)}) copy-start(s32[2048]{0:T(1024)} %param.11) | copy-start | bytes 24580
  0.0 10.0 %copy-start.1 = (s32[2048]{0:T(1024)S(1)}, s32[2048]{0:T(1024)}, u32[]{:S(2)}) copy-start(s32[2048]{0:T(1024)} %param.10) | copy-start | bytes 24580
  2.1 3.4 %collective-permute-start.2 = (f32[1,1024]{1,0:T(1,128)S(1)}, f32[1,1024]{1,0:T(1,128)S(1)}, u32[]{:S(2)}, u32[]{:S(2)}) collective-permute-start(f32[1,1024]{1,0:T(1,128)S(1)} %bitcast.5), channel_id=1, source_target_pairs={{0,3},{1,2},{2,1},{3,0},{4,7},{5,6},{6,5},{7,4},{8,11},{9,10},{10,... | collective-permute-start | bytes 12296 | tf_op jit(solution)/shard_map/ppermute | solution.py:402
  4.0 2.5 %collective-permute-start.1 = (f32[1,1024]{1,0:T(1,128)S(1)}, f32[1,1024]{1,0:T(1,128)S(1)}, u32[]{:S(2)}, u32[]{:S(2)}) collective-permute-start(f32[1,1024]{1,0:T(1,128)S(1)} %bitcast.6), channel_id=1, source_target_pairs={{0,2},{1,3},{2,0},{3,1},{4,6},{5,7},{6,4},{7,5},{8,10},{9,11},{10,... | collective-permute-start | bytes 12296 | tf_op jit(solution)/shard_map/ppermute | solution.py:402
  4.2 2.2 %collective-permute-start = (f32[1,1024]{1,0:T(1,128)S(1)}, f32[1,1024]{1,0:T(1,128)S(1)}, u32[]{:S(2)}, u32[]{:S(2)}) collective-permute-start(f32[1,1024]{1,0:T(1,128)S(1)} %bitcast.7), channel_id=1, source_target_pairs={{0,1},{1,0},{2,3},{3,2},{4,5},{5,4},{6,7},{7,6},{8,9},{9,8},{10,11... | collective-permute-start | bytes 12296 | tf_op jit(solution)/shard_map/ppermute | solution.py:402
  6.5 4.3 %collective-permute-start.5 = (f32[1,1024]{1,0:T(1,128)S(1)}, f32[1,1024]{1,0:T(1,128)S(1)}, u32[]{:S(2)}, u32[]{:S(2)}) collective-permute-start(f32[1,1024]{1,0:T(1,128)S(1)} %add.2.refs_0_), channel_id=1, source_target_pairs={{0,12},{1,13},{2,14},{3,15},{4,8},{5,9},{6,10},{7,11},{8,4},{9,5},... | collective-permute-start | bytes 12296 | tf_op jit(solution)/shard_map/ppermute | solution.py:402
  7.8 3.4 %collective-permute-start.4 = (f32[1,1024]{1,0:T(1,128)S(1)}, f32[1,1024]{1,0:T(1,128)S(1)}, u32[]{:S(2)}, u32[]{:S(2)}) collective-permute-start(f32[1,1024]{1,0:T(1,128)S(1)} %add.2.refs_0_), channel_id=1, source_target_pairs={{0,8},{1,9},{2,10},{3,11},{4,12},{5,13},{6,14},{7,15},{8,0},{9,1},... | collective-permute-start | bytes 12296 | tf_op jit(solution)/shard_map/ppermute | solution.py:402
  8.9 2.5 %collective-permute-start.3 = (f32[1,1024]{1,0:T(1,128)S(1)}, f32[1,1024]{1,0:T(1,128)S(1)}, u32[]{:S(2)}, u32[]{:S(2)}) collective-permute-start(f32[1,1024]{1,0:T(1,128)S(1)} %add.2.refs_0_), channel_id=1, source_target_pairs={{0,4},{1,5},{2,6},{3,7},{4,0},{5,1},{6,2},{7,3},{8,12},{9,13},{10,... | collective-permute-start | bytes 12296 | tf_op jit(solution)/shard_map/ppermute | solution.py:402
  10.7 1.6 %copy-start = (bf16[2,1024,512]{2,1,0:T(8,128)(2,1)S(1)}, bf16[2,1024,512]{2,1,0:T(8,128)(2,1)}, u32[]{:S(2)}) copy-start(bf16[2,1024,512]{2,1,0:T(8,128)(2,1)} %echoes_ref.7) | copy-start | bytes 6291460
  19.4 10.7 %slice-start = ((s8[8388608]{0:T(1024)(128)(4,1)}), s8[4194304]{0:T(1024)(128)(4,1)S(1)}, s32[]{:S(2)}) async-start(s8[8388608]{0:T(1024)(128)(4,1)} %bitcast.9), calls=%async_computation.2 | async-start | bytes 8388608
  19.5 10.6 %slice-start.1 = ((s8[8388608]{0:T(1024)(128)(4,1)}), s8[4194304]{0:T(1024)(128)(4,1)S(1)}, s32[]{:S(2)}) async-start(s8[8388608]{0:T(1024)(128)(4,1)} %bitcast.9), calls=%async_computation.3 | async-start | bytes 8388608
  19.5 18.6 %collective-permute-start.7 = (bf16[256,1024]{1,0:T(8,128)(2,1)}, bf16[256,1024]{1,0:T(8,128)(2,1)S(1)}, u32[]{:S(2)}, u32[]{:S(2)}) collective-permute-start(bf16[256,1024]{1,0:T(8,128)(2,1)} %get-tuple-element.49), channel_id=1, source_target_pairs={{0,16},{16,0},{1,17},{17,1},{2,18},{18,2},{3,19},{19,3},{4,20},{20... | collective-permute-start | bytes 1572872 | tf_op jit(solution)/shard_map/tile_sum/ppermute | solution.py:478
  29.8 13.8 %collective-permute-start.6 = (bf16[256,1024]{1,0:T(8,128)(2,1)}, bf16[256,1024]{1,0:T(8,128)(2,1)S(1)}, u32[]{:S(2)}, u32[]{:S(2)}) collective-permute-start(bf16[256,1024]{1,0:T(8,128)(2,1)} %get-tuple-element.47), channel_id=1, source_target_pairs={{0,16},{16,0},{1,17},{17,1},{2,18},{18,2},{3,19},{19,3},{4,20},{20... | collective-permute-start | bytes 1572872 | tf_op jit(solution)/shard_map/tile_sum/ppermute | solution.py:478
  36.7 1.3 %copy-start.7 = (bf16[256,1024]{1,0:T(8,128)(2,1)}, bf16[256,1024]{1,0:T(8,128)(2,1)S(1)}, u32[]{:S(2)}) copy-start(bf16[256,1024]{1,0:T(8,128)(2,1)S(1)} %get-tuple-element.57.rest_0_) | copy-start | bytes 1572868
  36.7 1.3 %copy-start.4 = (bf16[2,8]{1,0:T(2,128)(2,1)S(1)}, bf16[2,8]{1,0:T(2,128)(2,1)}, u32[]{:S(2)}) copy-start(bf16[2,8]{1,0:T(2,128)(2,1)} %code_ref.7) | copy-start | bytes 100
  46.0 33.7 %all-to-all-start.1 = ((bf16[16,256,128]{2,1,0:T(8,128)(2,1)}), bf16[16,256,128]{2,1,0:T(8,128)(2,1)S(1)}, u32[]{:S(2)}, u32[]{:S(2)}) async-start(bf16[16,256,128]{2,1,0:T(8,128)(2,1)} %get-tuple-element.62), calls=%async_computation.1 | async-start | bytes 2097152 | tf_op jit(solution)/shard_map/to_owners/all_to_all | solution.py:496
  52.8 13.4 %copy-start.6 = (bf16[2,112,1024]{2,1,0:T(8,128)(2,1)S(1)}, bf16[2,112,1024]{2,1,0:T(8,128)(2,1)}, u32[]{:S(2)}) copy-start(bf16[2,112,1024]{2,1,0:T(8,128)(2,1)} %get-tuple-element.59.rest_2_) | copy-start | bytes 1376260
  52.8 13.4 %copy-start.8 = (bf16[256,1024]{1,0:T(8,128)(2,1)S(1)}, bf16[256,1024]{1,0:T(8,128)(2,1)}, u32[]{:S(2)}) copy-start(bf16[256,1024]{1,0:T(8,128)(2,1)} %copy-done.7) | copy-start | bytes 1572868
  52.8 13.4 %collective-permute-start.9 = (bf16[256,1024]{1,0:T(8,128)(2,1)}, bf16[256,1024]{1,0:T(8,128)(2,1)S(1)}, u32[]{:S(2)}, u32[]{:S(2)}) collective-permute-start(bf16[256,1024]{1,0:T(8,128)(2,1)} %get-tuple-element.58), channel_id=1, source_target_pairs={{0,16},{16,0},{1,17},{17,1},{2,18},{18,2},{3,19},{19,3},{4,20},{20... | collective-permute-start | bytes 1572872 | tf_op jit(solution)/shard_map/tile_sum/ppermute | solution.py:478
  62.6 14.8 %collective-permute-start.8 = (bf16[256,1024]{1,0:T(8,128)(2,1)}, bf16[256,1024]{1,0:T(8,128)(2,1)S(1)}, u32[]{:S(2)}, u32[]{:S(2)}) collective-permute-start(bf16[256,1024]{1,0:T(8,128)(2,1)} %get-tuple-element.56), channel_id=1, source_target_pairs={{0,16},{16,0},{1,17},{17,1},{2,18},{18,2},{3,19},{19,3},{4,20},{20... | collective-permute-start | bytes 1572872 | tf_op jit(solution)/shard_map/tile_sum/ppermute | solution.py:478
  77.5 9.2 %copy-start.5 = (bf16[256,512]{1,0:T(8,128)(2,1)S(1)}, bf16[256,512]{1,0:T(8,128)(2,1)}, u32[]{:S(2)}) copy-start(bf16[256,512]{1,0:T(8,128)(2,1)} %constant.10.clone.table_ref) | copy-start | bytes 786436
  79.8 31.7 %all-to-all-start = ((bf16[16,256,128]{2,1,0:T(8,128)(2,1)}), bf16[16,256,128]{2,1,0:T(8,128)(2,1)S(1)}, u32[]{:S(2)}, u32[]{:S(2)}) async-start(bf16[16,256,128]{2,1,0:T(8,128)(2,1)} %compress.7), calls=%async_computation | async-start | bytes 2097152 | tf_op jit(solution)/shard_map/to_owners/all_to_all | solution.py:496

commit v5 on v4

--- a/solution.py
+++ b/solution.py
@@ -14,6 +14,7 @@
 CHUNK = 8
 TOGETHER = (2, 2)
 STREAMED = (0, 1, 3)
+LATER = (0, 3)
 NT = (((1,), (1,)), ((), ()))
 TN = (((0,), (0,)), ((), ()))
 MIB = 1024 * 1024
@@ -117,9 +118,8 @@
         return pltpu.make_async_copy(steer_hbm.at[part, at], steer_ref.at[part, at], sem.at[part, step])
 
     if streamed:
-        for step in range(min(2, steps)):
-            for part in range(2):
-                copy(part, step).start()
+        for part in range(2):
+            copy(part, 0).start()
     pulses = columns // gates
     rows = count * pulses
     row = lax.broadcasted_iota(jnp.int32, (rows, columns), 0)
@@ -135,6 +135,9 @@
     scaled_ref[rows:, :chans] = imag.astype(jnp.bfloat16)
     scaled_ref[rows:, chans:] = real.astype(jnp.bfloat16)
 
+    if streamed and steps > 1:
+        for part in range(2):
+            copy(part, 1).start()
     slots, tile_beams = row_ref.shape[1], beam_total // tiles
     starts = [start for tile in picks for start in range(tile * tile_beams, (tile + 1) * tile_beams, slots)]
     for step in range(steps):
@@ -191,7 +194,7 @@
     )(pltpu.with_memory_space_constraint(beams, pltpu.VMEM), order)
 
 
-def form_beams(echoes, power, order, steer, gates, gate, count, samples, tiles, streamed, picks):
+def form_beams(echoes, power, order, steer, gates, gate, count, samples, tiles, streamed, picks, micros):
     _, chans, columns = echoes.shape
     beam_total = steer.shape[1]
     tile_beams = beam_total // tiles
@@ -216,7 +219,7 @@
         ]
         + ([pltpu.VMEM(steer.shape, steer.dtype), pltpu.SemaphoreType.DMA((2, beam_total // wide))] if streamed else []),
         compiler_params=params(24),
-        cost_estimate=busy(9),
+        cost_estimate=busy(micros),
         name="beams",
     )(echoes, power, order, steer)
 
@@ -297,7 +300,7 @@
             beams_copy(block).wait()
 
 
-def compress(parts, ahead, code, at, lens, limits, pulses, owners, keep_ahead, ready, place, places):
+def compress(parts, ahead, code, at, lens, limits, pulses, owners, keep_ahead, ready, place, places, micros):
     taps = code.shape[1]
     rows, tile_beams = parts[0].shape[0] // 2, parts[0].shape[1]
     own = tile_beams // owners
@@ -329,61 +332,70 @@
         ),
         input_output_aliases={4 + len(near): 0} if shared else {},
         compiler_params=params(16),
-        cost_estimate=busy(3),
+        cost_estimate=busy(micros),
         name="compress",
     )(code, at, lens, limits, *near, *shared)
     return done if keep_ahead else (done[0], None)
 
 
-def doppler_kernel(pulses, got_ref, table_ref, *rest):
-    out_ref, lines_ref = rest[-2:]
+def doppler_kernel(pulses, first, some, got_ref, table_ref, *rest):
+    out_hbm, lines_ref, block_ref, sem = rest[-4:]
     owners, rows, lanes = got_ref.shape
     own, bins = lanes // 2, table_ref.shape[1] // 2
     gates = rows // pulses
-    some = block_of(gates, max(1, 512 // lanes))
-    for first in range(0, gates, some):
-        values = jnp.concatenate(
-            [
-                got_ref[:, gate * pulses : (gate + 1) * pulses].reshape(owners * pulses, lanes)
-                for gate in range(first, first + some)
-            ],
-            axis=1,
-        )
-        both = lax.dot_general(values, table_ref[...], TN, preferred_element_type=jnp.float32)
-        for index in range(some):
-            gate, start = first + index, index * lanes
-            upper, lower = both[start : start + own], both[start + own : start + lanes]
-            real = upper[:, :bins] - lower[:, bins:]
-            imag = lower[:, :bins] + upper[:, bins:]
-            for part, line in enumerate((real, imag)):
-                for at in range(lines_ref.shape[0]):
-                    lines_ref[at, pl.ds(part * gates + gate, own, stride=2 * gates), :] = line[
-                        :, at * 128 : (at + 1) * 128
-                    ]
-    for at in range(lines_ref.shape[0]):
-        out_ref[:, :, :, at * 128 : (at + 1) * 128] = lines_ref[at].reshape(own, 2, gates, 128)
+    batch = block_of(some, max(1, 512 // lanes))
+
+    def copy(block):
+        at = pl.ds(first + block * some, some)
+        return pltpu.make_async_copy(block_ref.at[block], out_hbm.at[:, :, at], sem.at[block])
+
+    for block in range(gates // some):
+        for start in range(0, some, batch):
+            values = jnp.concatenate(
+                [
+                    got_ref[:, gate * pulses : (gate + 1) * pulses].reshape(owners * pulses, lanes)
+                    for gate in range(block * some + start, block * some + start + batch)
+                ],
+                axis=1,
+            )
+            both = lax.dot_general(values, table_ref[...], TN, preferred_element_type=jnp.float32)
+            for index in range(batch):
+                upper = both[index * lanes : index * lanes + own]
+                lower = both[index * lanes + own : (index + 1) * lanes]
+                real = upper[:, :bins] - lower[:, bins:]
+                imag = lower[:, :bins] + upper[:, bins:]
+                for part, line in enumerate((real, imag)):
+                    for at in range(lines_ref.shape[0]):
+                        to = pl.ds(part * some + start + index, own, stride=2 * some)
+                        lines_ref[at, to, :] = line[:, at * 128 : (at + 1) * 128]
+        for at in range(lines_ref.shape[0]):
+            block_ref[block, :, :, :, at * 128 : (at + 1) * 128] = lines_ref[at].reshape(own, 2, some, 128)
+        copy(block).start()
+    for block in range(gates // some):
+        copy(block).wait()
 
 
 def doppler(got, table, out, first, pulses):
     owners, rows, lanes = got.shape
     own, bins, gates = lanes // 2, table.shape[1] // 2, rows // pulses
     some = CHUNK if gates % CHUNK == 0 else gates
+    whole, apart = pl.BlockSpec(memory_space=pltpu.VMEM), pl.BlockSpec(memory_space=pl.ANY)
+    before = [] if out is None else [out]
     return pl.pallas_call(
-        functools.partial(doppler_kernel, pulses),
-        grid=(gates // some,),
-        in_specs=[
-            pl.BlockSpec((owners, some * pulses, lanes), lambda i: (0, i, 0)),
-            pl.BlockSpec(table.shape, lambda i: (0, 0)),
-        ]
-        + ([] if out is None else [pl.BlockSpec(memory_space=pl.ANY)]),
-        out_specs=pl.BlockSpec((own, 2, some, bins), lambda i: (0, 0, first // some + i, 0)),
+        functools.partial(doppler_kernel, pulses, first, some),
+        in_specs=[whole, whole] + [apart] * len(before),
+        out_specs=apart,
         out_shape=jax.ShapeDtypeStruct((own, 2, G, bins), jnp.float32),
-        scratch_shapes=[pltpu.VMEM((bins // 128, own * 2 * some, 128), jnp.float32)],
-        input_output_aliases={} if out is None else {2: 0},
+        scratch_shapes=[
+            pltpu.VMEM((bins // 128, own * 2 * some, 128), jnp.float32),
+            pltpu.VMEM((gates // some, own, 2, some, bins), jnp.float32),
+            pltpu.SemaphoreType.DMA((gates // some,)),
+        ],
+        input_output_aliases={2: 0} if before else {},
         compiler_params=params(24),
         cost_estimate=busy(3),
         name="doppler",
-    )(got, table, *([] if out is None else [out]))
+    )(pltpu.with_memory_space_constraint(got, pltpu.VMEM), table, *before)
 
 
 def phase_table(total):
@@ -419,9 +431,11 @@
         ("own", 0),
         ("beams<beams", 1),
         ("beams", 2),
-        ("exchange", 2),
         ("beams<compress", (2, 0)),
         ("compress", 0),
+        ("compress<exchange", (0, 2)),
+        ("arrived<exchange", (1, 2)),
+        ("exchange", 2),
         ("compress", 1),
         ("compress<beams", 1),
         ("send", 0),
@@ -429,6 +443,8 @@
         ("exchange", 3),
         ("beams<compress", (3, 2)),
         ("compress", 2),
+        ("compress<own", 3),
+        ("own", 3),
         ("compress", 3),
         ("send", 1),
         ("doppler", 0),
@@ -461,15 +477,16 @@
         if kind == "beams":
             gate, gates = chunks[number]
             with jax.named_scope("beams"):
-                picks = tuple(range(1 if number == 0 and tiles > 1 else 0, tiles))
+                picks = tuple(range(1 if number in LATER and tiles > 1 else 0, tiles))
                 parts = form_beams(
-                    echoes, power, order, steer, G, gate, gates, total * G, tiles, number in STREAMED, picks
+                    echoes, power, order, steer, G, gate, gates, total * G, tiles, number in STREAMED, picks,
+                    9 if number < len(groups[0]) + 1 else 0,
                 )
             if len(picks) < tiles:
                 parts = [parts[-1], *parts[:-1]]
             own_parts[number], *others[number] = parts
         elif kind == "own":
-            if tiles > 1:
+            if tiles > 1 and number in LATER:
                 with jax.named_scope("beams"):
                     own_parts[number] = pick_own(own_parts[number], order, tiles)
         elif kind == "exchange":
@@ -489,7 +506,7 @@
                 ready[index], ahead[number] = compress(
                     [own_parts[number]] + others[number],
                     ahead.get(number - 1), code, at, lens, limits, pulses, owners, number < len(chunks) - 1,
-                    ready.get(index), len(groups[index]) - 1 - place, len(groups[index]),
+                    ready.get(index), len(groups[index]) - 1 - place, len(groups[index]), 100 if index else 3,
                 )
         elif kind == "send":
             with jax.named_scope("to_owners"):
@@ -507,6 +524,8 @@
             power, others[number][0] = lax.optimization_barrier((power, others[number][0]))
         elif kind == "arrived<doppler":
             table, others[number][0] = lax.optimization_barrier((table, others[number][0]))
+        elif kind == "compress<own":
+            own_parts[number], ahead = lax.optimization_barrier((own_parts[number], ahead))
         elif kind == "compress<exchange":
             index = owner_of[number[0]]
             others[number[1]][0], ready[index] = lax.optimization_barrier((others[number[1]][0], ready[index]))

time: 114 us -> 112 us (0.982)
  starting transfers between devices: 22.7 us -> 21 us
  waiting for transfers between devices: 40.6 us -> 39 us
    ppermute x4, waiting for transfers between devices: 15.8 us -> 13.1 us  [on_device(): lax.ppermute(part, 'tile', [(i, (i + away) % tiles) for i in range(tiles)])]
    pallas_call x4, Pallas kernels: 31.4 us -> 30 us  [form_beams(): pl.pallas_call(functools.partial(beam_kernel, samples, gates, gate, count...]
    pallas_call x1 -> x2, Pallas kernels: 1.3 us -> 2.61 us  [pick_own(): pl.pallas_call(own_kernel, in_specs=[whole] * 2, out_specs=whole, out_sha...]
  transfers between devices with their start and end apart: 12 -> 12, of which waited for: 8 -> 8; matrix products, arithmetic and copies ran while one was open for 0% -> 0% of each run, Pallas kernels for 31% -> 35%
where the time goes in v5:
time: 112 us
  Pallas kernels  48.2 us (43%)
  waiting for transfers between devices  39 us (35%)
  starting transfers between devices  21 us (19%)
  other arithmetic  2.11 us (2%)
    pallas_call x4, Pallas kernels, form_beams(): pl.pallas_call(functools.partial(beam_kernel, samples, gates, gate, count...  30 us
    all_to_all x2, waiting for transfers between devices, on_device(): lax.all_to_all(ready[number], 'beam', split_axis=0, concat_axis=0)  23.3 us
    ppermute x4, waiting for transfers between devices, on_device(): lax.ppermute(part, 'tile', [(i, (i + away) % tiles) for i in range(tiles)])  13.1 us
    all_to_all x2, starting transfers between devices, on_device(): lax.all_to_all(ready[number], 'beam', split_axis=0, concat_axis=0)  12.5 us
    pallas_call x4, Pallas kernels, compress(): pl.pallas_call(functools.partial(compress_kernel, pulses, taps, len(parts...  8.84 us
    pallas_call x2, Pallas kernels, doppler(): pl.pallas_call(functools.partial(doppler_kernel, pulses, first, some), in...  6.08 us
    ppermute x6, starting transfers between devices, sum_over(): lax.ppermute(values, axis, [(i, i ^ away) for i in range(size)])  5.9 us
    ppermute x6, waiting for transfers between devices, sum_over(): lax.ppermute(values, axis, [(i, i ^ away) for i in range(size)])  2.62 us
  transfers between devices with their start and end apart: 12, of which 8 were waited for; matrix products, arithmetic and copies ran while one was open for 0% of the time, Pallas kernels for 35%

profile of v5, /device:TPU:9, one launch (start us, length us, event | category | flops | bytes accessed | tf_op | source)
XLA Modules:
  0.0 111.7 jit_solution(17706733336957696069)
XLA Ops:
  0.0 0.0 copy-start.2
  0.0 0.0 copy-start.3
  0.0 0.0 copy-start.1
  0.0 2.1 %multiply_reduce_fusion = f32[1024]{0:T(1024)S(1)} fusion(bf16[2,1024,512]{2,1,0:T(8,128)(2,1)} %echoes_ref.7), kind=kLoop, calls=%fused_computation | loop fusion | flops 3144704 | bytes 2101248 | tf_op jit(solution)/shard_map/reduce_sum | solution.py:465
  2.1 1.9 %collective-permute-start.2 = (f32[1,1024]{1,0:T(1,128)S(1)}, f32[1,1024]{1,0:T(1,128)S(1)}, u32[]{:S(2)}, u32[]{:S(2)}) collective-permute-start(f32[1,1024]{1,0:T(1,128)S(1)} %bitcast.7), channel_id=1, source_target_pairs={{0,3},{1,2},{2,1},{3,0},{4,7},{5,6},{6,5},{7,4},{8,11},{9,10},{10,... | collective-permute-start | bytes 12296 | tf_op jit(solution)/shard_map/ppermute | solution.py:414
  4.0 0.2 collective-permute-start.1
  4.2 0.2 collective-permute-start
  4.5 1.0 collective-permute-done.2.refs_3_
  5.5 0.9 collective-permute-done.1.refs_2_
  6.4 0.0 collective-permute-done.refs_1_
  6.5 1.4 %collective-permute-start.5 = (f32[1,1024]{1,0:T(1,128)S(1)}, f32[1,1024]{1,0:T(1,128)S(1)}, u32[]{:S(2)}, u32[]{:S(2)}) collective-permute-start(f32[1,1024]{1,0:T(1,128)S(1)} %add.2.refs_0_), channel_id=1, source_target_pairs={{0,12},{1,13},{2,14},{3,15},{4,8},{5,9},{6,10},{7,11},{8,4},{9,5},... | collective-permute-start | bytes 12296 | tf_op jit(solution)/shard_map/ppermute | solution.py:414
  7.8 1.1 collective-permute-start.4
  8.9 1.1 collective-permute-start.3
  10.0 0.0 copy-done.2
  10.0 0.0 copy-done.3
  10.0 0.0 copy-done.1
  10.0 0.7 lookup.1
  10.7 0.0 copy-start
  10.7 0.0 collective-permute-done.5.refs_3_
  10.7 0.4 collective-permute-done.4.refs_2_
  11.2 0.2 collective-permute-done.3.refs_1_
  11.4 0.9 copy-done
  12.3 7.1 %beams.4 = (bf16[256,1024]{1,0:T(8,128)(2,1)}, bf16[256,2048]{1,0:T(8,128)(2,1)S(1)}) custom-call(bf16[2,1024,512]{2,1,0:T(8,128)(2,1)S(1)} %copy-done, f32[1,1024]{1,0:T(1,128)S(1)} %add.3.power_ref, s32[1,2048]{1,0:T(1,128)S(1)} %get-tuple-element.42.order_ref, bf16[2,2048,1024]{2,1,0:T(8,128)(2,1)} %steer_ref.7), custom_call_target="tpu_custom_call" | custom-call | flops 10350000128 | bytes 1 | tf_op jit(solution)/shard_map/beams/beams/pallas_call | solution.py:210
  19.4 0.0 slice-start
  19.5 0.0 slice-start.1
  19.5 1.3 %collective-permute-start.7 = (bf16[256,1024]{1,0:T(8,128)(2,1)}, bf16[256,1024]{1,0:T(8,128)(2,1)S(1)}, u32[]{:S(2)}, u32[]{:S(2)}) collective-permute-start(bf16[256,1024]{1,0:T(8,128)(2,1)} %get-tuple-element.56), channel_id=1, source_target_pairs={{0,16},{16,0},{1,17},{17,1},{2,18},{18,2},{3,19},{19,3},{4,20},{20... | collective-permute-start | bytes 1572872 | tf_op jit(solution)/shard_map/tile_sum/ppermute | solution.py:495
  20.7 9.1 %beams.5 = (bf16[256,1024]{1,0:T(8,128)(2,1)S(1)}, bf16[256,1024]{1,0:T(8,128)(2,1)}) custom-call(bf16[2,1024,512]{2,1,0:T(8,128)(2,1)S(1)} %copy-done, f32[1,1024]{1,0:T(1,128)S(1)} %add.3.power_ref, s32[1,2048]{1,0:T(1,128)S(1)} %get-tuple-element.42.order_ref, bf16[2,2048,1024]{2,1,0:T(8,128)(2,1)} %steer_ref.7), custom_call_target="tpu_custom_call" | custom-call | flops 10350000128 | bytes 1 | tf_op jit(solution)/shard_map/beams/beams/pallas_call | solution.py:210
  29.8 0.3 collective-permute-start.6
  30.1 0.0 slice-done
  30.1 0.0 slice-done.1
  30.1 6.6 %beams.6 = (bf16[256,1024]{1,0:T(8,128)(2,1)S(1)}, bf16[256,1024]{1,0:T(8,128)(2,1)}) custom-call(bf16[2,1024,512]{2,1,0:T(8,128)(2,1)S(1)} %copy-done, f32[1,1024]{1,0:T(1,128)S(1)} %add.3.power_ref, s32[1,2048]{1,0:T(1,128)S(1)} %get-tuple-element.42.order_ref, bf16[2,2048,1024]{2,1,0:T(8,128)(2,1)S(1)} %bitcast.6), custom_call_target="tpu_custom_call" | custom-call | flops 10350000128 | bytes 1 | tf_op jit(solution)/shard_map/beams/beams/pallas_call | solution.py:210
  36.8 0.0 copy-start.4
  36.8 1.3 %own.2.rest_0_ = bf16[256,1024]{1,0:T(8,128)(2,1)S(1)} custom-call(bf16[256,2048]{1,0:T(8,128)(2,1)S(1)} %get-tuple-element.47.beams_ref, s32[1,2048]{1,0:T(1,128)S(1)} %get-tuple-element.42.order_ref), custom_call_target="tpu_custom_call" | custom-call | flops 2300000000 | bytes 1 | tf_op jit(solution)/shard_map/beams/own/pallas_call | solution.py:185
  38.1 0.0 collective-permute-done.7.rest_1_
  38.1 0.0 copy-done.4
  38.1 1.9 %compress.4 = (bf16[16,256,128]{2,1,0:T(8,128)(2,1)}, bf16[2,112,1024]{2,1,0:T(8,128)(2,1)S(1)}) custom-call(bf16[2,8]{1,0:T(2,128)(2,1)S(1)} %copy-done.4, s32[1]{0:T(128)} %bitcast.at_ref, s32[1,1024]{1,0:T(1,128)S(1)} %get-tuple-element.40.lens_ref, s32[1,1024]{1,0:T(1,128)S(1)} %get-tuple-element.41.limits_ref, bf16[256,1024]{1,0:T(8,128)(2,1)S(1)} %own.2.rest_0_, ...), custom_call_target="tpu_custom_call" | custom-call | flops 3449999872 | bytes 1 | tf_op jit(solution)/shard_map/compress/compress/pallas_call | solution.py:316
  40.0 3.6 %collective-permute-done.6.rest_1_ = bf16[256,1024]{1,0:T(8,128)(2,1)S(1)} collective-permute-done((bf16[256,1024]{1,0:T(8,128)(2,1)}, bf16[256,1024]{1,0:T(8,128)(2,1)S(1)}, u32[]{:S(2)}, u32[]{:S(2)}) %collective-permute-start.6) | collective-permute-done | bytes 524320 | tf_op jit(solution)/shard_map/tile_sum/ppermute | solution.py:495
  43.6 0.7 collective-permute-start.8
  44.3 2.4 %compress.5 = (bf16[16,256,128]{2,1,0:T(8,128)(2,1)}, bf16[2,112,1024]{2,1,0:T(8,128)(2,1)}) custom-call(bf16[2,8]{1,0:T(2,128)(2,1)S(1)} %copy-done.4, s32[1]{0:T(128)} %bitcast.at_ref, s32[1,1024]{1,0:T(1,128)S(1)} %get-tuple-element.40.lens_ref, s32[1,1024]{1,0:T(1,128)S(1)} %get-tuple-element.41.limits_ref, ...), custom_call_target="tpu_custom_call", output_to_operand_aliasing={{0}: (7, {})} | custom-call | flops 3449999872 | bytes 1 | tf_op jit(solution)/shard_map/compress/compress/pallas_call | solution.py:316
  46.7 7.6 %all-to-all-start.1 = ((bf16[16,256,128]{2,1,0:T(8,128)(2,1)}), bf16[16,256,128]{2,1,0:T(8,128)(2,1)}, u32[]{:S(2)}, u32[]{:S(2)}) async-start(bf16[16,256,128]{2,1,0:T(8,128)(2,1)} %get-tuple-element.74), calls=%async_computation.1 | async-start | bytes 2097152 | tf_op jit(solution)/shard_map/to_owners/all_to_all | solution.py:513
  54.3 0.0 copy-start.6
  54.3 7.2 %beams.7 = (bf16[256,1024]{1,0:T(8,128)(2,1)}, bf16[256,2048]{1,0:T(8,128)(2,1)S(1)}) custom-call(bf16[2,1024,512]{2,1,0:T(8,128)(2,1)S(1)} %copy-done, f32[1,1024]{1,0:T(1,128)S(1)} %add.3.power_ref, s32[1,2048]{1,0:T(1,128)S(1)} %get-tuple-element.42.order_ref, bf16[2,2048,1024]{2,1,0:T(8,128)(2,1)} %steer_ref.7), custom_call_target="tpu_custom_call" | custom-call | bytes 1 | tf_op jit(solution)/shard_map/beams/beams/pallas_call | solution.py:210
  61.5 0.3 collective-permute-start.9
  61.8 0.0 collective-permute-done.8.rest_1_
  61.8 0.0 copy-done.6
  61.8 2.3 %compress.6 = (bf16[16,256,128]{2,1,0:T(8,128)(2,1)}, bf16[2,112,1024]{2,1,0:T(8,128)(2,1)S(1)}) custom-call(bf16[2,8]{1,0:T(2,128)(2,1)S(1)} %copy-done.4, s32[1]{0:T(128)} %bitcast.at_ref, s32[1,1024]{1,0:T(1,128)S(1)} %get-tuple-element.40.lens_ref, s32[1,1024]{1,0:T(1,128)S(1)} %get-tuple-element.41.limits_ref, ...), custom_call_target="tpu_custom_call" | custom-call | flops 115000000512 | bytes 1 | tf_op jit(solution)/shard_map/compress/compress/pallas_call | solution.py:316
  64.1 1.3 %own.3.rest_0_ = bf16[256,1024]{1,0:T(8,128)(2,1)S(1)} custom-call(bf16[256,2048]{1,0:T(8,128)(2,1)S(1)} %get-tuple-element.70.beams_ref, s32[1,2048]{1,0:T(1,128)S(1)} %get-tuple-element.42.order_ref), custom_call_target="tpu_custom_call" | custom-call | flops 2300000000 | bytes 1 | tf_op jit(solution)/shard_map/beams/own/pallas_call | solution.py:185
  65.4 9.5 %collective-permute-done.9.rest_1_ = bf16[256,1024]{1,0:T(8,128)(2,1)S(1)} collective-permute-done((bf16[256,1024]{1,0:T(8,128)(2,1)}, bf16[256,1024]{1,0:T(8,128)(2,1)S(1)}, u32[]{:S(2)}, u32[]{:S(2)}) %collective-permute-start.9) | collective-permute-done | bytes 524320 | tf_op jit(solution)/shard_map/tile_sum/ppermute | solution.py:495
  74.9 0.0 copy-start.5
  74.9 2.3 %compress.7 = bf16[16,256,128]{2,1,0:T(8,128)(2,1)} custom-call(bf16[2,8]{1,0:T(2,128)(2,1)S(1)} %copy-done.4, s32[1]{0:T(128)} %bitcast.at_ref, s32[1,1024]{1,0:T(1,128)S(1)} %get-tuple-element.40.lens_ref, s32[1,1024]{1,0:T(1,128)S(1)} %get-tuple-element.41.limits_ref, bf16[256,1024]{1,0:T(8,128)(2,1)S(1)} %own.3.rest_0_, ...), custom_call_target="tpu_custom_call", output_to_operand_aliasing={{}: (7, {})} | custom-call | flops 115000000512 | bytes 1 | tf_op jit(solution)/shard_map/compress/compress/pallas_call | solution.py:316
  77.2 2.1 %all-to-all-done.1.got_ref = bf16[16,256,128]{2,1,0:T(8,128)(2,1)} async-done(((bf16[16,256,128]{2,1,0:T(8,128)(2,1)}), bf16[16,256,128]{2,1,0:T(8,128)(2,1)}, u32[]{:S(2)}, u32[]{:S(2)}) %all-to-all-start.1) | async-done | bytes 1048608 | tf_op jit(solution)/shard_map/to_owners/all_to_all | solution.py:513
  79.3 4.9 %all-to-all-start = ((bf16[16,256,128]{2,1,0:T(8,128)(2,1)}), bf16[16,256,128]{2,1,0:T(8,128)(2,1)S(1)}, u32[]{:S(2)}, u32[]{:S(2)}) async-start(bf16[16,256,128]{2,1,0:T(8,128)(2,1)} %compress.7), calls=%async_computation | async-start | bytes 2097152 | tf_op jit(solution)/shard_map/to_owners/all_to_all | solution.py:513
  84.3 0.0 copy-done.5
  84.3 3.7 %doppler.2.rest_0_ = f32[64,2,32,256]{3,2,1,0:T(8,128)} custom-call(bf16[16,256,128]{2,1,0:T(8,128)(2,1)} %all-to-all-done.1.got_ref, bf16[256,512]{1,0:T(8,128)(2,1)S(1)} %copy-done.5), custom_call_target="tpu_custom_call" | custom-call | flops 3449999872 | bytes 1 | tf_op jit(solution)/shard_map/doppler/doppler/pallas_call | solution.py:384
  87.9 21.2 %all-to-all-done.got_ref = bf16[16,256,128]{2,1,0:T(8,128)(2,1)S(1)} async-done(((bf16[16,256,128]{2,1,0:T(8,128)(2,1)}), bf16[16,256,128]{2,1,0:T(8,128)(2,1)S(1)}, u32[]{:S(2)}, u32[]{:S(2)}) %all-to-all-start) | async-done | bytes 1048608 | tf_op jit(solution)/shard_map/to_owners/all_to_all | solution.py:513
  109.1 2.4 %doppler.3 = f32[64,2,32,256]{3,2,1,0:T(8,128)} custom-call(bf16[16,256,128]{2,1,0:T(8,128)(2,1)S(1)} %all-to-all-done.got_ref, bf16[256,512]{1,0:T(8,128)(2,1)S(1)} %copy-done.5, f32[64,2,32,256]{3,2,1,0:T(8,128)} %doppler.2.rest_0_), custom_call_target="tpu_custom_call", output_to_operand_aliasing={{}: (2, {})} | custom-call | flops 3449999872 | bytes 1 | tf_op jit(solution)/shard_map/doppler/doppler/pallas_call | solution.py:384
  (3 shorter events, 0.0 us)
Async XLA Ops:
  0.0 10.0 %copy-start.2 = (s32[2048]{0:T(1024)S(1)}, s32[2048]{0:T(1024)}, u32[]{:S(2)}) copy-start(s32[2048]{0:T(1024)} %param.12) | copy-start | bytes 24580
  0.0 10.0 %copy-start.3 = (s32[2048]{0:T(1024)S(1)}, s32[2048]{0:T(1024)}, u32[]{:S(2)}) copy-start(s32[2048]{0:T(1024)} %param.11) | copy-start | bytes 24580
  0.0 10.0 %copy-start.1 = (s32[2048]{0:T(1024)S(1)}, s32[2048]{0:T(1024)}, u32[]{:S(2)}) copy-start(s32[2048]{0:T(1024)} %param.10) | copy-start | bytes 24580
  2.1 3.4 %collective-permute-start.2 = (f32[1,1024]{1,0:T(1,128)S(1)}, f32[1,1024]{1,0:T(1,128)S(1)}, u32[]{:S(2)}, u32[]{:S(2)}) collective-permute-start(f32[1,1024]{1,0:T(1,128)S(1)} %bitcast.7), channel_id=1, source_target_pairs={{0,3},{1,2},{2,1},{3,0},{4,7},{5,6},{6,5},{7,4},{8,11},{9,10},{10,... | collective-permute-start | bytes 12296 | tf_op jit(solution)/shard_map/ppermute | solution.py:414
  4.0 2.5 %collective-permute-start.1 = (f32[1,1024]{1,0:T(1,128)S(1)}, f32[1,1024]{1,0:T(1,128)S(1)}, u32[]{:S(2)}, u32[]{:S(2)}) collective-permute-start(f32[1,1024]{1,0:T(1,128)S(1)} %bitcast.8), channel_id=1, source_target_pairs={{0,2},{1,3},{2,0},{3,1},{4,6},{5,7},{6,4},{7,5},{8,10},{9,11},{10,... | collective-permute-start | bytes 12296 | tf_op jit(solution)/shard_map/ppermute | solution.py:414
  4.2 2.2 %collective-permute-start = (f32[1,1024]{1,0:T(1,128)S(1)}, f32[1,1024]{1,0:T(1,128)S(1)}, u32[]{:S(2)}, u32[]{:S(2)}) collective-permute-start(f32[1,1024]{1,0:T(1,128)S(1)} %bitcast.9), channel_id=1, source_target_pairs={{0,1},{1,0},{2,3},{3,2},{4,5},{5,4},{6,7},{7,6},{8,9},{9,8},{10,11... | collective-permute-start | bytes 12296 | tf_op jit(solution)/shard_map/ppermute | solution.py:414
  6.5 4.3 %collective-permute-start.5 = (f32[1,1024]{1,0:T(1,128)S(1)}, f32[1,1024]{1,0:T(1,128)S(1)}, u32[]{:S(2)}, u32[]{:S(2)}) collective-permute-start(f32[1,1024]{1,0:T(1,128)S(1)} %add.2.refs_0_), channel_id=1, source_target_pairs={{0,12},{1,13},{2,14},{3,15},{4,8},{5,9},{6,10},{7,11},{8,4},{9,5},... | collective-permute-start | bytes 12296 | tf_op jit(solution)/shard_map/ppermute | solution.py:414
  7.8 3.4 %collective-permute-start.4 = (f32[1,1024]{1,0:T(1,128)S(1)}, f32[1,1024]{1,0:T(1,128)S(1)}, u32[]{:S(2)}, u32[]{:S(2)}) collective-permute-start(f32[1,1024]{1,0:T(1,128)S(1)} %add.2.refs_0_), channel_id=1, source_target_pairs={{0,8},{1,9},{2,10},{3,11},{4,12},{5,13},{6,14},{7,15},{8,0},{9,1},... | collective-permute-start | bytes 12296 | tf_op jit(solution)/shard_map/ppermute | solution.py:414
  8.9 2.5 %collective-permute-start.3 = (f32[1,1024]{1,0:T(1,128)S(1)}, f32[1,1024]{1,0:T(1,128)S(1)}, u32[]{:S(2)}, u32[]{:S(2)}) collective-permute-start(f32[1,1024]{1,0:T(1,128)S(1)} %add.2.refs_0_), channel_id=1, source_target_pairs={{0,4},{1,5},{2,6},{3,7},{4,0},{5,1},{6,2},{7,3},{8,12},{9,13},{10,... | collective-permute-start | bytes 12296 | tf_op jit(solution)/shard_map/ppermute | solution.py:414
  10.7 1.6 %copy-start = (bf16[2,1024,512]{2,1,0:T(8,128)(2,1)S(1)}, bf16[2,1024,512]{2,1,0:T(8,128)(2,1)}, u32[]{:S(2)}) copy-start(bf16[2,1024,512]{2,1,0:T(8,128)(2,1)} %echoes_ref.7) | copy-start | bytes 6291460
  19.4 10.7 %slice-start = ((s8[8388608]{0:T(1024)(128)(4,1)}), s8[4194304]{0:T(1024)(128)(4,1)S(1)}, s32[]{:S(2)}) async-start(s8[8388608]{0:T(1024)(128)(4,1)} %bitcast.5), calls=%async_computation.2 | async-start | bytes 8388608
  19.5 10.7 %slice-start.1 = ((s8[8388608]{0:T(1024)(128)(4,1)}), s8[4194304]{0:T(1024)(128)(4,1)S(1)}, s32[]{:S(2)}) async-start(s8[8388608]{0:T(1024)(128)(4,1)} %bitcast.5), calls=%async_computation.3 | async-start | bytes 8388608
  19.5 18.6 %collective-permute-start.7 = (bf16[256,1024]{1,0:T(8,128)(2,1)}, bf16[256,1024]{1,0:T(8,128)(2,1)S(1)}, u32[]{:S(2)}, u32[]{:S(2)}) collective-permute-start(bf16[256,1024]{1,0:T(8,128)(2,1)} %get-tuple-element.56), channel_id=1, source_target_pairs={{0,16},{16,0},{1,17},{17,1},{2,18},{18,2},{3,19},{19,3},{4,20},{20... | collective-permute-start | bytes 1572872 | tf_op jit(solution)/shard_map/tile_sum/ppermute | solution.py:495
  29.8 13.8 %collective-permute-start.6 = (bf16[256,1024]{1,0:T(8,128)(2,1)}, bf16[256,1024]{1,0:T(8,128)(2,1)S(1)}, u32[]{:S(2)}, u32[]{:S(2)}) collective-permute-start(bf16[256,1024]{1,0:T(8,128)(2,1)} %get-tuple-element.53), channel_id=1, source_target_pairs={{0,16},{16,0},{1,17},{17,1},{2,18},{18,2},{3,19},{19,3},{4,20},{20... | collective-permute-start | bytes 1572872 | tf_op jit(solution)/shard_map/tile_sum/ppermute | solution.py:495
  36.8 1.3 %copy-start.4 = (bf16[2,8]{1,0:T(2,128)(2,1)S(1)}, bf16[2,8]{1,0:T(2,128)(2,1)}, u32[]{:S(2)}) copy-start(bf16[2,8]{1,0:T(2,128)(2,1)} %code_ref.7) | copy-start | bytes 100
  43.6 18.2 %collective-permute-start.8 = (bf16[256,1024]{1,0:T(8,128)(2,1)}, bf16[256,1024]{1,0:T(8,128)(2,1)S(1)}, u32[]{:S(2)}, u32[]{:S(2)}) collective-permute-start(bf16[256,1024]{1,0:T(8,128)(2,1)} %get-tuple-element.68), channel_id=1, source_target_pairs={{0,16},{16,0},{1,17},{17,1},{2,18},{18,2},{3,19},{19,3},{4,20},{20... | collective-permute-start | bytes 1572872 | tf_op jit(solution)/shard_map/tile_sum/ppermute | solution.py:495
  46.7 32.6 %all-to-all-start.1 = ((bf16[16,256,128]{2,1,0:T(8,128)(2,1)}), bf16[16,256,128]{2,1,0:T(8,128)(2,1)}, u32[]{:S(2)}, u32[]{:S(2)}) async-start(bf16[16,256,128]{2,1,0:T(8,128)(2,1)} %get-tuple-element.74), calls=%async_computation.1 | async-start | bytes 2097152 | tf_op jit(solution)/shard_map/to_owners/all_to_all | solution.py:513
  54.3 7.5 %copy-start.6 = (bf16[2,112,1024]{2,1,0:T(8,128)(2,1)S(1)}, bf16[2,112,1024]{2,1,0:T(8,128)(2,1)}, u32[]{:S(2)}) copy-start(bf16[2,112,1024]{2,1,0:T(8,128)(2,1)} %get-tuple-element.66.rest_2_) | copy-start | bytes 1376260
  61.5 13.4 %collective-permute-start.9 = (bf16[256,1024]{1,0:T(8,128)(2,1)}, bf16[256,1024]{1,0:T(8,128)(2,1)S(1)}, u32[]{:S(2)}, u32[]{:S(2)}) collective-permute-start(bf16[256,1024]{1,0:T(8,128)(2,1)} %get-tuple-element.71), channel_id=1, source_target_pairs={{0,16},{16,0},{1,17},{17,1},{2,18},{18,2},{3,19},{19,3},{4,20},{20... | collective-permute-start | bytes 1572872 | tf_op jit(solution)/shard_map/tile_sum/ppermute | solution.py:495
  74.9 9.3 %copy-start.5 = (bf16[256,512]{1,0:T(8,128)(2,1)S(1)}, bf16[256,512]{1,0:T(8,128)(2,1)}, u32[]{:S(2)}) copy-start(bf16[256,512]{1,0:T(8,128)(2,1)} %constant.10.clone.table_ref) | copy-start | bytes 786436
  79.3 29.8 %all-to-all-start = ((bf16[16,256,128]{2,1,0:T(8,128)(2,1)}), bf16[16,256,128]{2,1,0:T(8,128)(2,1)S(1)}, u32[]{:S(2)}, u32[]{:S(2)}) async-start(bf16[16,256,128]{2,1,0:T(8,128)(2,1)} %compress.7), calls=%async_computation | async-start | bytes 2097152 | tf_op jit(solution)/shard_map/to_owners/all_to_all | solution.py:513

commit v6 on v5

--- a/solution.py
+++ b/solution.py
@@ -224,10 +224,56 @@
     )(echoes, power, order, steer)
 
 
+def factors_of(code_ref, lens, taps):
+    return [
+        tuple(
+            jnp.where(tap < lens, code_ref[part : part + 1, tap : tap + 1].astype(jnp.float32), 0.0)
+            for part in range(2)
+        )
+        for tap in range(taps)
+    ]
+
+
+def add_tap(real, imag, factor, shift_re, shift_im):
+    code_re, code_im = factor
+    term_re = code_re * shift_re + code_im * shift_im
+    term_im = code_re * shift_im - code_im * shift_re
+    return (term_re, term_im) if real is None else (real + term_re, imag + term_im)
+
+
+def edge_kernel(pulses, taps, lanes, code_ref, lens_ref, ahead_ref, sums_ref):
+    for first in range(0, lens_ref.shape[1], lanes):
+        at = slice(first, first + lanes)
+        factors = factors_of(code_ref, lens_ref[:, at], taps)
+        after = [
+            [ahead_ref[part, i * pulses : (i + 1) * pulses, at].astype(jnp.float32) for part in range(2)]
+            for i in range(taps - 1)
+        ]
+        for gate in range(taps - 1):
+            real = imag = None
+            for i in range(gate + 1):
+                real, imag = add_tap(real, imag, factors[taps - 1 - gate + i], *after[i])
+            sums_ref[0, gate * pulses : (gate + 1) * pulses, at] = real
+            sums_ref[1, gate * pulses : (gate + 1) * pulses, at] = imag
+
+
+def edge_sums(ahead, code, lens, pulses):
+    whole = pl.BlockSpec(memory_space=pltpu.VMEM)
+    return pl.pallas_call(
+        functools.partial(edge_kernel, pulses, code.shape[1], block_of(lens.shape[1], 256)),
+        in_specs=[whole] * 3,
+        out_specs=whole,
+        out_shape=pltpu.VMEM(ahead.shape, jnp.float32),
+        compiler_params=params(16),
+        cost_estimate=busy(1),
+        name="edge",
+    )(code, lens, pltpu.with_memory_space_constraint(ahead, pltpu.VMEM))
+
+
 def compress_kernel(pulses, taps, parts_in, halo, shared, keep_ahead, place, code_ref, at_ref, lens_ref, limits_ref, *rest):
     part_refs, rest = rest[:parts_in], rest[parts_in:]
     if halo:
-        ahead_ref, rest = rest[0], rest[1:]
+        sums_ref, rest = rest[0], rest[1:]
     out_hbm, rest = rest[shared], rest[shared + 1 :]
     away = keep_ahead and place == 0
     if away:
@@ -260,33 +306,25 @@
             rounded = total.astype(jnp.bfloat16)
             if keep_ahead:
                 beams_ref[part, :, at] = rounded[:edge]
-            wide_ref[part, :rows] = rounded.astype(jnp.float32)
-            if halo:
-                wide_ref[part, rows:] = ahead_ref[part, :, at].astype(jnp.float32)
-            else:
-                wide_ref[part, rows:] = jnp.zeros((edge, lanes), jnp.float32)
+            wide_ref[part] = rounded.astype(jnp.float32)
         if away:
             beams_copy(block).start()
         lens, limits = lens_ref[:, at], limits_ref[:, at]
         pulse = at_ref[0] + lax.broadcasted_iota(jnp.int32, (pulses, lanes), 0)
         keep = pulse < limits
-        factors = [
-            tuple(
-                jnp.where(tap < lens, code_ref[part : part + 1, tap : tap + 1].astype(jnp.float32), 0.0)
-                for part in range(2)
-            )
-            for tap in range(taps)
-        ]
-        for gate in range(rows // pulses):
+        factors = factors_of(code_ref, lens, taps)
+        gates = rows // pulses
+        for gate in range(gates):
             real = imag = None
-            for tap, (code_re, code_im) in enumerate(factors):
+            before = gate - (gates - taps + 1)
+            if halo and before >= 0:
+                real = sums_ref[0, before * pulses : (before + 1) * pulses, at]
+                imag = sums_ref[1, before * pulses : (before + 1) * pulses, at]
+            for tap in range(min(taps, gates - gate)):
                 start = (gate + tap) * pulses
-                shift_re = wide_ref[0, start : start + pulses]
-                shift_im = wide_ref[1, start : start + pulses]
-                term_re = code_re * shift_re + code_im * shift_im
-                term_im = code_re * shift_im - code_im * shift_re
-                real = term_re if real is None else real + term_re
-                imag = term_im if imag is None else imag + term_im
+                real, imag = add_tap(
+                    real, imag, factors[tap], wide_ref[0, start : start + pulses], wide_ref[1, start : start + pulses]
+                )
             real = jnp.where(keep, real, 0.0)
             imag = jnp.where(keep, imag, 0.0)
             for owner in range(some):
@@ -321,7 +359,7 @@
         out_specs=[apart] + [whole if place else apart] * keep_ahead,
         out_shape=out_shape,
         scratch_shapes=[
-            pltpu.VMEM((2, rows + edge, lanes), jnp.float32),
+            pltpu.VMEM((2, rows, lanes), jnp.float32),
             pltpu.VMEM((owners, rows, 2 * own), jnp.bfloat16),
             pltpu.SemaphoreType.DMA((tile_beams // lanes,)),
         ]
@@ -508,6 +546,9 @@
                     ahead.get(number - 1), code, at, lens, limits, pulses, owners, number < len(chunks) - 1,
                     ready.get(index), len(groups[index]) - 1 - place, len(groups[index]), 100 if index else 3,
                 )
+            if ahead[number] is not None:
+                with jax.named_scope("edge"):
+                    ahead[number] = edge_sums(ahead[number], code, lens, pulses)
         elif kind == "send":
             with jax.named_scope("to_owners"):
                 got[number] = lax.all_to_all(ready[number], "beam", split_axis=0, concat_axis=0)
@@ -527,8 +568,9 @@
         elif kind == "compress<own":
             own_parts[number], ahead = lax.optimization_barrier((own_parts[number], ahead))
         elif kind == "compress<exchange":
-            index = owner_of[number[0]]
-            others[number[1]][0], ready[index] = lax.optimization_barrier((others[number[1]][0], ready[index]))
+            others[number[1]][0], ahead[number[0]] = lax.optimization_barrier(
+                (others[number[1]][0], ahead[number[0]])
+            )
         elif kind == "compress<beams":
             index = owner_of[number]
             power, ready[index] = lax.optimization_barrier((power, ready[index]))

time: 112 us -> 112 us (level)
    pallas_call x0 -> x3, Pallas kernels: none -> 1.96 us  [edge_sums(): pl.pallas_call(functools.partial(edge_kernel, pulses, code.shape[1], bloc...]
    pallas_call x4, Pallas kernels: 8.84 us -> 7.25 us  [compress(): pl.pallas_call(functools.partial(compress_kernel, pulses, taps, len(parts...]
    ppermute x4, waiting for transfers between devices: 13.1 us -> 11.8 us  [on_device(): lax.ppermute(part, 'tile', [(i, (i + away) % tiles) for i in range(tiles)])]
where the time goes in v6:
time: 112 us; the launch traced here: 111 us
  Pallas kernels  48.6 us (43%)
  waiting for transfers between devices  38.2 us (34%)
  starting transfers between devices  21 us (19%)
  other arithmetic  2.11 us (2%)
    pallas_call x4, Pallas kernels, form_beams(): pl.pallas_call(functools.partial(beam_kernel, samples, gates, gate, count...  30 us
    all_to_all x2, waiting for transfers between devices, on_device(): lax.all_to_all(ready[number], 'beam', split_axis=0, concat_axis=0)  23.7 us
    all_to_all x2, starting transfers between devices, on_device(): lax.all_to_all(ready[number], 'beam', split_axis=0, concat_axis=0)  12.5 us
    ppermute x4, waiting for transfers between devices, on_device(): lax.ppermute(part, 'tile', [(i, (i + away) % tiles) for i in range(tiles)])  11.8 us
    pallas_call x4, Pallas kernels, compress(): pl.pallas_call(functools.partial(compress_kernel, pulses, taps, len(parts...  7.25 us
    pallas_call x2, Pallas kernels, doppler(): pl.pallas_call(functools.partial(doppler_kernel, pulses, first, some), in...  6.08 us
    ppermute x6, starting transfers between devices, sum_over(): lax.ppermute(values, axis, [(i, i ^ away) for i in range(size)])  5.9 us
    ppermute x6, waiting for transfers between devices, sum_over(): lax.ppermute(values, axis, [(i, i ^ away) for i in range(size)])  2.62 us
  transfers between devices with their start and end apart: 12, of which 8 were waited for; matrix products, arithmetic and copies ran while one was open for 0% of the time, Pallas kernels for 35%

profile of v6, /device:TPU:9, one launch (start us, length us, event | category | flops | bytes accessed | tf_op | source)
XLA Modules:
  0.0 111.2 jit_solution(16462243838662566151)
XLA Ops:
  0.0 0.0 copy-start.2
  0.0 0.0 copy-start.3
  0.0 0.0 copy-start.1
  0.0 2.1 %multiply_reduce_fusion = f32[1024]{0:T(1024)S(1)} fusion(bf16[2,1024,512]{2,1,0:T(8,128)(2,1)} %echoes_ref.7), kind=kLoop, calls=%fused_computation | loop fusion | flops 3144704 | bytes 2101248 | tf_op jit(solution)/shard_map/reduce_sum | solution.py:503
  2.1 1.9 %collective-permute-start.2 = (f32[1,1024]{1,0:T(1,128)S(1)}, f32[1,1024]{1,0:T(1,128)S(1)}, u32[]{:S(2)}, u32[]{:S(2)}) collective-permute-start(f32[1,1024]{1,0:T(1,128)S(1)} %bitcast.7), channel_id=1, source_target_pairs={{0,3},{1,2},{2,1},{3,0},{4,7},{5,6},{6,5},{7,4},{8,11},{9,10},{10,... | collective-permute-start | bytes 12296 | tf_op jit(solution)/shard_map/ppermute | solution.py:452
  4.0 0.2 collective-permute-start.1
  4.2 0.2 collective-permute-start
  4.5 1.0 collective-permute-done.2.refs_3_
  5.5 0.9 collective-permute-done.1.refs_2_
  6.4 0.0 collective-permute-done.refs_1_
  6.5 1.4 %collective-permute-start.5 = (f32[1,1024]{1,0:T(1,128)S(1)}, f32[1,1024]{1,0:T(1,128)S(1)}, u32[]{:S(2)}, u32[]{:S(2)}) collective-permute-start(f32[1,1024]{1,0:T(1,128)S(1)} %add.2.refs_0_), channel_id=1, source_target_pairs={{0,12},{1,13},{2,14},{3,15},{4,8},{5,9},{6,10},{7,11},{8,4},{9,5},... | collective-permute-start | bytes 12296 | tf_op jit(solution)/shard_map/ppermute | solution.py:452
  7.8 1.1 collective-permute-start.4
  8.9 1.1 collective-permute-start.3
  10.0 0.0 copy-done.2
  10.0 0.0 copy-done.3
  10.0 0.0 copy-done.1
  10.0 0.7 lookup.1
  10.7 0.0 copy-start
  10.7 0.0 collective-permute-done.5.refs_3_
  10.7 0.4 collective-permute-done.4.refs_2_
  11.2 0.2 collective-permute-done.3.refs_1_
  11.4 0.9 copy-done
  12.3 7.1 %beams.4 = (bf16[256,1024]{1,0:T(8,128)(2,1)}, bf16[256,2048]{1,0:T(8,128)(2,1)S(1)}) custom-call(bf16[2,1024,512]{2,1,0:T(8,128)(2,1)S(1)} %copy-done, f32[1,1024]{1,0:T(1,128)S(1)} %add.3.power_ref, s32[1,2048]{1,0:T(1,128)S(1)} %get-tuple-element.42.order_ref, bf16[2,2048,1024]{2,1,0:T(8,128)(2,1)} %steer_ref.7), custom_call_target="tpu_custom_call" | custom-call | flops 10350000128 | bytes 1 | tf_op jit(solution)/shard_map/beams/beams/pallas_call | solution.py:210
  19.4 0.0 slice-start
  19.5 0.0 slice-start.1
  19.5 1.3 %collective-permute-start.7 = (bf16[256,1024]{1,0:T(8,128)(2,1)}, bf16[256,1024]{1,0:T(8,128)(2,1)S(1)}, u32[]{:S(2)}, u32[]{:S(2)}) collective-permute-start(bf16[256,1024]{1,0:T(8,128)(2,1)} %get-tuple-element.56), channel_id=1, source_target_pairs={{0,16},{16,0},{1,17},{17,1},{2,18},{18,2},{3,19},{19,3},{4,20},{20... | collective-permute-start | bytes 1572872 | tf_op jit(solution)/shard_map/tile_sum/ppermute | solution.py:533
  20.7 9.1 %beams.5 = (bf16[256,1024]{1,0:T(8,128)(2,1)S(1)}, bf16[256,1024]{1,0:T(8,128)(2,1)}) custom-call(bf16[2,1024,512]{2,1,0:T(8,128)(2,1)S(1)} %copy-done, f32[1,1024]{1,0:T(1,128)S(1)} %add.3.power_ref, s32[1,2048]{1,0:T(1,128)S(1)} %get-tuple-element.42.order_ref, bf16[2,2048,1024]{2,1,0:T(8,128)(2,1)} %steer_ref.7), custom_call_target="tpu_custom_call" | custom-call | flops 10350000128 | bytes 1 | tf_op jit(solution)/shard_map/beams/beams/pallas_call | solution.py:210
  29.8 0.3 collective-permute-start.6
  30.1 0.0 slice-done
  30.1 0.0 slice-done.1
  30.1 6.6 %beams.6 = (bf16[256,1024]{1,0:T(8,128)(2,1)S(1)}, bf16[256,1024]{1,0:T(8,128)(2,1)}) custom-call(bf16[2,1024,512]{2,1,0:T(8,128)(2,1)S(1)} %copy-done, f32[1,1024]{1,0:T(1,128)S(1)} %add.3.power_ref, s32[1,2048]{1,0:T(1,128)S(1)} %get-tuple-element.42.order_ref, bf16[2,2048,1024]{2,1,0:T(8,128)(2,1)S(1)} %bitcast.6), custom_call_target="tpu_custom_call" | custom-call | flops 10350000128 | bytes 1 | tf_op jit(solution)/shard_map/beams/beams/pallas_call | solution.py:210
  36.7 0.0 copy-start.4
  36.7 1.3 %own.2.rest_0_ = bf16[256,1024]{1,0:T(8,128)(2,1)S(1)} custom-call(bf16[256,2048]{1,0:T(8,128)(2,1)S(1)} %get-tuple-element.47.beams_ref, s32[1,2048]{1,0:T(1,128)S(1)} %get-tuple-element.42.order_ref), custom_call_target="tpu_custom_call" | custom-call | flops 2300000000 | bytes 1 | tf_op jit(solution)/shard_map/beams/own/pallas_call | solution.py:185
  38.1 0.0 collective-permute-done.7.rest_1_
  38.1 0.0 copy-done.4
  38.1 1.8 %compress.4 = (bf16[16,256,128]{2,1,0:T(8,128)(2,1)}, bf16[2,112,1024]{2,1,0:T(8,128)(2,1)S(1)}) custom-call(bf16[2,8]{1,0:T(2,128)(2,1)S(1)} %copy-done.4, s32[1]{0:T(128)} %bitcast.at_ref, s32[1,1024]{1,0:T(1,128)S(1)} %get-tuple-element.40.lens_ref, s32[1,1024]{1,0:T(1,128)S(1)} %get-tuple-element.41.limits_ref, bf16[256,1024]{1,0:T(8,128)(2,1)S(1)} %own.2.rest_0_, ...), custom_call_target="tpu_custom_call" | custom-call | flops 3449999872 | bytes 1 | tf_op jit(solution)/shard_map/compress/compress/pallas_call | solution.py:354
  39.8 0.7 edge.3.rest_2_
  40.5 3.1 %collective-permute-done.6.rest_1_ = bf16[256,1024]{1,0:T(8,128)(2,1)S(1)} collective-permute-done((bf16[256,1024]{1,0:T(8,128)(2,1)}, bf16[256,1024]{1,0:T(8,128)(2,1)S(1)}, u32[]{:S(2)}, u32[]{:S(2)}) %collective-permute-start.6) | collective-permute-done | bytes 524320 | tf_op jit(solution)/shard_map/tile_sum/ppermute | solution.py:533
  43.6 0.7 collective-permute-start.8
  44.3 1.9 %compress.5 = (bf16[16,256,128]{2,1,0:T(8,128)(2,1)}, bf16[2,112,1024]{2,1,0:T(8,128)(2,1)}) custom-call(bf16[2,8]{1,0:T(2,128)(2,1)S(1)} %copy-done.4, s32[1]{0:T(128)} %bitcast.at_ref, s32[1,1024]{1,0:T(1,128)S(1)} %get-tuple-element.40.lens_ref, s32[1,1024]{1,0:T(1,128)S(1)} %get-tuple-element.41.limits_ref, ...), custom_call_target="tpu_custom_call", output_to_operand_aliasing={{0}: (7, {})} | custom-call | flops 3449999872 | bytes 1 | tf_op jit(solution)/shard_map/compress/compress/pallas_call | solution.py:354
  46.3 7.6 %all-to-all-start.1 = ((bf16[16,256,128]{2,1,0:T(8,128)(2,1)}), bf16[16,256,128]{2,1,0:T(8,128)(2,1)}, u32[]{:S(2)}, u32[]{:S(2)}) async-start(bf16[16,256,128]{2,1,0:T(8,128)(2,1)} %get-tuple-element.74), calls=%async_computation.1 | async-start | bytes 2097152 | tf_op jit(solution)/shard_map/to_owners/all_to_all | solution.py:554
  53.9 0.0 copy-start.6
  53.9 7.2 %beams.7 = (bf16[256,1024]{1,0:T(8,128)(2,1)}, bf16[256,2048]{1,0:T(8,128)(2,1)S(1)}) custom-call(bf16[2,1024,512]{2,1,0:T(8,128)(2,1)S(1)} %copy-done, f32[1,1024]{1,0:T(1,128)S(1)} %add.3.power_ref, s32[1,2048]{1,0:T(1,128)S(1)} %get-tuple-element.42.order_ref, bf16[2,2048,1024]{2,1,0:T(8,128)(2,1)} %steer_ref.7), custom_call_target="tpu_custom_call" | custom-call | bytes 1 | tf_op jit(solution)/shard_map/beams/beams/pallas_call | solution.py:210
  61.0 0.3 collective-permute-start.9
  61.4 0.0 copy-done.6
  61.4 0.7 edge.4.rest_2_
  62.0 0.0 collective-permute-done.8.rest_1_
  62.0 1.8 %compress.6 = (bf16[16,256,128]{2,1,0:T(8,128)(2,1)}, bf16[2,112,1024]{2,1,0:T(8,128)(2,1)S(1)}) custom-call(bf16[2,8]{1,0:T(2,128)(2,1)S(1)} %copy-done.4, s32[1]{0:T(128)} %bitcast.at_ref, s32[1,1024]{1,0:T(1,128)S(1)} %get-tuple-element.40.lens_ref, s32[1,1024]{1,0:T(1,128)S(1)} %get-tuple-element.41.limits_ref, ...), custom_call_target="tpu_custom_call" | custom-call | flops 115000000512 | bytes 1 | tf_op jit(solution)/shard_map/compress/compress/pallas_call | solution.py:354
  63.8 0.7 edge.5.rest_2_
  64.5 1.3 %own.3.rest_0_ = bf16[256,1024]{1,0:T(8,128)(2,1)S(1)} custom-call(bf16[256,2048]{1,0:T(8,128)(2,1)S(1)} %get-tuple-element.70.beams_ref, s32[1,2048]{1,0:T(1,128)S(1)} %get-tuple-element.42.order_ref), custom_call_target="tpu_custom_call" | custom-call | flops 2300000000 | bytes 1 | tf_op jit(solution)/shard_map/beams/own/pallas_call | solution.py:185
  65.8 8.7 %collective-permute-done.9.rest_1_ = bf16[256,1024]{1,0:T(8,128)(2,1)S(1)} collective-permute-done((bf16[256,1024]{1,0:T(8,128)(2,1)}, bf16[256,1024]{1,0:T(8,128)(2,1)S(1)}, u32[]{:S(2)}, u32[]{:S(2)}) %collective-permute-start.9) | collective-permute-done | bytes 524320 | tf_op jit(solution)/shard_map/tile_sum/ppermute | solution.py:533
  74.5 0.0 copy-start.5
  74.5 1.8 %compress.7 = bf16[16,256,128]{2,1,0:T(8,128)(2,1)} custom-call(bf16[2,8]{1,0:T(2,128)(2,1)S(1)} %copy-done.4, s32[1]{0:T(128)} %bitcast.at_ref, s32[1,1024]{1,0:T(1,128)S(1)} %get-tuple-element.40.lens_ref, s32[1,1024]{1,0:T(1,128)S(1)} %get-tuple-element.41.limits_ref, bf16[256,1024]{1,0:T(8,128)(2,1)S(1)} %own.3.rest_0_, ...), custom_call_target="tpu_custom_call", output_to_operand_aliasing={{}: (7, {})} | custom-call | flops 115000000512 | bytes 1 | tf_op jit(solution)/shard_map/compress/compress/pallas_call | solution.py:354
  76.3 2.6 %all-to-all-done.1.got_ref = bf16[16,256,128]{2,1,0:T(8,128)(2,1)} async-done(((bf16[16,256,128]{2,1,0:T(8,128)(2,1)}), bf16[16,256,128]{2,1,0:T(8,128)(2,1)}, u32[]{:S(2)}, u32[]{:S(2)}) %all-to-all-start.1) | async-done | bytes 1048608 | tf_op jit(solution)/shard_map/to_owners/all_to_all | solution.py:554
  78.8 4.9 %all-to-all-start = ((bf16[16,256,128]{2,1,0:T(8,128)(2,1)}), bf16[16,256,128]{2,1,0:T(8,128)(2,1)S(1)}, u32[]{:S(2)}, u32[]{:S(2)}) async-start(bf16[16,256,128]{2,1,0:T(8,128)(2,1)} %compress.7), calls=%async_computation | async-start | bytes 2097152 | tf_op jit(solution)/shard_map/to_owners/all_to_all | solution.py:554
  83.8 0.0 copy-done.5
  83.8 3.7 %doppler.2.rest_0_ = f32[64,2,32,256]{3,2,1,0:T(8,128)} custom-call(bf16[16,256,128]{2,1,0:T(8,128)(2,1)} %all-to-all-done.1.got_ref, bf16[256,512]{1,0:T(8,128)(2,1)S(1)} %copy-done.5), custom_call_target="tpu_custom_call" | custom-call | flops 3449999872 | bytes 1 | tf_op jit(solution)/shard_map/doppler/doppler/pallas_call | solution.py:422
  87.4 21.2 %all-to-all-done.got_ref = bf16[16,256,128]{2,1,0:T(8,128)(2,1)S(1)} async-done(((bf16[16,256,128]{2,1,0:T(8,128)(2,1)}), bf16[16,256,128]{2,1,0:T(8,128)(2,1)S(1)}, u32[]{:S(2)}, u32[]{:S(2)}) %all-to-all-start) | async-done | bytes 1048608 | tf_op jit(solution)/shard_map/to_owners/all_to_all | solution.py:554
  108.6 2.4 %doppler.3 = f32[64,2,32,256]{3,2,1,0:T(8,128)} custom-call(bf16[16,256,128]{2,1,0:T(8,128)(2,1)S(1)} %all-to-all-done.got_ref, bf16[256,512]{1,0:T(8,128)(2,1)S(1)} %copy-done.5, f32[64,2,32,256]{3,2,1,0:T(8,128)} %doppler.2.rest_0_), custom_call_target="tpu_custom_call", output_to_operand_aliasing={{}: (2, {})} | custom-call | flops 3449999872 | bytes 1 | tf_op jit(solution)/shard_map/doppler/doppler/pallas_call | solution.py:422
  (3 shorter events, 0.0 us)
Async XLA Ops:
  0.0 10.0 %copy-start.2 = (s32[2048]{0:T(1024)S(1)}, s32[2048]{0:T(1024)}, u32[]{:S(2)}) copy-start(s32[2048]{0:T(1024)} %param.12) | copy-start | bytes 24580
  0.0 10.0 %copy-start.3 = (s32[2048]{0:T(1024)S(1)}, s32[2048]{0:T(1024)}, u32[]{:S(2)}) copy-start(s32[2048]{0:T(1024)} %param.11) | copy-start | bytes 24580
  0.0 10.0 %copy-start.1 = (s32[2048]{0:T(1024)S(1)}, s32[2048]{0:T(1024)}, u32[]{:S(2)}) copy-start(s32[2048]{0:T(1024)} %param.10) | copy-start | bytes 24580
  2.1 3.4 %collective-permute-start.2 = (f32[1,1024]{1,0:T(1,128)S(1)}, f32[1,1024]{1,0:T(1,128)S(1)}, u32[]{:S(2)}, u32[]{:S(2)}) collective-permute-start(f32[1,1024]{1,0:T(1,128)S(1)} %bitcast.7), channel_id=1, source_target_pairs={{0,3},{1,2},{2,1},{3,0},{4,7},{5,6},{6,5},{7,4},{8,11},{9,10},{10,... | collective-permute-start | bytes 12296 | tf_op jit(solution)/shard_map/ppermute | solution.py:452
  4.0 2.5 %collective-permute-start.1 = (f32[1,1024]{1,0:T(1,128)S(1)}, f32[1,1024]{1,0:T(1,128)S(1)}, u32[]{:S(2)}, u32[]{:S(2)}) collective-permute-start(f32[1,1024]{1,0:T(1,128)S(1)} %bitcast.8), channel_id=1, source_target_pairs={{0,2},{1,3},{2,0},{3,1},{4,6},{5,7},{6,4},{7,5},{8,10},{9,11},{10,... | collective-permute-start | bytes 12296 | tf_op jit(solution)/shard_map/ppermute | solution.py:452
  4.2 2.2 %collective-permute-start = (f32[1,1024]{1,0:T(1,128)S(1)}, f32[1,1024]{1,0:T(1,128)S(1)}, u32[]{:S(2)}, u32[]{:S(2)}) collective-permute-start(f32[1,1024]{1,0:T(1,128)S(1)} %bitcast.9), channel_id=1, source_target_pairs={{0,1},{1,0},{2,3},{3,2},{4,5},{5,4},{6,7},{7,6},{8,9},{9,8},{10,11... | collective-permute-start | bytes 12296 | tf_op jit(solution)/shard_map/ppermute | solution.py:452
  6.5 4.3 %collective-permute-start.5 = (f32[1,1024]{1,0:T(1,128)S(1)}, f32[1,1024]{1,0:T(1,128)S(1)}, u32[]{:S(2)}, u32[]{:S(2)}) collective-permute-start(f32[1,1024]{1,0:T(1,128)S(1)} %add.2.refs_0_), channel_id=1, source_target_pairs={{0,12},{1,13},{2,14},{3,15},{4,8},{5,9},{6,10},{7,11},{8,4},{9,5},... | collective-permute-start | bytes 12296 | tf_op jit(solution)/shard_map/ppermute | solution.py:452
  7.8 3.4 %collective-permute-start.4 = (f32[1,1024]{1,0:T(1,128)S(1)}, f32[1,1024]{1,0:T(1,128)S(1)}, u32[]{:S(2)}, u32[]{:S(2)}) collective-permute-start(f32[1,1024]{1,0:T(1,128)S(1)} %add.2.refs_0_), channel_id=1, source_target_pairs={{0,8},{1,9},{2,10},{3,11},{4,12},{5,13},{6,14},{7,15},{8,0},{9,1},... | collective-permute-start | bytes 12296 | tf_op jit(solution)/shard_map/ppermute | solution.py:452
  8.9 2.5 %collective-permute-start.3 = (f32[1,1024]{1,0:T(1,128)S(1)}, f32[1,1024]{1,0:T(1,128)S(1)}, u32[]{:S(2)}, u32[]{:S(2)}) collective-permute-start(f32[1,1024]{1,0:T(1,128)S(1)} %add.2.refs_0_), channel_id=1, source_target_pairs={{0,4},{1,5},{2,6},{3,7},{4,0},{5,1},{6,2},{7,3},{8,12},{9,13},{10,... | collective-permute-start | bytes 12296 | tf_op jit(solution)/shard_map/ppermute | solution.py:452
  10.7 1.6 %copy-start = (bf16[2,1024,512]{2,1,0:T(8,128)(2,1)S(1)}, bf16[2,1024,512]{2,1,0:T(8,128)(2,1)}, u32[]{:S(2)}) copy-start(bf16[2,1024,512]{2,1,0:T(8,128)(2,1)} %echoes_ref.7) | copy-start | bytes 6291460
  19.4 10.7 %slice-start = ((s8[8388608]{0:T(1024)(128)(4,1)}), s8[4194304]{0:T(1024)(128)(4,1)S(1)}, s32[]{:S(2)}) async-start(s8[8388608]{0:T(1024)(128)(4,1)} %bitcast.5), calls=%async_computation.2 | async-start | bytes 8388608
  19.5 10.7 %slice-start.1 = ((s8[8388608]{0:T(1024)(128)(4,1)}), s8[4194304]{0:T(1024)(128)(4,1)S(1)}, s32[]{:S(2)}) async-start(s8[8388608]{0:T(1024)(128)(4,1)} %bitcast.5), calls=%async_computation.3 | async-start | bytes 8388608
  19.5 18.6 %collective-permute-start.7 = (bf16[256,1024]{1,0:T(8,128)(2,1)}, bf16[256,1024]{1,0:T(8,128)(2,1)S(1)}, u32[]{:S(2)}, u32[]{:S(2)}) collective-permute-start(bf16[256,1024]{1,0:T(8,128)(2,1)} %get-tuple-element.56), channel_id=1, source_target_pairs={{0,16},{16,0},{1,17},{17,1},{2,18},{18,2},{3,19},{19,3},{4,20},{20... | collective-permute-start | bytes 1572872 | tf_op jit(solution)/shard_map/tile_sum/ppermute | solution.py:533
  29.8 13.8 %collective-permute-start.6 = (bf16[256,1024]{1,0:T(8,128)(2,1)}, bf16[256,1024]{1,0:T(8,128)(2,1)S(1)}, u32[]{:S(2)}, u32[]{:S(2)}) collective-permute-start(bf16[256,1024]{1,0:T(8,128)(2,1)} %get-tuple-element.53), channel_id=1, source_target_pairs={{0,16},{16,0},{1,17},{17,1},{2,18},{18,2},{3,19},{19,3},{4,20},{20... | collective-permute-start | bytes 1572872 | tf_op jit(solution)/shard_map/tile_sum/ppermute | solution.py:533
  36.7 1.3 %copy-start.4 = (bf16[2,8]{1,0:T(2,128)(2,1)S(1)}, bf16[2,8]{1,0:T(2,128)(2,1)}, u32[]{:S(2)}) copy-start(bf16[2,8]{1,0:T(2,128)(2,1)} %code_ref.13) | copy-start | bytes 100
  43.6 18.4 %collective-permute-start.8 = (bf16[256,1024]{1,0:T(8,128)(2,1)}, bf16[256,1024]{1,0:T(8,128)(2,1)S(1)}, u32[]{:S(2)}, u32[]{:S(2)}) collective-permute-start(bf16[256,1024]{1,0:T(8,128)(2,1)} %get-tuple-element.68), channel_id=1, source_target_pairs={{0,16},{16,0},{1,17},{17,1},{2,18},{18,2},{3,19},{19,3},{4,20},{20... | collective-permute-start | bytes 1572872 | tf_op jit(solution)/shard_map/tile_sum/ppermute | solution.py:533
  46.3 32.6 %all-to-all-start.1 = ((bf16[16,256,128]{2,1,0:T(8,128)(2,1)}), bf16[16,256,128]{2,1,0:T(8,128)(2,1)}, u32[]{:S(2)}, u32[]{:S(2)}) async-start(bf16[16,256,128]{2,1,0:T(8,128)(2,1)} %get-tuple-element.74), calls=%async_computation.1 | async-start | bytes 2097152 | tf_op jit(solution)/shard_map/to_owners/all_to_all | solution.py:554
  53.9 7.5 %copy-start.6 = (bf16[2,112,1024]{2,1,0:T(8,128)(2,1)S(1)}, bf16[2,112,1024]{2,1,0:T(8,128)(2,1)}, u32[]{:S(2)}) copy-start(bf16[2,112,1024]{2,1,0:T(8,128)(2,1)} %get-tuple-element.66.ahead_ref) | copy-start | bytes 1376260
  61.0 13.4 %collective-permute-start.9 = (bf16[256,1024]{1,0:T(8,128)(2,1)}, bf16[256,1024]{1,0:T(8,128)(2,1)S(1)}, u32[]{:S(2)}, u32[]{:S(2)}) collective-permute-start(bf16[256,1024]{1,0:T(8,128)(2,1)} %get-tuple-element.71), channel_id=1, source_target_pairs={{0,16},{16,0},{1,17},{17,1},{2,18},{18,2},{3,19},{19,3},{4,20},{20... | collective-permute-start | bytes 1572872 | tf_op jit(solution)/shard_map/tile_sum/ppermute | solution.py:533
  74.5 9.3 %copy-start.5 = (bf16[256,512]{1,0:T(8,128)(2,1)S(1)}, bf16[256,512]{1,0:T(8,128)(2,1)}, u32[]{:S(2)}) copy-start(bf16[256,512]{1,0:T(8,128)(2,1)} %constant.10.clone.table_ref) | copy-start | bytes 786436
  78.8 29.8 %all-to-all-start = ((bf16[16,256,128]{2,1,0:T(8,128)(2,1)}), bf16[16,256,128]{2,1,0:T(8,128)(2,1)S(1)}, u32[]{:S(2)}, u32[]{:S(2)}) async-start(bf16[16,256,128]{2,1,0:T(8,128)(2,1)} %compress.7), calls=%async_computation | async-start | bytes 2097152 | tf_op jit(solution)/shard_map/to_owners/all_to_all | solution.py:554

commit v7 on v6

--- a/solution.py
+++ b/solution.py
@@ -225,11 +225,9 @@
 
 
 def factors_of(code_ref, lens, taps):
+    code = code_ref[...].astype(jnp.float32)
     return [
-        tuple(
-            jnp.where(tap < lens, code_ref[part : part + 1, tap : tap + 1].astype(jnp.float32), 0.0)
-            for part in range(2)
-        )
+        tuple(jnp.where(tap < lens, code[part : part + 1, tap : tap + 1], 0.0) for part in range(2))
         for tap in range(taps)
     ]
 

time: 112 us -> 112 us (level)
  no operation moved by 1% of the time
where the time goes in v7:
time: 112 us; the launch traced here: 111 us
  Pallas kernels  48.6 us (43%)
  waiting for transfers between devices  38.2 us (34%)
  starting transfers between devices  21 us (19%)
  other arithmetic  2.11 us (2%)
    pallas_call x4, Pallas kernels, form_beams(): pl.pallas_call(functools.partial(beam_kernel, samples, gates, gate, count...  30 us
    all_to_all x2, waiting for transfers between devices, on_device(): lax.all_to_all(ready[number], 'beam', split_axis=0, concat_axis=0)  23.7 us
    all_to_all x2, starting transfers between devices, on_device(): lax.all_to_all(ready[number], 'beam', split_axis=0, concat_axis=0)  12.5 us
    ppermute x4, waiting for transfers between devices, on_device(): lax.ppermute(part, 'tile', [(i, (i + away) % tiles) for i in range(tiles)])  11.8 us
    pallas_call x4, Pallas kernels, compress(): pl.pallas_call(functools.partial(compress_kernel, pulses, taps, len(parts...  7.25 us
    pallas_call x2, Pallas kernels, doppler(): pl.pallas_call(functools.partial(doppler_kernel, pulses, first, some), in...  6.08 us
    ppermute x6, starting transfers between devices, sum_over(): lax.ppermute(values, axis, [(i, i ^ away) for i in range(size)])  5.9 us
    ppermute x6, waiting for transfers between devices, sum_over(): lax.ppermute(values, axis, [(i, i ^ away) for i in range(size)])  2.62 us
  transfers between devices with their start and end apart: 12, of which 8 were waited for; matrix products, arithmetic and copies ran while one was open for 0% of the time, Pallas kernels for 35%

profile of v7, /device:TPU:9, one launch (start us, length us, event | category | flops | bytes accessed | tf_op | source)
XLA Modules:
  0.0 111.2 jit_solution(16462243838662566151)
XLA Ops:
  0.0 0.0 copy-start.2
  0.0 0.0 copy-start.3
  0.0 0.0 copy-start.1
  0.0 2.1 %multiply_reduce_fusion = f32[1024]{0:T(1024)S(1)} fusion(bf16[2,1024,512]{2,1,0:T(8,128)(2,1)} %echoes_ref.7), kind=kLoop, calls=%fused_computation | loop fusion | flops 3144704 | bytes 2101248 | tf_op jit(solution)/shard_map/reduce_sum | solution.py:501
  2.1 1.9 %collective-permute-start.2 = (f32[1,1024]{1,0:T(1,128)S(1)}, f32[1,1024]{1,0:T(1,128)S(1)}, u32[]{:S(2)}, u32[]{:S(2)}) collective-permute-start(f32[1,1024]{1,0:T(1,128)S(1)} %bitcast.7), channel_id=1, source_target_pairs={{0,3},{1,2},{2,1},{3,0},{4,7},{5,6},{6,5},{7,4},{8,11},{9,10},{10,... | collective-permute-start | bytes 12296 | tf_op jit(solution)/shard_map/ppermute | solution.py:450
  4.0 0.2 collective-permute-start.1
  4.2 0.2 collective-permute-start
  4.5 1.0 collective-permute-done.2.refs_3_
  5.5 0.9 collective-permute-done.1.refs_2_
  6.4 0.0 collective-permute-done.refs_1_
  6.5 1.4 %collective-permute-start.5 = (f32[1,1024]{1,0:T(1,128)S(1)}, f32[1,1024]{1,0:T(1,128)S(1)}, u32[]{:S(2)}, u32[]{:S(2)}) collective-permute-start(f32[1,1024]{1,0:T(1,128)S(1)} %add.2.refs_0_), channel_id=1, source_target_pairs={{0,12},{1,13},{2,14},{3,15},{4,8},{5,9},{6,10},{7,11},{8,4},{9,5},... | collective-permute-start | bytes 12296 | tf_op jit(solution)/shard_map/ppermute | solution.py:450
  7.8 1.1 collective-permute-start.4
  8.9 1.1 collective-permute-start.3
  10.0 0.0 copy-done.2
  10.0 0.0 copy-done.3
  10.0 0.0 copy-done.1
  10.0 0.7 lookup.1
  10.7 0.0 copy-start
  10.7 0.0 collective-permute-done.5.refs_3_
  10.7 0.4 collective-permute-done.4.refs_2_
  11.2 0.2 collective-permute-done.3.refs_1_
  11.4 0.9 copy-done
  12.3 7.1 %beams.4 = (bf16[256,1024]{1,0:T(8,128)(2,1)}, bf16[256,2048]{1,0:T(8,128)(2,1)S(1)}) custom-call(bf16[2,1024,512]{2,1,0:T(8,128)(2,1)S(1)} %copy-done, f32[1,1024]{1,0:T(1,128)S(1)} %add.3.power_ref, s32[1,2048]{1,0:T(1,128)S(1)} %get-tuple-element.42.order_ref, bf16[2,2048,1024]{2,1,0:T(8,128)(2,1)} %steer_ref.7), custom_call_target="tpu_custom_call" | custom-call | flops 10350000128 | bytes 1 | tf_op jit(solution)/shard_map/beams/beams/pallas_call | solution.py:210
  19.4 0.0 slice-start
  19.5 0.0 slice-start.1
  19.5 1.3 %collective-permute-start.7 = (bf16[256,1024]{1,0:T(8,128)(2,1)}, bf16[256,1024]{1,0:T(8,128)(2,1)S(1)}, u32[]{:S(2)}, u32[]{:S(2)}) collective-permute-start(bf16[256,1024]{1,0:T(8,128)(2,1)} %get-tuple-element.56), channel_id=1, source_target_pairs={{0,16},{16,0},{1,17},{17,1},{2,18},{18,2},{3,19},{19,3},{4,20},{20... | collective-permute-start | bytes 1572872 | tf_op jit(solution)/shard_map/tile_sum/ppermute | solution.py:531
  20.7 9.1 %beams.5 = (bf16[256,1024]{1,0:T(8,128)(2,1)S(1)}, bf16[256,1024]{1,0:T(8,128)(2,1)}) custom-call(bf16[2,1024,512]{2,1,0:T(8,128)(2,1)S(1)} %copy-done, f32[1,1024]{1,0:T(1,128)S(1)} %add.3.power_ref, s32[1,2048]{1,0:T(1,128)S(1)} %get-tuple-element.42.order_ref, bf16[2,2048,1024]{2,1,0:T(8,128)(2,1)} %steer_ref.7), custom_call_target="tpu_custom_call" | custom-call | flops 10350000128 | bytes 1 | tf_op jit(solution)/shard_map/beams/beams/pallas_call | solution.py:210
  29.8 0.3 collective-permute-start.6
  30.1 0.0 slice-done
  30.1 0.0 slice-done.1
  30.1 6.6 %beams.6 = (bf16[256,1024]{1,0:T(8,128)(2,1)S(1)}, bf16[256,1024]{1,0:T(8,128)(2,1)}) custom-call(bf16[2,1024,512]{2,1,0:T(8,128)(2,1)S(1)} %copy-done, f32[1,1024]{1,0:T(1,128)S(1)} %add.3.power_ref, s32[1,2048]{1,0:T(1,128)S(1)} %get-tuple-element.42.order_ref, bf16[2,2048,1024]{2,1,0:T(8,128)(2,1)S(1)} %bitcast.6), custom_call_target="tpu_custom_call" | custom-call | flops 10350000128 | bytes 1 | tf_op jit(solution)/shard_map/beams/beams/pallas_call | solution.py:210
  36.7 0.0 copy-start.4
  36.7 1.3 %own.2.rest_0_ = bf16[256,1024]{1,0:T(8,128)(2,1)S(1)} custom-call(bf16[256,2048]{1,0:T(8,128)(2,1)S(1)} %get-tuple-element.47.beams_ref, s32[1,2048]{1,0:T(1,128)S(1)} %get-tuple-element.42.order_ref), custom_call_target="tpu_custom_call" | custom-call | flops 2300000000 | bytes 1 | tf_op jit(solution)/shard_map/beams/own/pallas_call | solution.py:185
  38.1 0.0 collective-permute-done.7.rest_1_
  38.1 0.0 copy-done.4
  38.1 1.8 %compress.4 = (bf16[16,256,128]{2,1,0:T(8,128)(2,1)}, bf16[2,112,1024]{2,1,0:T(8,128)(2,1)S(1)}) custom-call(bf16[2,8]{1,0:T(2,128)(2,1)S(1)} %copy-done.4, s32[1]{0:T(128)} %bitcast.at_ref, s32[1,1024]{1,0:T(1,128)S(1)} %get-tuple-element.40.lens_ref, s32[1,1024]{1,0:T(1,128)S(1)} %get-tuple-element.41.limits_ref, bf16[256,1024]{1,0:T(8,128)(2,1)S(1)} %own.2.rest_0_, ...), custom_call_target="tpu_custom_call" | custom-call | flops 3449999872 | bytes 1 | tf_op jit(solution)/shard_map/compress/compress/pallas_call | solution.py:352
  39.8 0.7 edge.3.rest_2_
  40.5 3.1 %collective-permute-done.6.rest_1_ = bf16[256,1024]{1,0:T(8,128)(2,1)S(1)} collective-permute-done((bf16[256,1024]{1,0:T(8,128)(2,1)}, bf16[256,1024]{1,0:T(8,128)(2,1)S(1)}, u32[]{:S(2)}, u32[]{:S(2)}) %collective-permute-start.6) | collective-permute-done | bytes 524320 | tf_op jit(solution)/shard_map/tile_sum/ppermute | solution.py:531
  43.6 0.7 collective-permute-start.8
  44.3 1.9 %compress.5 = (bf16[16,256,128]{2,1,0:T(8,128)(2,1)}, bf16[2,112,1024]{2,1,0:T(8,128)(2,1)}) custom-call(bf16[2,8]{1,0:T(2,128)(2,1)S(1)} %copy-done.4, s32[1]{0:T(128)} %bitcast.at_ref, s32[1,1024]{1,0:T(1,128)S(1)} %get-tuple-element.40.lens_ref, s32[1,1024]{1,0:T(1,128)S(1)} %get-tuple-element.41.limits_ref, ...), custom_call_target="tpu_custom_call", output_to_operand_aliasing={{0}: (7, {})} | custom-call | flops 3449999872 | bytes 1 | tf_op jit(solution)/shard_map/compress/compress/pallas_call | solution.py:352
  46.3 7.6 %all-to-all-start.1 = ((bf16[16,256,128]{2,1,0:T(8,128)(2,1)}), bf16[16,256,128]{2,1,0:T(8,128)(2,1)}, u32[]{:S(2)}, u32[]{:S(2)}) async-start(bf16[16,256,128]{2,1,0:T(8,128)(2,1)} %get-tuple-element.74), calls=%async_computation.1 | async-start | bytes 2097152 | tf_op jit(solution)/shard_map/to_owners/all_to_all | solution.py:552
  53.9 0.0 copy-start.6
  53.9 7.2 %beams.7 = (bf16[256,1024]{1,0:T(8,128)(2,1)}, bf16[256,2048]{1,0:T(8,128)(2,1)S(1)}) custom-call(bf16[2,1024,512]{2,1,0:T(8,128)(2,1)S(1)} %copy-done, f32[1,1024]{1,0:T(1,128)S(1)} %add.3.power_ref, s32[1,2048]{1,0:T(1,128)S(1)} %get-tuple-element.42.order_ref, bf16[2,2048,1024]{2,1,0:T(8,128)(2,1)} %steer_ref.7), custom_call_target="tpu_custom_call" | custom-call | bytes 1 | tf_op jit(solution)/shard_map/beams/beams/pallas_call | solution.py:210
  61.0 0.3 collective-permute-start.9
  61.4 0.0 copy-done.6
  61.4 0.7 edge.4.rest_2_
  62.0 0.0 collective-permute-done.8.rest_1_
  62.0 1.8 %compress.6 = (bf16[16,256,128]{2,1,0:T(8,128)(2,1)}, bf16[2,112,1024]{2,1,0:T(8,128)(2,1)S(1)}) custom-call(bf16[2,8]{1,0:T(2,128)(2,1)S(1)} %copy-done.4, s32[1]{0:T(128)} %bitcast.at_ref, s32[1,1024]{1,0:T(1,128)S(1)} %get-tuple-element.40.lens_ref, s32[1,1024]{1,0:T(1,128)S(1)} %get-tuple-element.41.limits_ref, ...), custom_call_target="tpu_custom_call" | custom-call | flops 115000000512 | bytes 1 | tf_op jit(solution)/shard_map/compress/compress/pallas_call | solution.py:352
  63.8 0.7 edge.5.rest_2_
  64.5 1.3 %own.3.rest_0_ = bf16[256,1024]{1,0:T(8,128)(2,1)S(1)} custom-call(bf16[256,2048]{1,0:T(8,128)(2,1)S(1)} %get-tuple-element.70.beams_ref, s32[1,2048]{1,0:T(1,128)S(1)} %get-tuple-element.42.order_ref), custom_call_target="tpu_custom_call" | custom-call | flops 2300000000 | bytes 1 | tf_op jit(solution)/shard_map/beams/own/pallas_call | solution.py:185
  65.8 8.7 %collective-permute-done.9.rest_1_ = bf16[256,1024]{1,0:T(8,128)(2,1)S(1)} collective-permute-done((bf16[256,1024]{1,0:T(8,128)(2,1)}, bf16[256,1024]{1,0:T(8,128)(2,1)S(1)}, u32[]{:S(2)}, u32[]{:S(2)}) %collective-permute-start.9) | collective-permute-done | bytes 524320 | tf_op jit(solution)/shard_map/tile_sum/ppermute | solution.py:531
  74.5 0.0 copy-start.5
  74.5 1.8 %compress.7 = bf16[16,256,128]{2,1,0:T(8,128)(2,1)} custom-call(bf16[2,8]{1,0:T(2,128)(2,1)S(1)} %copy-done.4, s32[1]{0:T(128)} %bitcast.at_ref, s32[1,1024]{1,0:T(1,128)S(1)} %get-tuple-element.40.lens_ref, s32[1,1024]{1,0:T(1,128)S(1)} %get-tuple-element.41.limits_ref, bf16[256,1024]{1,0:T(8,128)(2,1)S(1)} %own.3.rest_0_, ...), custom_call_target="tpu_custom_call", output_to_operand_aliasing={{}: (7, {})} | custom-call | flops 115000000512 | bytes 1 | tf_op jit(solution)/shard_map/compress/compress/pallas_call | solution.py:352
  76.3 2.6 %all-to-all-done.1.got_ref = bf16[16,256,128]{2,1,0:T(8,128)(2,1)} async-done(((bf16[16,256,128]{2,1,0:T(8,128)(2,1)}), bf16[16,256,128]{2,1,0:T(8,128)(2,1)}, u32[]{:S(2)}, u32[]{:S(2)}) %all-to-all-start.1) | async-done | bytes 1048608 | tf_op jit(solution)/shard_map/to_owners/all_to_all | solution.py:552
  78.8 4.9 %all-to-all-start = ((bf16[16,256,128]{2,1,0:T(8,128)(2,1)}), bf16[16,256,128]{2,1,0:T(8,128)(2,1)S(1)}, u32[]{:S(2)}, u32[]{:S(2)}) async-start(bf16[16,256,128]{2,1,0:T(8,128)(2,1)} %compress.7), calls=%async_computation | async-start | bytes 2097152 | tf_op jit(solution)/shard_map/to_owners/all_to_all | solution.py:552
  83.8 0.0 copy-done.5
  83.8 3.7 %doppler.2.rest_0_ = f32[64,2,32,256]{3,2,1,0:T(8,128)} custom-call(bf16[16,256,128]{2,1,0:T(8,128)(2,1)} %all-to-all-done.1.got_ref, bf16[256,512]{1,0:T(8,128)(2,1)S(1)} %copy-done.5), custom_call_target="tpu_custom_call" | custom-call | flops 3449999872 | bytes 1 | tf_op jit(solution)/shard_map/doppler/doppler/pallas_call | solution.py:420
  87.4 21.2 %all-to-all-done.got_ref = bf16[16,256,128]{2,1,0:T(8,128)(2,1)S(1)} async-done(((bf16[16,256,128]{2,1,0:T(8,128)(2,1)}), bf16[16,256,128]{2,1,0:T(8,128)(2,1)S(1)}, u32[]{:S(2)}, u32[]{:S(2)}) %all-to-all-start) | async-done | bytes 1048608 | tf_op jit(solution)/shard_map/to_owners/all_to_all | solution.py:552
  108.6 2.4 %doppler.3 = f32[64,2,32,256]{3,2,1,0:T(8,128)} custom-call(bf16[16,256,128]{2,1,0:T(8,128)(2,1)S(1)} %all-to-all-done.got_ref, bf16[256,512]{1,0:T(8,128)(2,1)S(1)} %copy-done.5, f32[64,2,32,256]{3,2,1,0:T(8,128)} %doppler.2.rest_0_), custom_call_target="tpu_custom_call", output_to_operand_aliasing={{}: (2, {})} | custom-call | flops 3449999872 | bytes 1 | tf_op jit(solution)/shard_map/doppler/doppler/pallas_call | solution.py:420
  (3 shorter events, 0.0 us)
Async XLA Ops:
  0.0 10.0 %copy-start.2 = (s32[2048]{0:T(1024)S(1)}, s32[2048]{0:T(1024)}, u32[]{:S(2)}) copy-start(s32[2048]{0:T(1024)} %param.12) | copy-start | bytes 24580
  0.0 10.0 %copy-start.3 = (s32[2048]{0:T(1024)S(1)}, s32[2048]{0:T(1024)}, u32[]{:S(2)}) copy-start(s32[2048]{0:T(1024)} %param.11) | copy-start | bytes 24580
  0.0 10.0 %copy-start.1 = (s32[2048]{0:T(1024)S(1)}, s32[2048]{0:T(1024)}, u32[]{:S(2)}) copy-start(s32[2048]{0:T(1024)} %param.10) | copy-start | bytes 24580
  2.1 3.4 %collective-permute-start.2 = (f32[1,1024]{1,0:T(1,128)S(1)}, f32[1,1024]{1,0:T(1,128)S(1)}, u32[]{:S(2)}, u32[]{:S(2)}) collective-permute-start(f32[1,1024]{1,0:T(1,128)S(1)} %bitcast.7), channel_id=1, source_target_pairs={{0,3},{1,2},{2,1},{3,0},{4,7},{5,6},{6,5},{7,4},{8,11},{9,10},{10,... | collective-permute-start | bytes 12296 | tf_op jit(solution)/shard_map/ppermute | solution.py:450
  4.0 2.5 %collective-permute-start.1 = (f32[1,1024]{1,0:T(1,128)S(1)}, f32[1,1024]{1,0:T(1,128)S(1)}, u32[]{:S(2)}, u32[]{:S(2)}) collective-permute-start(f32[1,1024]{1,0:T(1,128)S(1)} %bitcast.8), channel_id=1, source_target_pairs={{0,2},{1,3},{2,0},{3,1},{4,6},{5,7},{6,4},{7,5},{8,10},{9,11},{10,... | collective-permute-start | bytes 12296 | tf_op jit(solution)/shard_map/ppermute | solution.py:450
  4.2 2.2 %collective-permute-start = (f32[1,1024]{1,0:T(1,128)S(1)}, f32[1,1024]{1,0:T(1,128)S(1)}, u32[]{:S(2)}, u32[]{:S(2)}) collective-permute-start(f32[1,1024]{1,0:T(1,128)S(1)} %bitcast.9), channel_id=1, source_target_pairs={{0,1},{1,0},{2,3},{3,2},{4,5},{5,4},{6,7},{7,6},{8,9},{9,8},{10,11... | collective-permute-start | bytes 12296 | tf_op jit(solution)/shard_map/ppermute | solution.py:450
  6.5 4.3 %collective-permute-start.5 = (f32[1,1024]{1,0:T(1,128)S(1)}, f32[1,1024]{1,0:T(1,128)S(1)}, u32[]{:S(2)}, u32[]{:S(2)}) collective-permute-start(f32[1,1024]{1,0:T(1,128)S(1)} %add.2.refs_0_), channel_id=1, source_target_pairs={{0,12},{1,13},{2,14},{3,15},{4,8},{5,9},{6,10},{7,11},{8,4},{9,5},... | collective-permute-start | bytes 12296 | tf_op jit(solution)/shard_map/ppermute | solution.py:450
  7.8 3.4 %collective-permute-start.4 = (f32[1,1024]{1,0:T(1,128)S(1)}, f32[1,1024]{1,0:T(1,128)S(1)}, u32[]{:S(2)}, u32[]{:S(2)}) collective-permute-start(f32[1,1024]{1,0:T(1,128)S(1)} %add.2.refs_0_), channel_id=1, source_target_pairs={{0,8},{1,9},{2,10},{3,11},{4,12},{5,13},{6,14},{7,15},{8,0},{9,1},... | collective-permute-start | bytes 12296 | tf_op jit(solution)/shard_map/ppermute | solution.py:450
  8.9 2.5 %collective-permute-start.3 = (f32[1,1024]{1,0:T(1,128)S(1)}, f32[1,1024]{1,0:T(1,128)S(1)}, u32[]{:S(2)}, u32[]{:S(2)}) collective-permute-start(f32[1,1024]{1,0:T(1,128)S(1)} %add.2.refs_0_), channel_id=1, source_target_pairs={{0,4},{1,5},{2,6},{3,7},{4,0},{5,1},{6,2},{7,3},{8,12},{9,13},{10,... | collective-permute-start | bytes 12296 | tf_op jit(solution)/shard_map/ppermute | solution.py:450
  10.7 1.6 %copy-start = (bf16[2,1024,512]{2,1,0:T(8,128)(2,1)S(1)}, bf16[2,1024,512]{2,1,0:T(8,128)(2,1)}, u32[]{:S(2)}) copy-start(bf16[2,1024,512]{2,1,0:T(8,128)(2,1)} %echoes_ref.7) | copy-start | bytes 6291460
  19.4 10.7 %slice-start = ((s8[8388608]{0:T(1024)(128)(4,1)}), s8[4194304]{0:T(1024)(128)(4,1)S(1)}, s32[]{:S(2)}) async-start(s8[8388608]{0:T(1024)(128)(4,1)} %bitcast.5), calls=%async_computation.2 | async-start | bytes 8388608
  19.5 10.7 %slice-start.1 = ((s8[8388608]{0:T(1024)(128)(4,1)}), s8[4194304]{0:T(1024)(128)(4,1)S(1)}, s32[]{:S(2)}) async-start(s8[8388608]{0:T(1024)(128)(4,1)} %bitcast.5), calls=%async_computation.3 | async-start | bytes 8388608
  19.5 18.6 %collective-permute-start.7 = (bf16[256,1024]{1,0:T(8,128)(2,1)}, bf16[256,1024]{1,0:T(8,128)(2,1)S(1)}, u32[]{:S(2)}, u32[]{:S(2)}) collective-permute-start(bf16[256,1024]{1,0:T(8,128)(2,1)} %get-tuple-element.56), channel_id=1, source_target_pairs={{0,16},{16,0},{1,17},{17,1},{2,18},{18,2},{3,19},{19,3},{4,20},{20... | collective-permute-start | bytes 1572872 | tf_op jit(solution)/shard_map/tile_sum/ppermute | solution.py:531
  29.8 13.8 %collective-permute-start.6 = (bf16[256,1024]{1,0:T(8,128)(2,1)}, bf16[256,1024]{1,0:T(8,128)(2,1)S(1)}, u32[]{:S(2)}, u32[]{:S(2)}) collective-permute-start(bf16[256,1024]{1,0:T(8,128)(2,1)} %get-tuple-element.53), channel_id=1, source_target_pairs={{0,16},{16,0},{1,17},{17,1},{2,18},{18,2},{3,19},{19,3},{4,20},{20... | collective-permute-start | bytes 1572872 | tf_op jit(solution)/shard_map/tile_sum/ppermute | solution.py:531
  36.7 1.3 %copy-start.4 = (bf16[2,8]{1,0:T(2,128)(2,1)S(1)}, bf16[2,8]{1,0:T(2,128)(2,1)}, u32[]{:S(2)}) copy-start(bf16[2,8]{1,0:T(2,128)(2,1)} %code_ref.13) | copy-start | bytes 100
  43.6 18.4 %collective-permute-start.8 = (bf16[256,1024]{1,0:T(8,128)(2,1)}, bf16[256,1024]{1,0:T(8,128)(2,1)S(1)}, u32[]{:S(2)}, u32[]{:S(2)}) collective-permute-start(bf16[256,1024]{1,0:T(8,128)(2,1)} %get-tuple-element.68), channel_id=1, source_target_pairs={{0,16},{16,0},{1,17},{17,1},{2,18},{18,2},{3,19},{19,3},{4,20},{20... | collective-permute-start | bytes 1572872 | tf_op jit(solution)/shard_map/tile_sum/ppermute | solution.py:531
  46.3 32.6 %all-to-all-start.1 = ((bf16[16,256,128]{2,1,0:T(8,128)(2,1)}), bf16[16,256,128]{2,1,0:T(8,128)(2,1)}, u32[]{:S(2)}, u32[]{:S(2)}) async-start(bf16[16,256,128]{2,1,0:T(8,128)(2,1)} %get-tuple-element.74), calls=%async_computation.1 | async-start | bytes 2097152 | tf_op jit(solution)/shard_map/to_owners/all_to_all | solution.py:552
  53.9 7.5 %copy-start.6 = (bf16[2,112,1024]{2,1,0:T(8,128)(2,1)S(1)}, bf16[2,112,1024]{2,1,0:T(8,128)(2,1)}, u32[]{:S(2)}) copy-start(bf16[2,112,1024]{2,1,0:T(8,128)(2,1)} %get-tuple-element.66.ahead_ref) | copy-start | bytes 1376260
  61.0 13.4 %collective-permute-start.9 = (bf16[256,1024]{1,0:T(8,128)(2,1)}, bf16[256,1024]{1,0:T(8,128)(2,1)S(1)}, u32[]{:S(2)}, u32[]{:S(2)}) collective-permute-start(bf16[256,1024]{1,0:T(8,128)(2,1)} %get-tuple-element.71), channel_id=1, source_target_pairs={{0,16},{16,0},{1,17},{17,1},{2,18},{18,2},{3,19},{19,3},{4,20},{20... | collective-permute-start | bytes 1572872 | tf_op jit(solution)/shard_map/tile_sum/ppermute | solution.py:531
  74.5 9.3 %copy-start.5 = (bf16[256,512]{1,0:T(8,128)(2,1)S(1)}, bf16[256,512]{1,0:T(8,128)(2,1)}, u32[]{:S(2)}) copy-start(bf16[256,512]{1,0:T(8,128)(2,1)} %constant.10.clone.table_ref) | copy-start | bytes 786436
  78.8 29.8 %all-to-all-start = ((bf16[16,256,128]{2,1,0:T(8,128)(2,1)}), bf16[16,256,128]{2,1,0:T(8,128)(2,1)S(1)}, u32[]{:S(2)}, u32[]{:S(2)}) async-start(bf16[16,256,128]{2,1,0:T(8,128)(2,1)} %compress.7), calls=%async_computation | async-start | bytes 2097152 | tf_op jit(solution)/shard_map/to_owners/all_to_all | solution.py:552

commit v8 on v7

--- a/solution.py
+++ b/solution.py
@@ -379,7 +379,7 @@
     owners, rows, lanes = got_ref.shape
     own, bins = lanes // 2, table_ref.shape[1] // 2
     gates = rows // pulses
-    batch = block_of(some, max(1, 512 // lanes))
+    batch = block_of(some, max(1, 256 // lanes))
 
     def copy(block):
         at = pl.ds(first + block * some, some)

time: 112 us -> 112 us (level)
  no operation moved by 1% of the time
where the time goes in v8:
time: 112 us; the launch traced here: 111 us
  Pallas kernels  48.5 us (43%)
  waiting for transfers between devices  38.2 us (34%)
  starting transfers between devices  21 us (19%)
  other arithmetic  2.11 us (2%)
    pallas_call x4, Pallas kernels, form_beams(): pl.pallas_call(functools.partial(beam_kernel, samples, gates, gate, count...  30 us
    all_to_all x2, waiting for transfers between devices, on_device(): lax.all_to_all(ready[number], 'beam', split_axis=0, concat_axis=0)  23.8 us
    all_to_all x2, starting transfers between devices, on_device(): lax.all_to_all(ready[number], 'beam', split_axis=0, concat_axis=0)  12.5 us
    ppermute x4, waiting for transfers between devices, on_device(): lax.ppermute(part, 'tile', [(i, (i + away) % tiles) for i in range(tiles)])  11.8 us
    pallas_call x4, Pallas kernels, compress(): pl.pallas_call(functools.partial(compress_kernel, pulses, taps, len(parts...  7.25 us
    pallas_call x2, Pallas kernels, doppler(): pl.pallas_call(functools.partial(doppler_kernel, pulses, first, some), in...  5.99 us
    ppermute x6, starting transfers between devices, sum_over(): lax.ppermute(values, axis, [(i, i ^ away) for i in range(size)])  5.9 us
    ppermute x6, waiting for transfers between devices, sum_over(): lax.ppermute(values, axis, [(i, i ^ away) for i in range(size)])  2.62 us
  transfers between devices with their start and end apart: 12, of which 8 were waited for; matrix products, arithmetic and copies ran while one was open for 0% of the time, Pallas kernels for 35%

profile of v8, /device:TPU:9, one launch (start us, length us, event | category | flops | bytes accessed | tf_op | source)
XLA Modules:
  0.0 111.2 jit_solution(8265449781525052808)
XLA Ops:
  0.0 0.0 copy-start.2
  0.0 0.0 copy-start.3
  0.0 0.0 copy-start.1
  0.0 2.1 %multiply_reduce_fusion = f32[1024]{0:T(1024)S(1)} fusion(bf16[2,1024,512]{2,1,0:T(8,128)(2,1)} %echoes_ref.7), kind=kLoop, calls=%fused_computation | loop fusion | flops 3144704 | bytes 2101248 | tf_op jit(solution)/shard_map/reduce_sum | solution.py:501
  2.1 1.9 %collective-permute-start.2 = (f32[1,1024]{1,0:T(1,128)S(1)}, f32[1,1024]{1,0:T(1,128)S(1)}, u32[]{:S(2)}, u32[]{:S(2)}) collective-permute-start(f32[1,1024]{1,0:T(1,128)S(1)} %bitcast.7), channel_id=1, source_target_pairs={{0,3},{1,2},{2,1},{3,0},{4,7},{5,6},{6,5},{7,4},{8,11},{9,10},{10,... | collective-permute-start | bytes 12296 | tf_op jit(solution)/shard_map/ppermute | solution.py:450
  4.0 0.2 collective-permute-start.1
  4.2 0.2 collective-permute-start
  4.5 1.0 collective-permute-done.2.refs_3_
  5.5 0.9 collective-permute-done.1.refs_2_
  6.4 0.0 collective-permute-done.refs_1_
  6.5 1.4 %collective-permute-start.5 = (f32[1,1024]{1,0:T(1,128)S(1)}, f32[1,1024]{1,0:T(1,128)S(1)}, u32[]{:S(2)}, u32[]{:S(2)}) collective-permute-start(f32[1,1024]{1,0:T(1,128)S(1)} %add.2.refs_0_), channel_id=1, source_target_pairs={{0,12},{1,13},{2,14},{3,15},{4,8},{5,9},{6,10},{7,11},{8,4},{9,5},... | collective-permute-start | bytes 12296 | tf_op jit(solution)/shard_map/ppermute | solution.py:450
  7.8 1.1 collective-permute-start.4
  8.9 1.1 collective-permute-start.3
  10.0 0.0 copy-done.2
  10.0 0.0 copy-done.3
  10.0 0.0 copy-done.1
  10.0 0.7 lookup.1
  10.7 0.0 copy-start
  10.7 0.0 collective-permute-done.5.refs_3_
  10.7 0.4 collective-permute-done.4.refs_2_
  11.2 0.2 collective-permute-done.3.refs_1_
  11.4 0.9 copy-done
  12.3 7.1 %beams.4 = (bf16[256,1024]{1,0:T(8,128)(2,1)}, bf16[256,2048]{1,0:T(8,128)(2,1)S(1)}) custom-call(bf16[2,1024,512]{2,1,0:T(8,128)(2,1)S(1)} %copy-done, f32[1,1024]{1,0:T(1,128)S(1)} %add.3.power_ref, s32[1,2048]{1,0:T(1,128)S(1)} %get-tuple-element.42.order_ref, bf16[2,2048,1024]{2,1,0:T(8,128)(2,1)} %steer_ref.7), custom_call_target="tpu_custom_call" | custom-call | flops 10350000128 | bytes 1 | tf_op jit(solution)/shard_map/beams/beams/pallas_call | solution.py:210
  19.4 0.0 slice-start
  19.5 0.0 slice-start.1
  19.5 1.3 %collective-permute-start.7 = (bf16[256,1024]{1,0:T(8,128)(2,1)}, bf16[256,1024]{1,0:T(8,128)(2,1)S(1)}, u32[]{:S(2)}, u32[]{:S(2)}) collective-permute-start(bf16[256,1024]{1,0:T(8,128)(2,1)} %get-tuple-element.56), channel_id=1, source_target_pairs={{0,16},{16,0},{1,17},{17,1},{2,18},{18,2},{3,19},{19,3},{4,20},{20... | collective-permute-start | bytes 1572872 | tf_op jit(solution)/shard_map/tile_sum/ppermute | solution.py:531
  20.7 9.1 %beams.5 = (bf16[256,1024]{1,0:T(8,128)(2,1)S(1)}, bf16[256,1024]{1,0:T(8,128)(2,1)}) custom-call(bf16[2,1024,512]{2,1,0:T(8,128)(2,1)S(1)} %copy-done, f32[1,1024]{1,0:T(1,128)S(1)} %add.3.power_ref, s32[1,2048]{1,0:T(1,128)S(1)} %get-tuple-element.42.order_ref, bf16[2,2048,1024]{2,1,0:T(8,128)(2,1)} %steer_ref.7), custom_call_target="tpu_custom_call" | custom-call | flops 10350000128 | bytes 1 | tf_op jit(solution)/shard_map/beams/beams/pallas_call | solution.py:210
  29.8 0.3 collective-permute-start.6
  30.1 0.0 slice-done
  30.1 0.0 slice-done.1
  30.1 6.6 %beams.6 = (bf16[256,1024]{1,0:T(8,128)(2,1)S(1)}, bf16[256,1024]{1,0:T(8,128)(2,1)}) custom-call(bf16[2,1024,512]{2,1,0:T(8,128)(2,1)S(1)} %copy-done, f32[1,1024]{1,0:T(1,128)S(1)} %add.3.power_ref, s32[1,2048]{1,0:T(1,128)S(1)} %get-tuple-element.42.order_ref, bf16[2,2048,1024]{2,1,0:T(8,128)(2,1)S(1)} %bitcast.6), custom_call_target="tpu_custom_call" | custom-call | flops 10350000128 | bytes 1 | tf_op jit(solution)/shard_map/beams/beams/pallas_call | solution.py:210
  36.7 0.0 copy-start.4
  36.7 1.3 %own.2.rest_0_ = bf16[256,1024]{1,0:T(8,128)(2,1)S(1)} custom-call(bf16[256,2048]{1,0:T(8,128)(2,1)S(1)} %get-tuple-element.47.beams_ref, s32[1,2048]{1,0:T(1,128)S(1)} %get-tuple-element.42.order_ref), custom_call_target="tpu_custom_call" | custom-call | flops 2300000000 | bytes 1 | tf_op jit(solution)/shard_map/beams/own/pallas_call | solution.py:185
  38.1 0.0 collective-permute-done.7.rest_1_
  38.1 0.0 copy-done.4
  38.1 1.8 %compress.4 = (bf16[16,256,128]{2,1,0:T(8,128)(2,1)}, bf16[2,112,1024]{2,1,0:T(8,128)(2,1)S(1)}) custom-call(bf16[2,8]{1,0:T(2,128)(2,1)S(1)} %copy-done.4, s32[1]{0:T(128)} %bitcast.at_ref, s32[1,1024]{1,0:T(1,128)S(1)} %get-tuple-element.40.lens_ref, s32[1,1024]{1,0:T(1,128)S(1)} %get-tuple-element.41.limits_ref, bf16[256,1024]{1,0:T(8,128)(2,1)S(1)} %own.2.rest_0_, ...), custom_call_target="tpu_custom_call" | custom-call | flops 3449999872 | bytes 1 | tf_op jit(solution)/shard_map/compress/compress/pallas_call | solution.py:352
  39.8 0.7 edge.3.rest_2_
  40.5 3.1 %collective-permute-done.6.rest_1_ = bf16[256,1024]{1,0:T(8,128)(2,1)S(1)} collective-permute-done((bf16[256,1024]{1,0:T(8,128)(2,1)}, bf16[256,1024]{1,0:T(8,128)(2,1)S(1)}, u32[]{:S(2)}, u32[]{:S(2)}) %collective-permute-start.6) | collective-permute-done | bytes 524320 | tf_op jit(solution)/shard_map/tile_sum/ppermute | solution.py:531
  43.6 0.7 collective-permute-start.8
  44.3 1.9 %compress.5 = (bf16[16,256,128]{2,1,0:T(8,128)(2,1)}, bf16[2,112,1024]{2,1,0:T(8,128)(2,1)}) custom-call(bf16[2,8]{1,0:T(2,128)(2,1)S(1)} %copy-done.4, s32[1]{0:T(128)} %bitcast.at_ref, s32[1,1024]{1,0:T(1,128)S(1)} %get-tuple-element.40.lens_ref, s32[1,1024]{1,0:T(1,128)S(1)} %get-tuple-element.41.limits_ref, ...), custom_call_target="tpu_custom_call", output_to_operand_aliasing={{0}: (7, {})} | custom-call | flops 3449999872 | bytes 1 | tf_op jit(solution)/shard_map/compress/compress/pallas_call | solution.py:352
  46.3 7.6 %all-to-all-start.1 = ((bf16[16,256,128]{2,1,0:T(8,128)(2,1)}), bf16[16,256,128]{2,1,0:T(8,128)(2,1)}, u32[]{:S(2)}, u32[]{:S(2)}) async-start(bf16[16,256,128]{2,1,0:T(8,128)(2,1)} %get-tuple-element.74), calls=%async_computation.1 | async-start | bytes 2097152 | tf_op jit(solution)/shard_map/to_owners/all_to_all | solution.py:552
  53.9 0.0 copy-start.6
  53.9 7.2 %beams.7 = (bf16[256,1024]{1,0:T(8,128)(2,1)}, bf16[256,2048]{1,0:T(8,128)(2,1)S(1)}) custom-call(bf16[2,1024,512]{2,1,0:T(8,128)(2,1)S(1)} %copy-done, f32[1,1024]{1,0:T(1,128)S(1)} %add.3.power_ref, s32[1,2048]{1,0:T(1,128)S(1)} %get-tuple-element.42.order_ref, bf16[2,2048,1024]{2,1,0:T(8,128)(2,1)} %steer_ref.7), custom_call_target="tpu_custom_call" | custom-call | bytes 1 | tf_op jit(solution)/shard_map/beams/beams/pallas_call | solution.py:210
  61.0 0.3 collective-permute-start.9
  61.4 0.0 copy-done.6
  61.4 0.7 edge.4.rest_2_
  62.0 0.0 collective-permute-done.8.rest_1_
  62.0 1.8 %compress.6 = (bf16[16,256,128]{2,1,0:T(8,128)(2,1)}, bf16[2,112,1024]{2,1,0:T(8,128)(2,1)S(1)}) custom-call(bf16[2,8]{1,0:T(2,128)(2,1)S(1)} %copy-done.4, s32[1]{0:T(128)} %bitcast.at_ref, s32[1,1024]{1,0:T(1,128)S(1)} %get-tuple-element.40.lens_ref, s32[1,1024]{1,0:T(1,128)S(1)} %get-tuple-element.41.limits_ref, ...), custom_call_target="tpu_custom_call" | custom-call | flops 115000000512 | bytes 1 | tf_op jit(solution)/shard_map/compress/compress/pallas_call | solution.py:352
  63.8 0.7 edge.5.rest_2_
  64.5 1.3 %own.3.rest_0_ = bf16[256,1024]{1,0:T(8,128)(2,1)S(1)} custom-call(bf16[256,2048]{1,0:T(8,128)(2,1)S(1)} %get-tuple-element.70.beams_ref, s32[1,2048]{1,0:T(1,128)S(1)} %get-tuple-element.42.order_ref), custom_call_target="tpu_custom_call" | custom-call | flops 2300000000 | bytes 1 | tf_op jit(solution)/shard_map/beams/own/pallas_call | solution.py:185
  65.8 8.7 %collective-permute-done.9.rest_1_ = bf16[256,1024]{1,0:T(8,128)(2,1)S(1)} collective-permute-done((bf16[256,1024]{1,0:T(8,128)(2,1)}, bf16[256,1024]{1,0:T(8,128)(2,1)S(1)}, u32[]{:S(2)}, u32[]{:S(2)}) %collective-permute-start.9) | collective-permute-done | bytes 524320 | tf_op jit(solution)/shard_map/tile_sum/ppermute | solution.py:531
  74.5 0.0 copy-start.5
  74.5 1.8 %compress.7 = bf16[16,256,128]{2,1,0:T(8,128)(2,1)} custom-call(bf16[2,8]{1,0:T(2,128)(2,1)S(1)} %copy-done.4, s32[1]{0:T(128)} %bitcast.at_ref, s32[1,1024]{1,0:T(1,128)S(1)} %get-tuple-element.40.lens_ref, s32[1,1024]{1,0:T(1,128)S(1)} %get-tuple-element.41.limits_ref, bf16[256,1024]{1,0:T(8,128)(2,1)S(1)} %own.3.rest_0_, ...), custom_call_target="tpu_custom_call", output_to_operand_aliasing={{}: (7, {})} | custom-call | flops 115000000512 | bytes 1 | tf_op jit(solution)/shard_map/compress/compress/pallas_call | solution.py:352
  76.3 2.6 %all-to-all-done.1.got_ref = bf16[16,256,128]{2,1,0:T(8,128)(2,1)} async-done(((bf16[16,256,128]{2,1,0:T(8,128)(2,1)}), bf16[16,256,128]{2,1,0:T(8,128)(2,1)}, u32[]{:S(2)}, u32[]{:S(2)}) %all-to-all-start.1) | async-done | bytes 1048608 | tf_op jit(solution)/shard_map/to_owners/all_to_all | solution.py:552
  78.8 4.9 %all-to-all-start = ((bf16[16,256,128]{2,1,0:T(8,128)(2,1)}), bf16[16,256,128]{2,1,0:T(8,128)(2,1)S(1)}, u32[]{:S(2)}, u32[]{:S(2)}) async-start(bf16[16,256,128]{2,1,0:T(8,128)(2,1)} %compress.7), calls=%async_computation | async-start | bytes 2097152 | tf_op jit(solution)/shard_map/to_owners/all_to_all | solution.py:552
  83.8 0.0 copy-done.5
  83.8 3.6 %doppler.2.rest_0_ = f32[64,2,32,256]{3,2,1,0:T(8,128)} custom-call(bf16[16,256,128]{2,1,0:T(8,128)(2,1)} %all-to-all-done.1.got_ref, bf16[256,512]{1,0:T(8,128)(2,1)S(1)} %copy-done.5), custom_call_target="tpu_custom_call" | custom-call | flops 3449999872 | bytes 1 | tf_op jit(solution)/shard_map/doppler/doppler/pallas_call | solution.py:420
  87.4 21.2 %all-to-all-done.got_ref = bf16[16,256,128]{2,1,0:T(8,128)(2,1)S(1)} async-done(((bf16[16,256,128]{2,1,0:T(8,128)(2,1)}), bf16[16,256,128]{2,1,0:T(8,128)(2,1)S(1)}, u32[]{:S(2)}, u32[]{:S(2)}) %all-to-all-start) | async-done | bytes 1048608 | tf_op jit(solution)/shard_map/to_owners/all_to_all | solution.py:552
  108.6 2.4 %doppler.3 = f32[64,2,32,256]{3,2,1,0:T(8,128)} custom-call(bf16[16,256,128]{2,1,0:T(8,128)(2,1)S(1)} %all-to-all-done.got_ref, bf16[256,512]{1,0:T(8,128)(2,1)S(1)} %copy-done.5, f32[64,2,32,256]{3,2,1,0:T(8,128)} %doppler.2.rest_0_), custom_call_target="tpu_custom_call", output_to_operand_aliasing={{}: (2, {})} | custom-call | flops 3449999872 | bytes 1 | tf_op jit(solution)/shard_map/doppler/doppler/pallas_call | solution.py:420
  (3 shorter events, 0.0 us)
Async XLA Ops:
  0.0 10.0 %copy-start.2 = (s32[2048]{0:T(1024)S(1)}, s32[2048]{0:T(1024)}, u32[]{:S(2)}) copy-start(s32[2048]{0:T(1024)} %param.12) | copy-start | bytes 24580
  0.0 10.0 %copy-start.3 = (s32[2048]{0:T(1024)S(1)}, s32[2048]{0:T(1024)}, u32[]{:S(2)}) copy-start(s32[2048]{0:T(1024)} %param.11) | copy-start | bytes 24580
  0.0 10.0 %copy-start.1 = (s32[2048]{0:T(1024)S(1)}, s32[2048]{0:T(1024)}, u32[]{:S(2)}) copy-start(s32[2048]{0:T(1024)} %param.10) | copy-start | bytes 24580
  2.1 3.4 %collective-permute-start.2 = (f32[1,1024]{1,0:T(1,128)S(1)}, f32[1,1024]{1,0:T(1,128)S(1)}, u32[]{:S(2)}, u32[]{:S(2)}) collective-permute-start(f32[1,1024]{1,0:T(1,128)S(1)} %bitcast.7), channel_id=1, source_target_pairs={{0,3},{1,2},{2,1},{3,0},{4,7},{5,6},{6,5},{7,4},{8,11},{9,10},{10,... | collective-permute-start | bytes 12296 | tf_op jit(solution)/shard_map/ppermute | solution.py:450
  4.0 2.5 %collective-permute-start.1 = (f32[1,1024]{1,0:T(1,128)S(1)}, f32[1,1024]{1,0:T(1,128)S(1)}, u32[]{:S(2)}, u32[]{:S(2)}) collective-permute-start(f32[1,1024]{1,0:T(1,128)S(1)} %bitcast.8), channel_id=1, source_target_pairs={{0,2},{1,3},{2,0},{3,1},{4,6},{5,7},{6,4},{7,5},{8,10},{9,11},{10,... | collective-permute-start | bytes 12296 | tf_op jit(solution)/shard_map/ppermute | solution.py:450
  4.2 2.2 %collective-permute-start = (f32[1,1024]{1,0:T(1,128)S(1)}, f32[1,1024]{1,0:T(1,128)S(1)}, u32[]{:S(2)}, u32[]{:S(2)}) collective-permute-start(f32[1,1024]{1,0:T(1,128)S(1)} %bitcast.9), channel_id=1, source_target_pairs={{0,1},{1,0},{2,3},{3,2},{4,5},{5,4},{6,7},{7,6},{8,9},{9,8},{10,11... | collective-permute-start | bytes 12296 | tf_op jit(solution)/shard_map/ppermute | solution.py:450
  6.5 4.3 %collective-permute-start.5 = (f32[1,1024]{1,0:T(1,128)S(1)}, f32[1,1024]{1,0:T(1,128)S(1)}, u32[]{:S(2)}, u32[]{:S(2)}) collective-permute-start(f32[1,1024]{1,0:T(1,128)S(1)} %add.2.refs_0_), channel_id=1, source_target_pairs={{0,12},{1,13},{2,14},{3,15},{4,8},{5,9},{6,10},{7,11},{8,4},{9,5},... | collective-permute-start | bytes 12296 | tf_op jit(solution)/shard_map/ppermute | solution.py:450
  7.8 3.4 %collective-permute-start.4 = (f32[1,1024]{1,0:T(1,128)S(1)}, f32[1,1024]{1,0:T(1,128)S(1)}, u32[]{:S(2)}, u32[]{:S(2)}) collective-permute-start(f32[1,1024]{1,0:T(1,128)S(1)} %add.2.refs_0_), channel_id=1, source_target_pairs={{0,8},{1,9},{2,10},{3,11},{4,12},{5,13},{6,14},{7,15},{8,0},{9,1},... | collective-permute-start | bytes 12296 | tf_op jit(solution)/shard_map/ppermute | solution.py:450
  8.9 2.5 %collective-permute-start.3 = (f32[1,1024]{1,0:T(1,128)S(1)}, f32[1,1024]{1,0:T(1,128)S(1)}, u32[]{:S(2)}, u32[]{:S(2)}) collective-permute-start(f32[1,1024]{1,0:T(1,128)S(1)} %add.2.refs_0_), channel_id=1, source_target_pairs={{0,4},{1,5},{2,6},{3,7},{4,0},{5,1},{6,2},{7,3},{8,12},{9,13},{10,... | collective-permute-start | bytes 12296 | tf_op jit(solution)/shard_map/ppermute | solution.py:450
  10.7 1.6 %copy-start = (bf16[2,1024,512]{2,1,0:T(8,128)(2,1)S(1)}, bf16[2,1024,512]{2,1,0:T(8,128)(2,1)}, u32[]{:S(2)}) copy-start(bf16[2,1024,512]{2,1,0:T(8,128)(2,1)} %echoes_ref.7) | copy-start | bytes 6291460
  19.4 10.7 %slice-start = ((s8[8388608]{0:T(1024)(128)(4,1)}), s8[4194304]{0:T(1024)(128)(4,1)S(1)}, s32[]{:S(2)}) async-start(s8[8388608]{0:T(1024)(128)(4,1)} %bitcast.5), calls=%async_computation.2 | async-start | bytes 8388608
  19.5 10.7 %slice-start.1 = ((s8[8388608]{0:T(1024)(128)(4,1)}), s8[4194304]{0:T(1024)(128)(4,1)S(1)}, s32[]{:S(2)}) async-start(s8[8388608]{0:T(1024)(128)(4,1)} %bitcast.5), calls=%async_computation.3 | async-start | bytes 8388608
  19.5 18.6 %collective-permute-start.7 = (bf16[256,1024]{1,0:T(8,128)(2,1)}, bf16[256,1024]{1,0:T(8,128)(2,1)S(1)}, u32[]{:S(2)}, u32[]{:S(2)}) collective-permute-start(bf16[256,1024]{1,0:T(8,128)(2,1)} %get-tuple-element.56), channel_id=1, source_target_pairs={{0,16},{16,0},{1,17},{17,1},{2,18},{18,2},{3,19},{19,3},{4,20},{20... | collective-permute-start | bytes 1572872 | tf_op jit(solution)/shard_map/tile_sum/ppermute | solution.py:531
  29.8 13.8 %collective-permute-start.6 = (bf16[256,1024]{1,0:T(8,128)(2,1)}, bf16[256,1024]{1,0:T(8,128)(2,1)S(1)}, u32[]{:S(2)}, u32[]{:S(2)}) collective-permute-start(bf16[256,1024]{1,0:T(8,128)(2,1)} %get-tuple-element.53), channel_id=1, source_target_pairs={{0,16},{16,0},{1,17},{17,1},{2,18},{18,2},{3,19},{19,3},{4,20},{20... | collective-permute-start | bytes 1572872 | tf_op jit(solution)/shard_map/tile_sum/ppermute | solution.py:531
  36.7 1.3 %copy-start.4 = (bf16[2,8]{1,0:T(2,128)(2,1)S(1)}, bf16[2,8]{1,0:T(2,128)(2,1)}, u32[]{:S(2)}) copy-start(bf16[2,8]{1,0:T(2,128)(2,1)} %code_ref.13) | copy-start | bytes 100
  43.6 18.4 %collective-permute-start.8 = (bf16[256,1024]{1,0:T(8,128)(2,1)}, bf16[256,1024]{1,0:T(8,128)(2,1)S(1)}, u32[]{:S(2)}, u32[]{:S(2)}) collective-permute-start(bf16[256,1024]{1,0:T(8,128)(2,1)} %get-tuple-element.68), channel_id=1, source_target_pairs={{0,16},{16,0},{1,17},{17,1},{2,18},{18,2},{3,19},{19,3},{4,20},{20... | collective-permute-start | bytes 1572872 | tf_op jit(solution)/shard_map/tile_sum/ppermute | solution.py:531
  46.3 32.6 %all-to-all-start.1 = ((bf16[16,256,128]{2,1,0:T(8,128)(2,1)}), bf16[16,256,128]{2,1,0:T(8,128)(2,1)}, u32[]{:S(2)}, u32[]{:S(2)}) async-start(bf16[16,256,128]{2,1,0:T(8,128)(2,1)} %get-tuple-element.74), calls=%async_computation.1 | async-start | bytes 2097152 | tf_op jit(solution)/shard_map/to_owners/all_to_all | solution.py:552
  53.9 7.5 %copy-start.6 = (bf16[2,112,1024]{2,1,0:T(8,128)(2,1)S(1)}, bf16[2,112,1024]{2,1,0:T(8,128)(2,1)}, u32[]{:S(2)}) copy-start(bf16[2,112,1024]{2,1,0:T(8,128)(2,1)} %get-tuple-element.66.ahead_ref) | copy-start | bytes 1376260
  61.0 13.4 %collective-permute-start.9 = (bf16[256,1024]{1,0:T(8,128)(2,1)}, bf16[256,1024]{1,0:T(8,128)(2,1)S(1)}, u32[]{:S(2)}, u32[]{:S(2)}) collective-permute-start(bf16[256,1024]{1,0:T(8,128)(2,1)} %get-tuple-element.71), channel_id=1, source_target_pairs={{0,16},{16,0},{1,17},{17,1},{2,18},{18,2},{3,19},{19,3},{4,20},{20... | collective-permute-start | bytes 1572872 | tf_op jit(solution)/shard_map/tile_sum/ppermute | solution.py:531
  74.5 9.3 %copy-start.5 = (bf16[256,512]{1,0:T(8,128)(2,1)S(1)}, bf16[256,512]{1,0:T(8,128)(2,1)}, u32[]{:S(2)}) copy-start(bf16[256,512]{1,0:T(8,128)(2,1)} %constant.10.clone.table_ref) | copy-start | bytes 786436
  78.8 29.8 %all-to-all-start = ((bf16[16,256,128]{2,1,0:T(8,128)(2,1)}), bf16[16,256,128]{2,1,0:T(8,128)(2,1)S(1)}, u32[]{:S(2)}, u32[]{:S(2)}) async-start(bf16[16,256,128]{2,1,0:T(8,128)(2,1)} %compress.7), calls=%async_computation | async-start | bytes 2097152 | tf_op jit(solution)/shard_map/to_owners/all_to_all | solution.py:552
